TPU v7x, 1024 devices: a whole 4x8x16 slice. The times are simulated.
1024 devices in a mesh: dp: 16 (over y, core), expert: 64 (over z, x).
Axes of the slice: x: 4, y: 8, z: 16, core: 2. Of those that a mesh axis runs over, the one named last changes fastest.
Arguments:
- out_grad: bfloat16 [16384, 4096], P(('dp', 'expert')), may hold values from -6 to 6
- hidden: bfloat16 [16384, 8, 768], P(('dp', 'expert')), may hold values from -3 to 3
- combine: float32 [16384, 8], P(('dp', 'expert')), may hold values from 0.02 to 0.5
- expert_ids: int32 [16384, 8], P(('dp', 'expert')), may hold values from 0 to 63, all different within a row; in each aligned block of 16 rows (0 to 15, 16 to 31, ...) at most 3 rows name the same one
- down_weight: bfloat16 [64, 4096, 768], P('expert'), may hold values from -0.21875 to 0.21875
Outputs:
- grad_hidden: bfloat16 [16384, 8, 768], P(('dp', 'expert'))
- grad_weights: float32 [16384, 8], P(('dp', 'expert'))
- grad_down: bfloat16 [64, 4096, 768], P('expert', 'dp')
Inputs may be any that keep to these rules, and one draw needn't show every extreme that they name: `expert_ids`: among the 16 tokens of one device no expert is named more than 3 times, a bound that some block reaches; the 8 experts of a token are different.
All inputs are finite; a program needn't handle non-finite values.
Results may differ from a plain program's by a relative error of at most 0.022.
Values may be sent and summed in bfloat16 or wider, within the bound.
No kernel may reach another device: no remote copies, remote signals or barrier semaphores. Data moves between devices by JAX's collectives and lax.ppermute only.
A program may use at most 64 MiB of HBM per device.

v0:
```python
import jax
import jax.numpy as jnp
from jax import lax
from jax.sharding import PartitionSpec as P


def local(out_grad, hidden, combine, expert_ids, down_weight):
    tok, width = out_grad.shape
    topk = expert_ids.shape[1]
    ffw = hidden.shape[2]
    owners = lax.axis_size("expert")
    cap = min(tok, 3 * tok * topk // (2 * owners))
    rows = tok * topk
    slots_here = owners * cap
    flat_ids = expert_ids.reshape(rows)
    onehot = (flat_ids[:, None] == jnp.arange(owners, dtype=jnp.int32)[None, :]).astype(jnp.int32)
    before = jnp.cumsum(onehot, axis=0) - onehot
    slot = jnp.sum(onehot * before, axis=1)
    target = flat_ids * cap + slot
    placing = (target[None, :] == jnp.arange(slots_here, dtype=jnp.int32)[:, None]).astype(
        jnp.bfloat16
    )
    by_token = jnp.sum(placing.reshape(slots_here, tok, topk).astype(jnp.float32), axis=2).astype(
        jnp.bfloat16
    )
    weighted = (
        (combine[:, :, None] * hidden.astype(jnp.float32)).astype(jnp.bfloat16).reshape(rows, ffw)
    )
    send_grad = jnp.dot(by_token, out_grad, preferred_element_type=jnp.float32).astype(jnp.bfloat16)
    send_act = jnp.dot(placing, weighted, preferred_element_type=jnp.float32).astype(jnp.bfloat16)
    recv_grad, recv_act = (
        lax.all_to_all(
            send_grad.reshape(owners, cap, width), "expert", split_axis=0, concat_axis=0, tiled=True
        ),
        lax.all_to_all(
            send_act.reshape(owners, cap, ffw), "expert", split_axis=0, concat_axis=0, tiled=True
        ),
    )
    flat_grad = recv_grad.reshape(slots_here, width)
    flat_act = recv_act.reshape(slots_here, ffw)
    projected = jnp.dot(flat_grad, down_weight[0], preferred_element_type=jnp.float32).astype(
        jnp.bfloat16
    )
    returned = lax.all_to_all(
        projected.reshape(owners, cap, ffw), "expert", split_axis=0, concat_axis=0, tiled=True
    )
    back = jnp.dot(
        placing.T, returned.reshape(slots_here, ffw), preferred_element_type=jnp.float32
    ).reshape(tok, topk, ffw)
    grad_hidden = (combine[:, :, None] * back).astype(jnp.bfloat16)
    grad_weights = jnp.sum(hidden.astype(jnp.float32) * back, axis=2)
    partial_value = lax.dot_general(
        flat_grad, flat_act, (((0,), (0,)), ((), ())), preferred_element_type=jnp.float32
    ).astype(jnp.bfloat16)
    partial_value = lax.optimization_barrier(partial_value)
    grad_down = lax.psum_scatter(
        partial_value.astype(jnp.float32).astype(jnp.bfloat16),
        "dp",
        scatter_dimension=0,
        tiled=True,
    )
    return (grad_hidden, grad_weights, grad_down[None])


def solution(mesh):
    placed = (
        P(("dp", "expert"), None),
        P(("dp", "expert"), None, None),
        P(("dp", "expert"), None),
        P(("dp", "expert"), None),
        P("expert", None, None),
    )
    return jax.shard_map(
        local,
        mesh=mesh,
        in_specs=placed,
        out_specs=(
            P(("dp", "expert"), None, None),
            P(("dp", "expert"), None),
            P("expert", "dp", None),
        ),
        check_vma=False,
    )
```

profile of v0, /device:TPU:6, one launch (start us, length us, event | category | flops | bytes accessed | tf_op | source)
XLA Modules:
  0.0 245.7 jit_solution(6823593985185758735)
XLA Ops:
  7.2 0.0 copy-start
  7.2 0.8 copy.26
  8.0 0.1 reshape.67
  8.1 0.1 fusion.18
  8.2 0.2 reduce_window_sum.11
  8.3 0.2 select_reduce_fusion
  8.5 0.8 copy.25
  9.3 1.2 convolution_convert_fusion.1
  10.5 0.9 reshape.73
  11.4 22.3 %all-to-all-start.2 = ((bf16[64,3,768]{2,1,0:T(4,128)(2,1)}), bf16[64,3,768]{2,1,0:T(4,128)(2,1)S(1)}, u32[]{:S(2)}, u32[]{:S(2)}) async-start(bf16[64,3,768]{2,1,0:T(4,128)(2,1)} %reshape.73), calls=%async_computation.2 | async-start | bytes 786432 | tf_op jit(solution)/shard_map/all_to_all | solution.py:35
  33.7 0.0 reduce-scatter.2.cloned.1.call-start
  33.7 0.1 reduce_sum.33
  33.8 0.1 fusion.16
  33.9 0.0 copy-done
  33.9 0.6 convolution_convert_fusion
  34.5 2.4 reshape.68
  36.9 23.9 %all-to-all-done.2 = bf16[64,3,768]{2,1,0:T(4,128)(2,1)S(1)} async-done(((bf16[64,3,768]{2,1,0:T(4,128)(2,1)}), bf16[64,3,768]{2,1,0:T(4,128)(2,1)S(1)}, u32[]{:S(2)}, u32[]{:S(2)}) %all-to-all-start.2) | async-done | bytes 294944 | tf_op jit(solution)/shard_map/all_to_all | solution.py:35
  60.8 105.4 %all_to_all.15 = bf16[64,3,4096]{2,1,0:T(4,128)(2,1)S(1)} all-to-all(bf16[64,3,4096]{2,1,0:T(4,128)(2,1)} %reshape.68), channel_id=1, replica_groups=mesh['dp'=16,'expert'=64] {'expert'}, dimensions={0} | all-to-all | bytes 3145728 | tf_op jit(solution)/shard_map/all_to_all | solution.py:32
  166.2 6.1 %bitcast_convert_fusion = bf16[4096,768]{1,0:T(8,128)(2,1)} fusion(bf16[64,3,4096]{2,1,0:T(4,128)(2,1)S(1)} %all_to_all.15, bf16[64,3,768]{2,1,0:T(4,128)(2,1)S(1)} %all-to-all-done.2), kind=kOutput, calls=%fused_computation | convolution fusion | flops 1211105280 | bytes 8159232 | tf_op jit(solution)/shard_map/dot_general | solution.py:52
  172.3 0.0 reduce-scatter.2.cloned.1.call-update
  172.3 2.5 %reshape.69 = bf16[192,4096]{1,0:T(8,128)(2,1)} reshape(bf16[64,3,4096]{2,1,0:T(4,128)(2,1)S(1)} %all_to_all.15) | data formatting | bytes 3145728 | tf_op jit(solution)/shard_map/reshape | solution.py:39
  174.9 4.7 %fusion.3 = bf16[192,768]{1,0:T(8,128)(2,1)S(1)} fusion(bf16[192,4096]{1,0:T(8,128)(2,1)} %reshape.69, bf16[1,4096,768]{2,1,0:T(8,128)(2,1)} %param.9), kind=kOutput, calls=%fused_computation.5 | convolution fusion | flops 1208107008 | bytes 8159232 | tf_op jit(solution)/shard_map/dot_general | solution.py:41
  179.5 0.0 copy-start.1
  179.5 0.1 reshape.70
  179.7 31.8 %all_to_all.16 = bf16[64,3,768]{2,1,0:T(4,128)(2,1)S(1)} all-to-all(bf16[64,3,768]{2,1,0:T(4,128)(2,1)S(1)} %reshape.70), channel_id=1, replica_groups=mesh['dp'=16,'expert'=64] {'expert'}, dimensions={0} | all-to-all | bytes 589824 | tf_op jit(solution)/shard_map/all_to_all | solution.py:44
  211.5 0.2 reshape.74
  211.8 0.0 copy-done.1
  211.8 1.0 fusion.6
  212.8 0.7 copy.30
  213.5 25.4 %reduce-scatter.2.cloned.1.call-done = bf16[256,768]{1,0:T(8,128)(2,1)} async-done(((bf16[4096,768]{1,0:T(8,128)(2,1)}), bf16[256,768]{1,0:T(8,128)(2,1)}) %reduce-scatter.2.cloned.1.call-update) | async-done | bytes 393232 | tf_op jit(solution)/shard_map/reduce_scatter | solution.py:56
  (2 shorter events, 0.0 us)
Async XLA Ops:
  7.2 26.8 %copy-start = (bf16[16,4096]{1,0:T(8,128)(2,1)S(1)}, bf16[16,4096]{1,0:T(8,128)(2,1)}, u32[]{:S(2)}) copy-start(bf16[16,4096]{1,0:T(8,128)(2,1)} %param.5) | copy-start | bytes 393220
  11.4 49.4 %all-to-all-start.2 = ((bf16[64,3,768]{2,1,0:T(4,128)(2,1)}), bf16[64,3,768]{2,1,0:T(4,128)(2,1)S(1)}, u32[]{:S(2)}, u32[]{:S(2)}) async-start(bf16[64,3,768]{2,1,0:T(4,128)(2,1)} %reshape.73), calls=%async_computation.2 | async-start | bytes 786432 | tf_op jit(solution)/shard_map/all_to_all | solution.py:35
  33.7 205.2 %reduce-scatter.2.cloned.1.call-start = ((), (), s32[]{:S(2)}) async-start(), calls=%async_computation.4 | async-start | bytes 6684672 | tf_op jit(solution)/shard_map/reduce_scatter | solution.py:56
  179.5 32.3 %copy-start.1 = (bf16[16,8,768]{2,1,0:T(8,128)(2,1)S(1)}, bf16[16,8,768]{2,1,0:T(8,128)(2,1)}, u32[]{:S(2)}) copy-start(bf16[16,8,768]{2,1,0:T(8,128)(2,1)} %param.6) | copy-start | bytes 589828
Sparse Core Ops, SparseCore 0:
  172.4 66.3 reduce-scatter.1
where the time goes:
time: 246 us
  blocking collectives  137 us (56%)
  waiting for transfers between devices  49.3 us (20%)
  starting transfers between devices  22.3 us (9%)
  between operations  14.1 us (6%)
  matrix products  13.6 us (6%)
  local copies, waits for them, and re-layouts  8.56 us (3%)
    all_to_all x1, blocking collectives, local(): lax.all_to_all(send_grad.reshape(owners, cap, width), 'expert', split_axi...  105 us
    all_to_all x1, blocking collectives, local(): lax.all_to_all(projected.reshape(owners, cap, ffw), 'expert', split_axis=...  31.8 us
    reduce_scatter x1, waiting for transfers between devices, local(): lax.psum_scatter(partial_value.astype(jnp.float32).astype(jnp.bfloat16),...  25.4 us
    all_to_all x1, waiting for transfers between devices, local(): lax.all_to_all(send_act.reshape(owners, cap, ffw), 'expert', split_axis=0...  23.9 us
    all_to_all x1, starting transfers between devices, local(): lax.all_to_all(send_act.reshape(owners, cap, ffw), 'expert', split_axis=0...  22.3 us
    dot_general x1, matrix products, local(): lax.dot_general(flat_grad, flat_act, (((0,), (0,)), ((), ())), preferred_...  6.12 us
  transfers between devices with their start and end apart: 2, of which 2 were waited for; matrix products, arithmetic and copies ran while one was open for 5% of the time, Pallas kernels for 0%

commit v1 on v0

v1 whole, which is shorter than its diff:
```python
import jax
import jax.numpy as jnp
from jax import lax
from jax.sharding import Mesh
from jax.sharding import PartitionSpec as P

CORES = 2
XS = 4
DIRECT = 1280
F32 = jnp.float32
BF16 = jnp.bfloat16


def dot(a, b, dims=(((1,), (0,)), ((), ()))):
    return lax.dot_general(a, b, dims, preferred_element_type=F32)


def local(out_grad, hidden, combine, expert_ids, down_weight):
    tok, width = out_grad.shape
    topk = expert_ids.shape[1]
    ffw = hidden.shape[2]
    xs, zs, ys = lax.axis_size("x"), lax.axis_size("z"), lax.axis_size("y")
    core, z_here = lax.axis_index("core"), lax.axis_index("z")
    owners = xs * zs
    cap = min(tok, 3 * tok * topk // (2 * owners))
    rows = tok * topk
    slots_here = owners * cap
    half = width // CORES
    direct = DIRECT // CORES
    relay = half - direct
    piece = half // ys

    by_core = (
        out_grad.reshape(tok, ys, CORES, piece).transpose(0, 2, 1, 3).reshape(tok, CORES, half)
    )
    ids_wide = jnp.pad(expert_ids.astype(BF16), ((0, 0), (0, 128 - topk)))
    relay_send = jnp.concatenate(
        [by_core[:, 0, direct:], by_core[:, 1, direct:], ids_wide], axis=1
    )
    relay_all = lax.all_gather(relay_send, "z", axis=0, tiled=True)

    flat_ids = expert_ids.reshape(rows)
    owner = (flat_ids % xs) * zs + flat_ids // xs
    onehot = (owner[:, None] == jnp.arange(owners, dtype=jnp.int32)[None, :]).astype(jnp.int32)
    before = jnp.cumsum(onehot, axis=0) - onehot
    slot = jnp.sum(onehot * before, axis=1)
    target = owner * cap + slot
    placing = (target[None, :] == jnp.arange(slots_here, dtype=jnp.int32)[:, None]).astype(BF16)
    by_token = jnp.sum(placing.reshape(slots_here, tok, topk).astype(F32), axis=2).astype(BF16)
    weighted = (combine[:, :, None] * hidden.astype(F32)).astype(BF16).reshape(rows, ffw)
    direct_cols = jnp.concatenate([by_core[:, 0, :direct], by_core[:, 1, :direct]], axis=1)
    send = jnp.concatenate(
        [dot(placing, weighted).astype(BF16), dot(by_token, direct_cols).astype(BF16)], axis=1
    )
    wide = send.shape[1]
    got = lax.all_to_all(
        send.reshape(owners, cap * wide // 128, 128),
        ("x", "z"),
        split_axis=0,
        concat_axis=0,
        tiled=True,
    ).reshape(slots_here, wide)
    acts = got[:, :ffw]
    got_direct = got[:, ffw:]

    seen = relay_all[:, CORES * relay : CORES * relay + topk].astype(jnp.int32)
    experts_here = z_here * xs + jnp.arange(xs, dtype=jnp.int32)
    names = jnp.any(seen[:, :, None] == experts_here[None, None, :], axis=1)
    names = names.reshape(zs, tok, xs).astype(jnp.int32)
    nth = jnp.cumsum(names, axis=1) - names
    chosen = (names[None] > 0) & (nth[None] == jnp.arange(cap, dtype=jnp.int32)[:, None, None, None])
    chosen = chosen.transpose(3, 1, 0, 2)
    picking = (
        chosen[:, :, :, None, :]
        & (jnp.arange(zs)[:, None] == jnp.arange(zs)[None, :])[None, :, None, :, None]
    )
    picking = picking.astype(BF16).reshape(slots_here, zs * tok)
    relay_rows = dot(picking, relay_all[:, : CORES * relay]).astype(BF16)
    got_relay = lax.all_to_all(
        relay_rows.reshape(xs, zs * cap, CORES * relay), "x", split_axis=0, concat_axis=0, tiled=True
    ).reshape(slots_here, CORES * relay)

    halves = [
        jnp.concatenate(
            [
                got_direct[:, c * direct : (c + 1) * direct],
                got_relay[:, c * relay : (c + 1) * relay],
            ],
            axis=1,
        )
        for c in range(CORES)
    ]
    mine = jnp.where(core == 0, halves[0], halves[1])
    theirs = jnp.where(core == 0, halves[1], halves[0])
    swap = [(0, 1), (1, 0)]
    other_acts = lax.ppermute(acts, "core", swap)
    other_grad = lax.ppermute(theirs, "core", swap)

    rows_dim = (((0,), (0,)), ((), ()))
    partial_value = dot(
        jnp.concatenate([mine, other_grad], axis=0),
        jnp.concatenate([acts, other_acts], axis=0),
        rows_dim,
    ).astype(BF16)
    grad_down = lax.psum_scatter(partial_value, "y", scatter_dimension=0, tiled=True)

    weight = down_weight[0].reshape(ys, CORES, piece, ffw)
    projected = sum(
        dot(halves[c], weight[:, c].reshape(half, ffw)) for c in range(CORES)
    ).astype(BF16)
    returned = lax.all_to_all(
        projected.reshape(owners, cap * ffw // 1152, 1152),
        ("x", "z"),
        split_axis=0,
        concat_axis=0,
        tiled=True,
    ).reshape(slots_here, ffw)
    back = dot(placing, returned, rows_dim).reshape(tok, topk, ffw)
    grad_hidden = (combine[:, :, None] * back).astype(BF16)
    grad_weights = jnp.sum(hidden.astype(F32) * back, axis=2)
    return (grad_hidden, grad_weights, grad_down[None])


def solution(mesh):
    dp, expert = mesh.shape["dp"], mesh.shape["expert"]
    fine = Mesh(
        mesh.devices.reshape(dp // CORES, CORES, expert // XS, XS), ("y", "core", "z", "x")
    )
    tokens = ("y", "core", "z", "x")
    placed = (
        P(tokens, None),
        P(tokens, None, None),
        P(tokens, None),
        P(tokens, None),
        P(("z", "x"), None, None),
    )
    return jax.shard_map(
        local,
        mesh=fine,
        in_specs=placed,
        out_specs=(
            P(tokens, None, None),
            P(tokens, None),
            P(("z", "x"), ("y", "core"), None),
        ),
        check_vma=False,
    )
```

time: 246 us -> 195 us (0.79)
  blocking collectives: 137 us -> 34 us
  waiting for transfers between devices: 49.3 us -> 92 us
  starting transfers between devices: 22.3 us -> 31.6 us
  matrix products: 13.6 us -> 8.12 us
  other arithmetic: 0.57 us -> 3.46 us
    all_to_all x2 -> x1, blocking collectives: 137 us -> 34 us  [local(): lax.all_to_all(projected.reshape(owners, cap * ffw // 1152, 1152), ('x',...]
    all_gather x0 -> x1, waiting for transfers between devices: none -> 71.9 us  [local(): relay_all = lax.all_gather(relay_send, 'z', axis=0, tiled=True)]
    all_to_all x1 -> x2, waiting for transfers between devices: 23.9 us -> 8.61 us  [the longest x1 8.61 us: local(): lax.all_to_all(relay_rows.reshape(xs, zs * cap, CORES * relay), 'x', spli...]
    reduce_scatter x1, waiting for transfers between devices: 25.4 us -> 10.3 us  [local(): lax.psum_scatter(partial_value, 'y', scatter_dimension=0, tiled=True)]
    dot_general x5 -> x7, matrix products: 13.6 us -> 8.12 us  [dot(): return lax.dot_general(a, b, dims, preferred_element_type=F32)]
    all_to_all x1 -> x2, starting transfers between devices: 22.3 us -> 27.3 us  [the longest x1 22.5 us: local(): lax.all_to_all(send.reshape(owners, cap * wide // 128, 128), ('x', 'z'),...]
    slice x0 -> x5, local copies, waits for them, and re-layouts: none -> 4.38 us  [the longest x1 3.26 us: local(): weight[:, c].reshape(half, ffw)]
    ppermute x0 -> x2, starting transfers between devices: none -> 4.33 us  [the longest x1 2.41 us: local(): other_acts = lax.ppermute(acts, 'core', swap)]
  transfers between devices with their start and end apart: 2 -> 6, of which waited for: 2 -> 4; matrix products, arithmetic and copies ran while one was open for 5% -> 8% of each run, Pallas kernels for 0% -> 0%
where the time goes in v1:
time: 195 us
  waiting for transfers between devices  92 us (47%)
  blocking collectives  34 us (17%)
  starting transfers between devices  31.6 us (16%)
  between operations  14.3 us (7%)
  local copies, waits for them, and re-layouts  11 us (6%)
  matrix products  8.12 us (4%)
  other arithmetic  3.46 us (2%)
    all_gather x1, waiting for transfers between devices, local(): relay_all = lax.all_gather(relay_send, 'z', axis=0, tiled=True)  71.9 us
    all_to_all x1, blocking collectives, local(): lax.all_to_all(projected.reshape(owners, cap * ffw // 1152, 1152), ('x',...  34 us
    all_to_all x1, starting transfers between devices, local(): lax.all_to_all(send.reshape(owners, cap * wide // 128, 128), ('x', 'z'),...  22.5 us
    reduce_scatter x1, waiting for transfers between devices, local(): lax.psum_scatter(partial_value, 'y', scatter_dimension=0, tiled=True)  10.3 us
    all_to_all x1, waiting for transfers between devices, local(): lax.all_to_all(relay_rows.reshape(xs, zs * cap, CORES * relay), 'x', spli...  8.61 us
    dot_general x7, matrix products, dot(): return lax.dot_general(a, b, dims, preferred_element_type=F32)  8.12 us
    all_to_all x1, starting transfers between devices, local(): lax.all_to_all(relay_rows.reshape(xs, zs * cap, CORES * relay), 'x', spli...  4.8 us
  transfers between devices with their start and end apart: 6, of which 4 were waited for; matrix products, arithmetic and copies ran while one was open for 8% of the time, Pallas kernels for 0%

profile of v1, /device:TPU:6, one launch (start us, length us, event | category | flops | bytes accessed | tf_op | source)
XLA Modules:
  0.0 194.5 jit_solution(1760859482672965992)
XLA Ops:
  7.2 0.7 convert_element_type.66
  7.9 0.1 copy.84
  8.0 1.0 reshape.226
  9.0 0.1 reshape.227
  9.1 0.6 fusion.21
  9.8 0.8 copy.71
  10.6 0.1 reshape.224
  10.7 0.1 fusion.24
  10.8 0.2 reduce_window_sum.22
  10.9 0.2 select_reduce_fusion
  11.1 0.1 reduce_sum.33
  11.2 0.8 copy.70
  12.0 0.1 fusion.22
  12.2 0.3 convolution_convert_fusion.2
  12.5 0.3 convolution_convert_fusion.3
  12.8 0.1 pad_maximum_fusion
  12.9 1.2 reshape.228
  14.1 22.5 %all-to-all-start = ((bf16[64,48,128]{2,1,0:T(8,128)(2,1)}), bf16[64,48,128]{2,1,0:T(8,128)(2,1)S(1)}, u32[]{:S(2)}, u32[]{:S(2)}) async-start(bf16[64,48,128]{2,1,0:T(8,128)(2,1)} %reshape.228), calls=%async_computation | async-start | bytes 1572864 | tf_op jit(solution)/shard_map/all_to_all | solution.py:56
  36.6 71.9 %all-gather.2.cloned.1.call-done = bf16[256,2944]{1,0:T(8,128)(2,1)} async-done(((bf16[16,2944]{1,0:T(8,128)(2,1)}), bf16[256,2944]{1,0:T(8,128)(2,1)}) %all-gather.2.cloned.1.call-update) | async-done | bytes 1507344 | tf_op jit(solution)/shard_map/all_gather | solution.py:40
  108.5 1.0 slice.60
  109.4 0.1 copy.83
  109.5 0.1 compare_reduce_fusion
  109.6 0.1 reshape.234
  109.7 0.2 copy.79
  109.9 0.7 fusion.5
  110.6 0.2 copy.81
  110.8 0.1 fusion.20
  110.9 0.3 broadcast_and_fusion
  111.1 0.6 and.96
  111.8 1.4 convolution_convert_fusion
  113.2 4.8 %all-to-all-start.1 = ((bf16[4,48,2816]{2,1,0:T(8,128)(2,1)}), bf16[4,48,2816]{2,1,0:T(8,128)(2,1)S(1)}, u32[]{:S(2)}, u32[]{:S(2)}) async-start(bf16[4,48,2816]{2,1,0:T(8,128)(2,1)} %bitcast.9), calls=%async_computation.1 | async-start | bytes 2162688 | tf_op jit(solution)/shard_map/all_to_all | solution.py:79
  118.0 0.3 reshape.229
  118.4 8.6 %all-to-all-done.1 = bf16[4,48,2816]{2,1,0:T(8,128)(2,1)S(1)} async-done(((bf16[4,48,2816]{2,1,0:T(8,128)(2,1)}), bf16[4,48,2816]{2,1,0:T(8,128)(2,1)S(1)}, u32[]{:S(2)}, u32[]{:S(2)}) %all-to-all-start.1) | async-done | bytes 1081376 | tf_op jit(solution)/shard_map/all_to_all | solution.py:79
  127.0 0.1 fusion.44
  127.1 0.3 broadcast_select_fusion.1
  127.4 1.9 collective-permute-start
  129.3 2.4 %collective-permute-start.1 = (bf16[192,768]{1,0:T(8,128)(2,1)S(1)}, bf16[192,768]{1,0:T(8,128)(2,1)S(1)}, u32[]{:S(2)}, u32[]{:S(2)}) collective-permute-start(bf16[192,768]{1,0:T(8,128)(2,1)S(1)} %slice.67), channel_id=1, source_target_pairs={{0,64},{64,0},{1,65},{65,1},{2,66},{66,2},{3,67},{67,3},{4,68},{68... | collective-permute-start | bytes 884744 | tf_op jit(solution)/shard_map/ppermute | solution.py:96
  131.7 1.2 collective-permute-done.1
  132.9 3.5 %convolution_convert_fusion.1 = bf16[2048,768]{1,0:T(8,128)(2,1)} fusion(bf16[192,2048]{1,0:T(8,128)(2,1)S(1)} %collective-permute-done, bf16[192,2048]{1,0:T(8,128)(2,1)S(1)} %get-tuple-element.17, bf16[192,768]{1,0:T(8,128)(2,1)S(1)} %collective-permute-done.1, bf16[192,768]{1,0:T(8,128)(2,1)S(1)} %slice.67), kind=kOutput, calls=%fused_computation.1 | convolution fusion | flops 1213857792 | bytes 5308416 | tf_op jit(solution)/shard_map/dot_general | solution.py:15
  136.5 3.3 %fusion.43 = (bf16[8,1,256,768]{3,2,1,0:T(8,128)(2,1)S(1)}, bf16[8,1,256,768]{3,2,1,0:T(8,128)(2,1)S(1)}) fusion(bf16[8,2,256,768]{3,2,1,0:T(8,128)(2,1)} %bitcast.43), kind=kLoop, calls=%fused_computation.84 | loop fusion | bytes 12582912 | tf_op jit(solution)/shard_map/slice | solution.py:109
  139.7 0.8 fusion.11
  140.5 0.8 fusion.4
  141.3 0.2 reshape.232
  141.5 34.0 %all_to_all.15 = bf16[64,2,1152]{2,1,0:T(2,128)(2,1)S(1)} all-to-all(bf16[64,2,1152]{2,1,0:T(2,128)(2,1)S(1)} %reshape.232), channel_id=1, replica_groups=mesh['y'=8,'core'=2,'z'=16,'x'=4] {'x','z'}, dimensions={0} | all-to-all | bytes 589824 | tf_op jit(solution)/shard_map/all_to_all | solution.py:111
  175.6 0.2 reshape.235
  175.8 1.0 fusion.10
  176.8 0.7 copy.82
  177.4 10.3 %reduce-scatter.2.cloned.1.call-done = bf16[256,768]{1,0:T(8,128)(2,1)} async-done(((bf16[2048,768]{1,0:T(8,128)(2,1)}), bf16[256,768]{1,0:T(8,128)(2,1)}) %reduce-scatter.2.cloned.1.call-update) | async-done | bytes 393232 | tf_op jit(solution)/shard_map/reduce_scatter | solution.py:105
  (25 shorter events, 0.3 us)
Async XLA Ops:
  7.2 5.3 %copy-start.1 = (bf16[16,8,768]{2,1,0:T(8,128)(2,1)S(1)}, bf16[16,8,768]{2,1,0:T(8,128)(2,1)}, u32[]{:S(2)}) copy-start(bf16[16,8,768]{2,1,0:T(8,128)(2,1)} %param.6) | copy-start | bytes 589828
  7.2 101.3 %all-gather.2.cloned.1.call-start = ((), (), s32[]{:S(2)}) async-start(), calls=%async_computation.4 | async-start | bytes 1601536 | tf_op jit(solution)/shard_map/all_gather | solution.py:40
  14.1 99.1 %all-to-all-start = ((bf16[64,48,128]{2,1,0:T(8,128)(2,1)}), bf16[64,48,128]{2,1,0:T(8,128)(2,1)S(1)}, u32[]{:S(2)}, u32[]{:S(2)}) async-start(bf16[64,48,128]{2,1,0:T(8,128)(2,1)} %reshape.228), calls=%async_computation | async-start | bytes 1572864 | tf_op jit(solution)/shard_map/all_to_all | solution.py:56
  108.5 3.3 %copy-start = (bf16[256,2944]{1,0:T(8,128)(2,1)S(1)}, bf16[256,2944]{1,0:T(8,128)(2,1)}, u32[]{:S(2)}) copy-start(bf16[256,2944]{1,0:T(8,128)(2,1)} %all-gather.2.cloned.1.call-done) | copy-start | bytes 4521988
  113.2 13.8 %all-to-all-start.1 = ((bf16[4,48,2816]{2,1,0:T(8,128)(2,1)}), bf16[4,48,2816]{2,1,0:T(8,128)(2,1)S(1)}, u32[]{:S(2)}, u32[]{:S(2)}) async-start(bf16[4,48,2816]{2,1,0:T(8,128)(2,1)} %bitcast.9), calls=%async_computation.1 | async-start | bytes 2162688 | tf_op jit(solution)/shard_map/all_to_all | solution.py:79
  118.0 69.7 %reduce-scatter.2.cloned.1.call-start = ((), (), s32[]{:S(2)}) async-start(), calls=%async_computation.5 | async-start | bytes 3538944 | tf_op jit(solution)/shard_map/reduce_scatter | solution.py:105
  127.4 5.6 %collective-permute-start = (bf16[192,2048]{1,0:T(8,128)(2,1)S(1)}, bf16[192,2048]{1,0:T(8,128)(2,1)S(1)}, u32[]{:S(2)}, u32[]{:S(2)}) collective-permute-start(bf16[192,2048]{1,0:T(8,128)(2,1)S(1)} %get-tuple-element.18), channel_id=1, source_target_pairs={{0,64},{64,0},{1,65},{65,1},{2,66},{66,2},{3,67},{67,3},{4,68},{68... | collective-permute-start | bytes 2359304 | tf_op jit(solution)/shard_map/ppermute | solution.py:97
  129.3 3.6 %collective-permute-start.1 = (bf16[192,768]{1,0:T(8,128)(2,1)S(1)}, bf16[192,768]{1,0:T(8,128)(2,1)S(1)}, u32[]{:S(2)}, u32[]{:S(2)}) collective-permute-start(bf16[192,768]{1,0:T(8,128)(2,1)S(1)} %slice.67), channel_id=1, source_target_pairs={{0,64},{64,0},{1,65},{65,1},{2,66},{66,2},{3,67},{67,3},{4,68},{68... | collective-permute-start | bytes 884744 | tf_op jit(solution)/shard_map/ppermute | solution.py:96
  141.3 34.4 %copy-start.2 = (bf16[16,8,768]{2,1,0:T(8,128)(2,1)S(1)}, bf16[16,8,768]{2,1,0:T(8,128)(2,1)}, u32[]{:S(2)}) copy-start(bf16[16,8,768]{2,1,0:T(8,128)(2,1)} %param.6) | copy-start | bytes 589828
Sparse Core Ops, SparseCore 0:
  11.2 97.1 all-gather.1
  136.6 51.0 reduce-scatter.1

commit v2 on v1

--- a/solution.py
+++ b/solution.py
@@ -6,7 +6,7 @@
 
 CORES = 2
 XS = 4
-DIRECT = 1280
+FIRST = 896
 F32 = jnp.float32
 BF16 = jnp.bfloat16
 
@@ -26,18 +26,23 @@
     rows = tok * topk
     slots_here = owners * cap
     half = width // CORES
-    direct = DIRECT // CORES
-    relay = half - direct
     piece = half // ys
+    first = FIRST
+    second = half - first
 
     by_core = (
         out_grad.reshape(tok, ys, CORES, piece).transpose(0, 2, 1, 3).reshape(tok, CORES, half)
     )
+    all_second = lax.all_gather(
+        by_core[:, :, first:].reshape(tok, CORES * second), "z", axis=0, tiled=True
+    )
     ids_wide = jnp.pad(expert_ids.astype(BF16), ((0, 0), (0, 128 - topk)))
-    relay_send = jnp.concatenate(
-        [by_core[:, 0, direct:], by_core[:, 1, direct:], ids_wide], axis=1
+    all_first = lax.all_gather(
+        jnp.concatenate([ids_wide, by_core[:, 0, :first], by_core[:, 1, :first]], axis=1),
+        "z",
+        axis=0,
+        tiled=True,
     )
-    relay_all = lax.all_gather(relay_send, "z", axis=0, tiled=True)
 
     flat_ids = expert_ids.reshape(rows)
     owner = (flat_ids % xs) * zs + flat_ids // xs
@@ -46,24 +51,16 @@
     slot = jnp.sum(onehot * before, axis=1)
     target = owner * cap + slot
     placing = (target[None, :] == jnp.arange(slots_here, dtype=jnp.int32)[:, None]).astype(BF16)
-    by_token = jnp.sum(placing.reshape(slots_here, tok, topk).astype(F32), axis=2).astype(BF16)
     weighted = (combine[:, :, None] * hidden.astype(F32)).astype(BF16).reshape(rows, ffw)
-    direct_cols = jnp.concatenate([by_core[:, 0, :direct], by_core[:, 1, :direct]], axis=1)
-    send = jnp.concatenate(
-        [dot(placing, weighted).astype(BF16), dot(by_token, direct_cols).astype(BF16)], axis=1
-    )
-    wide = send.shape[1]
-    got = lax.all_to_all(
-        send.reshape(owners, cap * wide // 128, 128),
+    acts = lax.all_to_all(
+        dot(placing, weighted).astype(BF16).reshape(owners, 2, cap * ffw // 2),
         ("x", "z"),
         split_axis=0,
         concat_axis=0,
         tiled=True,
-    ).reshape(slots_here, wide)
-    acts = got[:, :ffw]
-    got_direct = got[:, ffw:]
+    ).reshape(slots_here, ffw)
 
-    seen = relay_all[:, CORES * relay : CORES * relay + topk].astype(jnp.int32)
+    seen = all_first[:, :topk].astype(jnp.int32)
     experts_here = z_here * xs + jnp.arange(xs, dtype=jnp.int32)
     names = jnp.any(seen[:, :, None] == experts_here[None, None, :], axis=1)
     names = names.reshape(zs, tok, xs).astype(jnp.int32)
@@ -75,16 +72,24 @@
         & (jnp.arange(zs)[:, None] == jnp.arange(zs)[None, :])[None, :, None, :, None]
     )
     picking = picking.astype(BF16).reshape(slots_here, zs * tok)
-    relay_rows = dot(picking, relay_all[:, : CORES * relay]).astype(BF16)
-    got_relay = lax.all_to_all(
-        relay_rows.reshape(xs, zs * cap, CORES * relay), "x", split_axis=0, concat_axis=0, tiled=True
-    ).reshape(slots_here, CORES * relay)
+    picking, acts = lax.optimization_barrier((picking, acts))
 
+    def relay(gathered):
+        return lax.all_to_all(
+            dot(picking, gathered).astype(BF16).reshape(xs, zs * cap, gathered.shape[1]),
+            "x",
+            split_axis=0,
+            concat_axis=0,
+            tiled=True,
+        ).reshape(slots_here, gathered.shape[1])
+
+    got_first = relay(all_first[:, 128:])
+    got_second = relay(all_second)
     halves = [
         jnp.concatenate(
             [
-                got_direct[:, c * direct : (c + 1) * direct],
-                got_relay[:, c * relay : (c + 1) * relay],
+                got_first[:, c * first : (c + 1) * first],
+                got_second[:, c * second : (c + 1) * second],
             ],
             axis=1,
         )

time: 195 us -> 183 us (0.938)
  waiting for transfers between devices: 92 us -> 46 us
  starting transfers between devices: 31.6 us -> 49.7 us
  blocking collectives: 34 us -> 49.3 us
  matrix products: 8.12 us -> 10.2 us
    all_gather x1, waiting for transfers between devices: 71.9 us -> 4.7 us  [local(): lax.all_gather(by_core[:, :, first:].reshape(tok, CORES * second), 'z', a...]
    all_gather x0 -> x1, blocking collectives: none -> 49.3 us  [local(): lax.all_gather(jnp.concatenate([ids_wide, by_core[:, 0, :first], by_core[...]
    all_to_all x1 -> x0, blocking collectives: 34 us -> none  [local(): lax.all_to_all(projected.reshape(owners, cap * ffw // 1152, 1152), ('x',...]
    all_to_all x2 -> x4, waiting for transfers between devices: 8.61 us -> 30.5 us  [the longest x1 22.7 us: local(): lax.all_to_all(projected.reshape(owners, cap * ffw // 1152, 1152), ('x',...]
    all_to_all x2 -> x4, starting transfers between devices: 27.3 us -> 45.3 us  [the longest x1 22.5 us: local(): lax.all_to_all(dot(placing, weighted).astype(BF16).reshape(owners, 2, cap...]
    dot_general x7, matrix products: 8.12 us -> 10.2 us  [dot(): return lax.dot_general(a, b, dims, preferred_element_type=F32)]
  transfers between devices with their start and end apart: 6 -> 8, of which waited for: 4 -> 5; matrix products, arithmetic and copies ran while one was open for 8% -> 10% of each run, Pallas kernels for 0% -> 0%
where the time goes in v2:
time: 183 us; the launch traced here: 182 us
  starting transfers between devices  49.7 us (27%)
  blocking collectives  49.3 us (27%)
  waiting for transfers between devices  46 us (25%)
  between operations  14.3 us (8%)
  local copies, waits for them, and re-layouts  11 us (6%)
  matrix products  10.2 us (6%)
  other arithmetic  1.89 us (1%)
    all_gather x1, blocking collectives, local(): lax.all_gather(jnp.concatenate([ids_wide, by_core[:, 0, :first], by_core[...  49.3 us
    all_to_all x1, waiting for transfers between devices, local(): lax.all_to_all(projected.reshape(owners, cap * ffw // 1152, 1152), ('x',...  22.7 us
    all_to_all x1, starting transfers between devices, local(): lax.all_to_all(dot(placing, weighted).astype(BF16).reshape(owners, 2, cap...  22.5 us
    all_to_all x1, starting transfers between devices, local(): lax.all_to_all(projected.reshape(owners, cap * ffw // 1152, 1152), ('x',...  13.2 us
    dot_general x7, matrix products, dot(): return lax.dot_general(a, b, dims, preferred_element_type=F32)  10.2 us
    all_to_all x2, starting transfers between devices, relay(): lax.all_to_all(dot(picking, gathered).astype(BF16).reshape(xs, zs * cap,...  9.62 us
    reduce_scatter x1, waiting for transfers between devices, local(): lax.psum_scatter(partial_value, 'y', scatter_dimension=0, tiled=True)  9.53 us
    all_to_all x2, waiting for transfers between devices, relay(): lax.all_to_all(dot(picking, gathered).astype(BF16).reshape(xs, zs * cap,...  7.88 us
  transfers between devices with their start and end apart: 8, of which 5 were waited for; matrix products, arithmetic and copies ran while one was open for 10% of the time, Pallas kernels for 0%

profile of v2, /device:TPU:6, one launch (start us, length us, event | category | flops | bytes accessed | tf_op | source)
XLA Modules:
  0.0 182.4 jit_solution(11630560609045725990)
XLA Ops:
  7.2 1.0 reshape.226
  8.3 0.1 reshape.227
  8.4 0.6 copy.98
  9.0 0.8 copy.82
  9.8 0.8 copy.83
  10.6 0.1 reshape.225
  10.7 0.1 fusion.21
  10.8 0.2 reduce_window_sum.22
  10.9 0.2 select_reduce_fusion
  11.1 0.3 convolution_convert_fusion.3
  11.4 0.9 reshape.229
  12.3 22.5 %all-to-all-start = ((bf16[64,2,1152]{2,1,0:T(2,128)(2,1)}), bf16[64,2,1152]{2,1,0:T(2,128)(2,1)S(1)}, u32[]{:S(2)}, u32[]{:S(2)}) async-start(bf16[64,2,1152]{2,1,0:T(2,128)(2,1)} %reshape.229), calls=%async_computation | async-start | bytes 589824 | tf_op jit(solution)/shard_map/all_to_all | solution.py:55
  34.9 0.1 copy.97
  35.0 49.3 %all_gather.6 = bf16[256,1920]{1,0:T(8,128)(2,1)S(1)} all-gather(bf16[16,1920]{1,0:T(8,128)(2,1)S(1)} %fusion.23), channel_id=1, replica_groups=mesh['y'=8,'core'=2,'z'=16,'x'=4] {'z'}, dimensions={0}, use_global_device_ids=true | all-gather | bytes 1044480 | tf_op jit(solution)/shard_map/all_gather | solution.py:40
  84.3 0.1 copy.96
  84.4 0.1 compare_reduce_fusion
  84.5 0.1 reshape.238
  84.6 0.2 copy.91
  84.8 0.7 fusion.4
  85.5 0.2 copy.93
  85.7 0.1 fusion.18
  85.7 0.3 and_convert_fusion
  86.0 0.7 reshape.239
  86.7 0.2 reshape.230
  86.9 1.2 convolution_convert_fusion.2
  88.1 4.5 %all-to-all-start.1 = ((bf16[4,48,1792]{2,1,0:T(8,128)(2,1)}), bf16[4,48,1792]{2,1,0:T(8,128)(2,1)S(1)}, u32[]{:S(2)}, u32[]{:S(2)}) async-start(bf16[4,48,1792]{2,1,0:T(8,128)(2,1)} %bitcast.7), calls=%async_computation.1 | async-start | bytes 1376256 | tf_op jit(solution)/shard_map/all_to_all | solution.py:78
  92.6 4.7 %all-gather.2.cloned.1.call-done = bf16[256,2304]{1,0:T(8,128)(2,1)} async-done(((bf16[16,2304]{1,0:T(8,128)(2,1)}), bf16[256,2304]{1,0:T(8,128)(2,1)}) %all-gather.2.cloned.1.call-update) | async-done | bytes 1179664 | tf_op jit(solution)/shard_map/all_gather | solution.py:36
  97.3 2.6 %convolution_convert_fusion = bf16[192,2304]{1,0:T(8,128)(2,1)} fusion(bf16[192,256]{1,0:T(8,128)(2,1)S(1)} %reshape.239, bf16[256,2304]{1,0:T(8,128)(2,1)} %all-gather.2.cloned.1.call-done), kind=kOutput, calls=%fused_computation | convolution fusion | flops 226934784 | bytes 2162688 | tf_op jit(solution)/shard_map/dot_general | solution.py:15
  99.9 5.1 %all-to-all-start.2 = ((bf16[4,48,2304]{2,1,0:T(8,128)(2,1)}), bf16[4,48,2304]{2,1,0:T(8,128)(2,1)S(1)}, u32[]{:S(2)}, u32[]{:S(2)}) async-start(bf16[4,48,2304]{2,1,0:T(8,128)(2,1)} %bitcast.9), calls=%async_computation.2 | async-start | bytes 1769472 | tf_op jit(solution)/shard_map/all_to_all | solution.py:78
  105.0 0.1 fusion.40
  105.1 7.9 %all-to-all-done.2 = bf16[4,48,2304]{2,1,0:T(8,128)(2,1)S(1)} async-done(((bf16[4,48,2304]{2,1,0:T(8,128)(2,1)}), bf16[4,48,2304]{2,1,0:T(8,128)(2,1)S(1)}, u32[]{:S(2)}, u32[]{:S(2)}) %all-to-all-start.2) | async-done | bytes 884768 | tf_op jit(solution)/shard_map/all_to_all | solution.py:78
  113.0 0.1 fusion.39
  113.1 0.3 broadcast_select_fusion.1
  113.3 1.9 %collective-permute-start = (bf16[192,2048]{1,0:T(8,128)(2,1)S(1)}, bf16[192,2048]{1,0:T(8,128)(2,1)S(1)}, u32[]{:S(2)}, u32[]{:S(2)}) collective-permute-start(bf16[192,2048]{1,0:T(8,128)(2,1)S(1)} %get-tuple-element.22), channel_id=1, source_target_pairs={{0,64},{64,0},{1,65},{65,1},{2,66},{66,2},{3,67},{67,3},{4,68},{68... | collective-permute-start | bytes 2359304 | tf_op jit(solution)/shard_map/ppermute | solution.py:102
  115.2 2.4 %collective-permute-start.1 = (bf16[192,768]{1,0:T(8,128)(2,1)S(1)}, bf16[192,768]{1,0:T(8,128)(2,1)S(1)}, u32[]{:S(2)}, u32[]{:S(2)}) collective-permute-start(bf16[192,768]{1,0:T(8,128)(2,1)S(1)} %reshape.230), channel_id=1, source_target_pairs={{0,64},{64,0},{1,65},{65,1},{2,66},{66,2},{3,67},{67,3},{4,68},{68... | collective-permute-start | bytes 884744 | tf_op jit(solution)/shard_map/ppermute | solution.py:101
  117.7 1.2 collective-permute-done.1
  118.9 3.5 %convolution_convert_fusion.1 = bf16[2048,768]{1,0:T(8,128)(2,1)} fusion(bf16[192,2048]{1,0:T(8,128)(2,1)S(1)} %collective-permute-done, bf16[192,2048]{1,0:T(8,128)(2,1)S(1)} %get-tuple-element.21, bf16[192,768]{1,0:T(8,128)(2,1)S(1)} %collective-permute-done.1, bf16[192,768]{1,0:T(8,128)(2,1)S(1)} %reshape.230), kind=kOutput, calls=%fused_computation.1 | convolution fusion | flops 1213857792 | bytes 5308416 | tf_op jit(solution)/shard_map/dot_general | solution.py:15
  122.4 3.3 %fusion.38 = (bf16[8,1,256,768]{3,2,1,0:T(8,128)(2,1)S(1)}, bf16[8,1,256,768]{3,2,1,0:T(8,128)(2,1)S(1)}) fusion(bf16[8,2,256,768]{3,2,1,0:T(8,128)(2,1)} %bitcast.45), kind=kLoop, calls=%fused_computation.76 | loop fusion | bytes 12582912 | tf_op jit(solution)/shard_map/slice | solution.py:114
  125.6 0.8 fusion.11
  126.4 0.8 fusion.3
  127.2 0.9 reshape.236
  128.1 13.2 %all-to-all-start.3 = ((bf16[64,2,1152]{2,1,0:T(2,128)(2,1)}), bf16[64,2,1152]{2,1,0:T(2,128)(2,1)S(1)}, u32[]{:S(2)}, u32[]{:S(2)}) async-start(bf16[64,2,1152]{2,1,0:T(2,128)(2,1)} %reshape.236), calls=%async_computation.3 | async-start | bytes 589824 | tf_op jit(solution)/shard_map/all_to_all | solution.py:116
  141.4 0.1 reduce_sum.21
  141.5 22.7 %all-to-all-done.3 = bf16[64,2,1152]{2,1,0:T(2,128)(2,1)S(1)} async-done(((bf16[64,2,1152]{2,1,0:T(2,128)(2,1)}), bf16[64,2,1152]{2,1,0:T(2,128)(2,1)S(1)}, u32[]{:S(2)}, u32[]{:S(2)}) %all-to-all-start.3) | async-done | bytes 294944 | tf_op jit(solution)/shard_map/all_to_all | solution.py:116
  164.1 0.2 reshape.240
  164.3 1.0 fusion.10
  165.3 0.7 copy.95
  166.0 9.5 %reduce-scatter.2.cloned.1.call-done = bf16[256,768]{1,0:T(8,128)(2,1)} async-done(((bf16[2048,768]{1,0:T(8,128)(2,1)}), bf16[256,768]{1,0:T(8,128)(2,1)}) %reduce-scatter.2.cloned.1.call-update) | async-done | bytes 393232 | tf_op jit(solution)/shard_map/reduce_scatter | solution.py:110
  (25 shorter events, 0.2 us)
Async XLA Ops:
  7.2 27.7 %copy-start.1 = (s32[16,8]{0,1:T(8,128)S(1)}, s32[16,8]{0,1:T(8,128)}, u32[]{:S(2)}) copy-start(s32[16,8]{0,1:T(8,128)} %param.8) | copy-start | bytes 1540
  7.2 4.0 %copy-start = (bf16[16,8,768]{2,1,0:T(8,128)(2,1)S(1)}, bf16[16,8,768]{2,1,0:T(8,128)(2,1)}, u32[]{:S(2)}) copy-start(bf16[16,8,768]{2,1,0:T(8,128)(2,1)} %param.6) | copy-start | bytes 589828
  7.2 90.1 %all-gather.2.cloned.1.call-start = ((), (), s32[]{:S(2)}) async-start(), calls=%async_computation.5 | async-start | bytes 1253376 | tf_op jit(solution)/shard_map/all_gather | solution.py:36
  12.3 74.3 %all-to-all-start = ((bf16[64,2,1152]{2,1,0:T(2,128)(2,1)}), bf16[64,2,1152]{2,1,0:T(2,128)(2,1)S(1)}, u32[]{:S(2)}, u32[]{:S(2)}) async-start(bf16[64,2,1152]{2,1,0:T(2,128)(2,1)} %reshape.229), calls=%async_computation | async-start | bytes 589824 | tf_op jit(solution)/shard_map/all_to_all | solution.py:55
  88.1 11.8 %all-to-all-start.1 = ((bf16[4,48,1792]{2,1,0:T(8,128)(2,1)}), bf16[4,48,1792]{2,1,0:T(8,128)(2,1)S(1)}, u32[]{:S(2)}, u32[]{:S(2)}) async-start(bf16[4,48,1792]{2,1,0:T(8,128)(2,1)} %bitcast.7), calls=%async_computation.1 | async-start | bytes 1376256 | tf_op jit(solution)/shard_map/all_to_all | solution.py:78
  99.9 13.1 %all-to-all-start.2 = ((bf16[4,48,2304]{2,1,0:T(8,128)(2,1)}), bf16[4,48,2304]{2,1,0:T(8,128)(2,1)S(1)}, u32[]{:S(2)}, u32[]{:S(2)}) async-start(bf16[4,48,2304]{2,1,0:T(8,128)(2,1)} %bitcast.9), calls=%async_computation.2 | async-start | bytes 1769472 | tf_op jit(solution)/shard_map/all_to_all | solution.py:78
  105.0 70.5 %reduce-scatter.2.cloned.1.call-start = ((), (), s32[]{:S(2)}) async-start(), calls=%async_computation.6 | async-start | bytes 3538944 | tf_op jit(solution)/shard_map/reduce_scatter | solution.py:110
  113.3 5.5 %collective-permute-start = (bf16[192,2048]{1,0:T(8,128)(2,1)S(1)}, bf16[192,2048]{1,0:T(8,128)(2,1)S(1)}, u32[]{:S(2)}, u32[]{:S(2)}) collective-permute-start(bf16[192,2048]{1,0:T(8,128)(2,1)S(1)} %get-tuple-element.22), channel_id=1, source_target_pairs={{0,64},{64,0},{1,65},{65,1},{2,66},{66,2},{3,67},{67,3},{4,68},{68... | collective-permute-start | bytes 2359304 | tf_op jit(solution)/shard_map/ppermute | solution.py:102
  115.2 3.6 %collective-permute-start.1 = (bf16[192,768]{1,0:T(8,128)(2,1)S(1)}, bf16[192,768]{1,0:T(8,128)(2,1)S(1)}, u32[]{:S(2)}, u32[]{:S(2)}) collective-permute-start(bf16[192,768]{1,0:T(8,128)(2,1)S(1)} %reshape.230), channel_id=1, source_target_pairs={{0,64},{64,0},{1,65},{65,1},{2,66},{66,2},{3,67},{67,3},{4,68},{68... | collective-permute-start | bytes 884744 | tf_op jit(solution)/shard_map/ppermute | solution.py:101
  128.1 36.0 %all-to-all-start.3 = ((bf16[64,2,1152]{2,1,0:T(2,128)(2,1)}), bf16[64,2,1152]{2,1,0:T(2,128)(2,1)S(1)}, u32[]{:S(2)}, u32[]{:S(2)}) async-start(bf16[64,2,1152]{2,1,0:T(2,128)(2,1)} %reshape.236), calls=%async_computation.3 | async-start | bytes 589824 | tf_op jit(solution)/shard_map/all_to_all | solution.py:116
Sparse Core Ops, SparseCore 0:
  11.3 85.9 all-gather.1
  122.5 52.9 reduce-scatter.1

commit v3 on v1

v3 whole, which is shorter than its diff:
```python
import jax
import jax.numpy as jnp
from jax import lax
from jax.sharding import Mesh
from jax.sharding import PartitionSpec as P

CORES = 2
XS = 4
PAIR = 2
DIRECT = 128
F32 = jnp.float32
BF16 = jnp.bfloat16


def dot(a, b, dims=(((1,), (0,)), ((), ()))):
    return lax.dot_general(a, b, dims, preferred_element_type=F32)


def exchange(value, axes):
    return lax.all_to_all(value, axes, split_axis=0, concat_axis=0, tiled=True)


def local(out_grad, hidden, combine, expert_ids, down_weight):
    tok, width = out_grad.shape
    topk = expert_ids.shape[1]
    ffw = hidden.shape[2]
    xs, ys = lax.axis_size("x"), lax.axis_size("y")
    far, near = lax.axis_size("far"), lax.axis_size("near")
    core, far_here = lax.axis_index("core"), lax.axis_index("far")
    owners = far * near * xs
    plane = near * xs
    cap = min(tok, 3 * tok * topk // (2 * owners))
    rows = tok * topk
    slots_here = owners * cap
    half = width // CORES
    piece = half // ys
    relayed = half - DIRECT

    flat_ids = expert_ids.reshape(rows)
    owner = (flat_ids % plane) * far + flat_ids // plane
    onehot = (owner[:, None] == jnp.arange(owners, dtype=jnp.int32)[None, :]).astype(jnp.int32)
    before = jnp.cumsum(onehot, axis=0) - onehot
    slot = jnp.sum(onehot * before, axis=1)
    target = owner * cap + slot
    placing = (target[None, :] == jnp.arange(slots_here, dtype=jnp.int32)[:, None]).astype(BF16)
    by_token = jnp.sum(placing.reshape(slots_here, tok, topk).astype(F32), axis=2).astype(BF16)
    weighted = (combine[:, :, None] * hidden.astype(F32)).astype(BF16).reshape(rows, ffw)

    by_core = (
        out_grad.reshape(tok, ys, CORES, piece).transpose(0, 2, 1, 3).reshape(tok, CORES, half)
    )
    direct_cols = by_core[:, :, :DIRECT].reshape(tok, CORES * DIRECT)
    send = jnp.concatenate(
        [dot(placing, weighted).astype(BF16), dot(by_token, direct_cols).astype(BF16)], axis=1
    )
    wide = send.shape[1]
    got = exchange(
        send.reshape(owners, cap * wide // 128, 128), ("near", "x", "far")
    ).reshape(slots_here, wide)

    ids_wide = jnp.pad(expert_ids.astype(BF16), ((0, 0), (0, 128 - topk)))
    gathered = lax.all_gather(
        jnp.concatenate([ids_wide, by_core[:, 0, DIRECT:], by_core[:, 1, DIRECT:]], axis=1),
        "far",
        axis=0,
        tiled=True,
    )

    seen = gathered[:, :topk].astype(jnp.int32)
    experts_here = far_here * plane + jnp.arange(plane, dtype=jnp.int32)
    names = jnp.any(seen[:, :, None] == experts_here[None, None, :], axis=1)
    names = names.reshape(far, tok, plane).astype(jnp.int32)
    nth = jnp.cumsum(names, axis=1) - names
    chosen = (names[None] > 0) & (nth[None] == jnp.arange(cap, dtype=jnp.int32)[:, None, None, None])
    chosen = chosen.transpose(3, 1, 0, 2)
    picking = (
        chosen[:, :, :, None, :]
        & (jnp.arange(far)[:, None] == jnp.arange(far)[None, :])[None, :, None, :, None]
    )
    picking = picking.astype(BF16).reshape(slots_here, far * tok)
    picking, got = lax.optimization_barrier((picking, got))
    relay_rows = dot(picking, gathered[:, 128:]).astype(BF16)
    got_relay = exchange(
        relay_rows.reshape(plane, far * cap, CORES * relayed), ("near", "x")
    ).reshape(slots_here, CORES * relayed)

    swap = [(0, 1), (1, 0)]
    acts = got[:, :ffw]
    both_acts = jnp.concatenate([acts, lax.ppermute(acts, "core", swap)], axis=0)
    weight = down_weight[0].reshape(ys, CORES, piece, ffw).transpose(1, 0, 2, 3)
    weight = weight.reshape(CORES, half, ffw)
    got_relay, both_acts, weight = lax.optimization_barrier((got_relay, both_acts, weight))

    halves = [
        jnp.concatenate(
            [
                got[:, ffw + c * DIRECT : ffw + (c + 1) * DIRECT],
                got_relay[:, c * relayed : (c + 1) * relayed],
            ],
            axis=1,
        )
        for c in range(CORES)
    ]
    mine = jnp.where(core == 0, halves[0], halves[1])
    theirs = jnp.where(core == 0, halves[1], halves[0])

    rows_dim = (((0,), (0,)), ((), ()))
    both_grads = jnp.concatenate([mine, lax.ppermute(theirs, "core", swap)], axis=0)
    partial_value = dot(both_grads, both_acts, rows_dim).astype(BF16)
    grad_down = lax.psum_scatter(partial_value, "y", scatter_dimension=0, tiled=True)

    projected = sum(dot(halves[c], weight[c]) for c in range(CORES)).astype(BF16)
    returned = exchange(
        projected.reshape(owners, 2, cap * ffw // 2), ("near", "x", "far")
    ).reshape(slots_here, ffw)
    back = dot(placing, returned, rows_dim).reshape(tok, topk, ffw)
    grad_hidden = (combine[:, :, None] * back).astype(BF16)
    grad_weights = jnp.sum(hidden.astype(F32) * back, axis=2)
    return (grad_hidden, grad_weights, grad_down[None])


def solution(mesh):
    dp, expert = mesh.shape["dp"], mesh.shape["expert"]
    shape = (dp // CORES, CORES, expert // (XS * PAIR), PAIR, XS)
    fine = Mesh(mesh.devices.reshape(shape), ("y", "core", "far", "near", "x"))
    tokens = ("y", "core", "far", "near", "x")
    owner = ("far", "near", "x")
    placed = (
        P(tokens, None),
        P(tokens, None, None),
        P(tokens, None),
        P(tokens, None),
        P(owner, None, None),
    )
    return jax.shard_map(
        local,
        mesh=fine,
        in_specs=placed,
        out_specs=(
            P(tokens, None, None),
            P(tokens, None),
            P(owner, ("y", "core"), None),
        ),
        check_vma=False,
    )
```

time: 195 us -> 175 us (0.90)
  waiting for transfers between devices: 92 us -> 19.4 us
  blocking collectives: 34 us -> 79 us
  matrix products: 8.12 us -> 13 us
  local copies, waits for them, and re-layouts: 11 us -> 13.9 us
    all_gather x1 -> x0, waiting for transfers between devices: 71.9 us -> none  [local(): relay_all = lax.all_gather(relay_send, 'z', axis=0, tiled=True)]
    all_gather x0 -> x1, blocking collectives: none -> 49.8 us  [local(): lax.all_gather(jnp.concatenate([ids_wide, by_core[:, 0, DIRECT:], by_core...]
    transpose x0 -> x1, local copies, waits for them, and re-layouts: none -> 6 us  [local(): weight = down_weight[0].reshape(ys, CORES, piece, ffw).transpose(1, 0, 2, 3)]
    dot_general x7, matrix products: 8.12 us -> 13 us  [dot(): return lax.dot_general(a, b, dims, preferred_element_type=F32)]
    all_to_all x1, blocking collectives: 34 us -> 29.2 us  [exchange(): return lax.all_to_all(value, axes, split_axis=0, concat_axis=0, tiled=True)]
    slice x4 -> x3, local copies, waits for them, and re-layouts: 4.35 us -> 0.76 us  [the longest x1 0.64 us: local(): got[:, ffw + c * DIRECT:ffw + (c + 1) * DIRECT]]
    all_to_all x2, waiting for transfers between devices: 8.61 us -> 6.37 us  [exchange(): return lax.all_to_all(value, axes, split_axis=0, concat_axis=0, tiled=True)]
  transfers between devices with their start and end apart: 6 -> 5, of which waited for: 4 -> 3; matrix products, arithmetic and copies ran while one was open for 8% -> 9% of each run, Pallas kernels for 0% -> 0%
where the time goes in v3:
time: 175 us
  blocking collectives  79 us (45%)
  starting transfers between devices  33 us (19%)
  waiting for transfers between devices  19.4 us (11%)
  between operations  14.3 us (8%)
  local copies, waits for them, and re-layouts  13.9 us (8%)
  matrix products  13 us (7%)
  other arithmetic  1.96 us (1%)
    all_gather x1, blocking collectives, local(): lax.all_gather(jnp.concatenate([ids_wide, by_core[:, 0, DIRECT:], by_core...  49.8 us
    all_to_all x1, blocking collectives, exchange(): return lax.all_to_all(value, axes, split_axis=0, concat_axis=0, tiled=True)  29.2 us
    all_to_all x2, starting transfers between devices, exchange(): return lax.all_to_all(value, axes, split_axis=0, concat_axis=0, tiled=True)  29.1 us
    dot_general x7, matrix products, dot(): return lax.dot_general(a, b, dims, preferred_element_type=F32)  13 us
    reduce_scatter x1, waiting for transfers between devices, local(): lax.psum_scatter(partial_value, 'y', scatter_dimension=0, tiled=True)  10.8 us
    all_to_all x2, waiting for transfers between devices, exchange(): return lax.all_to_all(value, axes, split_axis=0, concat_axis=0, tiled=True)  6.37 us
    transpose x1, local copies, waits for them, and re-layouts, local(): weight = down_weight[0].reshape(ys, CORES, piece, ffw).transpose(1, 0, 2, 3)  6 us
    unnamed x17, local copies, waits for them, and re-layouts  3.83 us
  transfers between devices with their start and end apart: 5, of which 3 were waited for; matrix products, arithmetic and copies ran while one was open for 9% of the time, Pallas kernels for 0%

profile of v3, /device:TPU:6, one launch (start us, length us, event | category | flops | bytes accessed | tf_op | source)
XLA Modules:
  0.0 174.6 jit_solution(15775354140900236517)
XLA Ops:
  7.2 0.8 copy.87
  7.9 0.1 reshape.232
  8.0 0.1 fusion.32
  8.1 0.2 reduce_window_sum.22
  8.3 0.2 select_reduce_fusion
  8.5 0.1 reduce_sum.33
  8.6 0.8 copy.86
  9.4 0.1 fusion.30
  9.5 1.0 reshape.233
  10.5 0.1 reshape.234
  10.6 0.2 convolution_convert_fusion.3
  10.8 1.2 convolution_convert_fusion.2
  12.1 0.9 reshape.237
  13.0 22.3 %all-to-all-start = ((bf16[64,24,128]{2,1,0:T(8,128)(2,1)}), bf16[64,24,128]{2,1,0:T(8,128)(2,1)S(1)}, u32[]{:S(2)}, u32[]{:S(2)}) async-start(bf16[64,24,128]{2,1,0:T(8,128)(2,1)} %reshape.237), calls=%async_computation | async-start | bytes 786432 | tf_op jit(solution)/shard_map/all_to_all | solution.py:20
  35.4 0.1 copy.102
  35.5 49.8 %all_gather.3 = bf16[128,3968]{1,0:T(8,128)(2,1)S(1)} all-gather(bf16[16,3968]{1,0:T(8,128)(2,1)S(1)} %fusion.29), channel_id=1, replica_groups=mesh['y'=8,'core'=2,'far'=8,'near'=2,'x'=4] {'far'}, dimensions={0}, use_global_device_ids=true | all-gather | bytes 1142784 | tf_op jit(solution)/shard_map/all_gather | solution.py:62
  85.3 0.1 copy.101
  85.4 0.1 compare_reduce_fusion
  85.4 0.1 reshape.244
  85.5 0.1 copy.95
  85.6 0.7 fusion.15
  86.3 0.1 copy.97
  86.4 0.1 fusion.26
  86.5 0.2 and_convert_fusion
  86.7 0.3 reshape.245
  87.0 0.2 reshape.238
  87.1 1.6 convolution_convert_fusion
  88.8 6.8 %all-to-all-start.1 = ((bf16[8,24,3840]{2,1,0:T(8,128)(2,1)}), bf16[8,24,3840]{2,1,0:T(8,128)(2,1)S(1)}, u32[]{:S(2)}, u32[]{:S(2)}) async-start(bf16[8,24,3840]{2,1,0:T(8,128)(2,1)} %bitcast.7), calls=%async_computation.1 | async-start | bytes 2949120 | tf_op jit(solution)/shard_map/all_to_all | solution.py:20
  95.7 1.9 %collective-permute-start = (bf16[192,768]{1,0:T(8,128)(2,1)S(1)}, bf16[192,768]{1,0:T(8,128)(2,1)S(1)}, u32[]{:S(2)}, u32[]{:S(2)}) collective-permute-start(bf16[192,768]{1,0:T(8,128)(2,1)S(1)} %slice.42), channel_id=1, source_target_pairs={{0,64},{64,0},{1,65},{65,1},{2,66},{66,2},{3,67},{67,3},{4,68},{68... | collective-permute-start | bytes 884744 | tf_op jit(solution)/shard_map/ppermute | solution.py:89
  97.6 6.0 %copy.99 = bf16[2,8,256,768]{3,2,1,0:T(8,128)(2,1)} copy(bf16[2,8,256,768]{3,2,0,1:T(8,128)(2,1)} %bitcast.56) | data formatting | bytes 12582912 | tf_op jit(solution)/shard_map/transpose | solution.py:90
  103.6 0.6 fusion.50
  104.3 6.4 %all-to-all-done.1 = bf16[8,24,3840]{2,1,0:T(8,128)(2,1)S(1)} async-done(((bf16[8,24,3840]{2,1,0:T(8,128)(2,1)}), bf16[8,24,3840]{2,1,0:T(8,128)(2,1)S(1)}, u32[]{:S(2)}, u32[]{:S(2)}) %all-to-all-start.1) | async-done | bytes 1474592 | tf_op jit(solution)/shard_map/all_to_all | solution.py:20
  110.7 0.1 fusion.49
  110.8 0.7 copy-done.1
  111.5 0.0 copy-done.3
  111.5 0.3 broadcast_select_fusion.1
  111.7 1.9 %collective-permute-start.1 = (bf16[192,2048]{1,0:T(8,128)(2,1)S(1)}, bf16[192,2048]{1,0:T(8,128)(2,1)S(1)}, u32[]{:S(2)}, u32[]{:S(2)}) collective-permute-start(bf16[192,2048]{1,0:T(8,128)(2,1)S(1)} %get-tuple-element.26), channel_id=1, source_target_pairs={{0,64},{64,0},{1,65},{65,1},{2,66},{66,2},{3,67},{67,3},{4,68},{68... | collective-permute-start | bytes 2359304 | tf_op jit(solution)/shard_map/ppermute | solution.py:108
  113.7 2.3 %collective-permute-done.1 = bf16[192,2048]{1,0:T(8,128)(2,1)S(1)} collective-permute-done((bf16[192,2048]{1,0:T(8,128)(2,1)S(1)}, bf16[192,2048]{1,0:T(8,128)(2,1)S(1)}, u32[]{:S(2)}, u32[]{:S(2)}) %collective-permute-start.1) | collective-permute-done | bytes 786464 | tf_op jit(solution)/shard_map/ppermute | solution.py:108
  115.9 3.5 %convolution_convert_fusion.1 = bf16[2048,768]{1,0:T(8,128)(2,1)} fusion(bf16[384,768]{1,0:T(8,128)(2,1)S(1)} %pad_maximum_fusion.2, bf16[192,2048]{1,0:T(8,128)(2,1)S(1)} %collective-permute-done.1, bf16[192,2048]{1,0:T(8,128)(2,1)S(1)} %get-tuple-element.25), kind=kOutput, calls=%fused_computation.1 | convolution fusion | flops 1212678144 | bytes 5308416 | tf_op jit(solution)/shard_map/dot_general | solution.py:16
  119.5 0.8 copy-done.4
  120.3 2.7 %fusion = f32[192,768]{1,0:T(8,128)S(1)} fusion(bf16[2,2048,768]{2,1,0:T(8,128)(2,1)} %bitcast.57, bf16[192,1920]{1,0:T(8,128)(2,1)S(1)} %get-tuple-element.28, bf16[192,128]{1,0:T(8,128)(2,1)S(1)} %copy-done.4), kind=kOutput, calls=%fused_computation.2 | convolution fusion | flops 605552640 | bytes 4521984 | tf_op jit(solution)/shard_map/dot_general | solution.py:16
  123.0 2.7 %fusion.12 = bf16[192,768]{1,0:T(8,128)(2,1)S(1)} fusion(f32[192,768]{1,0:T(8,128)S(1)} %fusion, bf16[2,2048,768]{2,1,0:T(8,128)(2,1)} %bitcast.58, bf16[192,1920]{1,0:T(8,128)(2,1)S(1)} %get-tuple-element.27, bf16[192,128]{1,0:T(8,128)(2,1)S(1)} %copy-done.2), kind=kOutput, calls=%fused_computation.12 | convolution fusion | flops 605847552 | bytes 4816896 | tf_op jit(solution)/shard_map/dot_general | solution.py:16
  125.7 0.2 reshape.242
  125.8 29.2 %all_to_all.15 = bf16[64,2,1152]{2,1,0:T(2,128)(2,1)S(1)} all-to-all(bf16[64,2,1152]{2,1,0:T(2,128)(2,1)S(1)} %reshape.242), channel_id=1, replica_groups=mesh['y'=8,'core'=2,'far'=8,'near'=2,'x'=4] {'near','x','far'}, dimensions={0} | all-to-all | bytes 589824 | tf_op jit(solution)/shard_map/all_to_all | solution.py:20
  155.1 0.2 reshape.246
  155.3 1.0 fusion.18
  156.3 0.7 copy.100
  157.0 10.8 %reduce-scatter.2.cloned.1.call-done = bf16[256,768]{1,0:T(8,128)(2,1)} async-done(((bf16[2048,768]{1,0:T(8,128)(2,1)}), bf16[256,768]{1,0:T(8,128)(2,1)}) %reduce-scatter.2.cloned.1.call-update) | async-done | bytes 393232 | tf_op jit(solution)/shard_map/reduce_scatter | solution.py:110
  (29 shorter events, 0.3 us)
Async XLA Ops:
  10.5 24.8 %copy-start.5 = (s32[16,8]{0,1:T(8,128)S(1)}, s32[16,8]{0,1:T(8,128)}, u32[]{:S(2)}) copy-start(s32[16,8]{0,1:T(8,128)} %param.8) | copy-start | bytes 1540
  13.0 73.9 %all-to-all-start = ((bf16[64,24,128]{2,1,0:T(8,128)(2,1)}), bf16[64,24,128]{2,1,0:T(8,128)(2,1)S(1)}, u32[]{:S(2)}, u32[]{:S(2)}) async-start(bf16[64,24,128]{2,1,0:T(8,128)(2,1)} %reshape.237), calls=%async_computation | async-start | bytes 786432 | tf_op jit(solution)/shard_map/all_to_all | solution.py:20
  88.8 21.9 %all-to-all-start.1 = ((bf16[8,24,3840]{2,1,0:T(8,128)(2,1)}), bf16[8,24,3840]{2,1,0:T(8,128)(2,1)S(1)}, u32[]{:S(2)}, u32[]{:S(2)}) async-start(bf16[8,24,3840]{2,1,0:T(8,128)(2,1)} %bitcast.7), calls=%async_computation.1 | async-start | bytes 2949120 | tf_op jit(solution)/shard_map/all_to_all | solution.py:20
  95.6 72.1 %reduce-scatter.2.cloned.1.call-start = ((), (), s32[]{:S(2)}) async-start(), calls=%async_computation.4 | async-start | bytes 3538944 | tf_op jit(solution)/shard_map/reduce_scatter | solution.py:110
  95.7 8.6 %collective-permute-start = (bf16[192,768]{1,0:T(8,128)(2,1)S(1)}, bf16[192,768]{1,0:T(8,128)(2,1)S(1)}, u32[]{:S(2)}, u32[]{:S(2)}) collective-permute-start(bf16[192,768]{1,0:T(8,128)(2,1)S(1)} %slice.42), channel_id=1, source_target_pairs={{0,64},{64,0},{1,65},{65,1},{2,66},{66,2},{3,67},{67,3},{4,68},{68... | collective-permute-start | bytes 884744 | tf_op jit(solution)/shard_map/ppermute | solution.py:89
  110.7 0.8 copy-start.1
  110.7 0.8 copy-start.3
  111.7 4.2 %collective-permute-start.1 = (bf16[192,2048]{1,0:T(8,128)(2,1)S(1)}, bf16[192,2048]{1,0:T(8,128)(2,1)S(1)}, u32[]{:S(2)}, u32[]{:S(2)}) collective-permute-start(bf16[192,2048]{1,0:T(8,128)(2,1)S(1)} %get-tuple-element.26), channel_id=1, source_target_pairs={{0,64},{64,0},{1,65},{65,1},{2,66},{66,2},{3,67},{67,3},{4,68},{68... | collective-permute-start | bytes 2359304 | tf_op jit(solution)/shard_map/ppermute | solution.py:108
  119.5 0.8 copy-start.4
  120.3 2.7 %copy-start.2 = (bf16[192,128]{1,0:T(8,128)(2,1)S(1)}, bf16[192,128]{1,0:T(8,128)(2,1)}, u32[]{:S(2)}) copy-start(bf16[192,128]{1,0:T(8,128)(2,1)} %get-tuple-element.31) | copy-start | bytes 147460
  125.6 29.6 %copy-start = (bf16[16,8,768]{2,1,0:T(8,128)(2,1)S(1)}, bf16[16,8,768]{2,1,0:T(8,128)(2,1)}, u32[]{:S(2)}) copy-start(bf16[16,8,768]{2,1,0:T(8,128)(2,1)} %param.6) | copy-start | bytes 589828
Sparse Core Ops, SparseCore 0:
  119.6 48.0 reduce-scatter.1

commit v4 on v3

v4 whole, which is shorter than its diff:
```python
import jax
import jax.numpy as jnp
from jax import lax
from jax.sharding import Mesh
from jax.sharding import PartitionSpec as P

CORES = 2
XS = 4
PAIR = 2
DIRECT = 128
F32 = jnp.float32
BF16 = jnp.bfloat16
ROWS = (((0,), (0,)), ((), ()))


def dot(a, b, dims=(((1,), (0,)), ((), ()))):
    return lax.dot_general(a, b, dims, preferred_element_type=F32)


def exchange(value, axes):
    return lax.all_to_all(value, axes, split_axis=0, concat_axis=0, tiled=True)


def local(out_grad, hidden, combine, expert_ids, down_weight):
    tok, width = out_grad.shape
    topk = expert_ids.shape[1]
    ffw = hidden.shape[2]
    xs, ys = lax.axis_size("x"), lax.axis_size("y")
    far, near = lax.axis_size("far"), lax.axis_size("near")
    core, far_here = lax.axis_index("core"), lax.axis_index("far")
    owners = far * near * xs
    plane = near * xs
    cap = min(tok, 3 * tok * topk // (2 * owners))
    rows = tok * topk
    slots_here = owners * cap
    half = width // CORES
    piece = half // ys

    flat_ids = expert_ids.reshape(rows)
    onehot = (flat_ids[:, None] == jnp.arange(owners, dtype=jnp.int32)[None, :]).astype(jnp.int32)
    before = jnp.cumsum(onehot, axis=0) - onehot
    slot = jnp.sum(onehot * before, axis=1)
    target = flat_ids * cap + slot
    all_slots = jnp.arange(slots_here, dtype=jnp.int32)[:, None]
    placing = (target[None, :] == all_slots).astype(BF16)
    weighted = (combine[:, :, None] * hidden.astype(F32)).astype(BF16).reshape(rows, ffw)

    by_core = (
        out_grad.reshape(tok, ys, CORES, piece).transpose(0, 2, 1, 3).reshape(tok, CORES, half)
    )
    direct = jnp.concatenate(
        [out_grad[:, c * piece : c * piece + DIRECT] for c in range(CORES)], axis=1
    )
    direct = jnp.broadcast_to(direct[:, None, :], (tok, topk, CORES * DIRECT))
    send = dot(
        placing, jnp.concatenate([weighted, direct.reshape(rows, CORES * DIRECT)], axis=1)
    ).astype(BF16)
    got = exchange(send.reshape(far, plane * cap, send.shape[1]), "far")

    slots_wide = jnp.pad(target.reshape(tok, topk).astype(BF16), ((0, 0), (0, 128 - topk)))
    gathered = lax.all_gather(
        jnp.concatenate([slots_wide, by_core[:, 0, DIRECT:], by_core[:, 1, DIRECT:]], axis=1),
        "far",
        axis=0,
        tiled=True,
    )

    row = jnp.arange(slots_here, dtype=jnp.int32)
    row_far = row // cap % far
    row_slot = (far_here * plane + row // (cap * far)) * cap + row % cap
    seen = gathered[:, :topk].astype(jnp.int32).T
    picking = jnp.any(seen[:, None, :] == row_slot[None, :, None], axis=0)
    column_far = jnp.arange(far * tok, dtype=jnp.int32) // tok
    picking = (picking & (row_far[:, None] == column_far[None, :])).astype(BF16)
    column = jnp.arange(slots_here, dtype=jnp.int32)
    turning = row_far * (plane * cap) + row // (cap * far) * cap + row % cap
    turning = (turning[:, None] == column[None, :]).astype(BF16)
    picking, got = lax.optimization_barrier((picking, got))
    near_rows = dot(turning, got.reshape(slots_here, ffw + CORES * DIRECT)).astype(BF16)
    relayed = half - DIRECT
    relay_send = jnp.stack(
        [
            jnp.concatenate(
                [
                    near_rows[:, ffw + c * DIRECT : ffw + (c + 1) * DIRECT],
                    dot(
                        picking, gathered[:, 128 + c * relayed : 128 + (c + 1) * relayed]
                    ).astype(BF16),
                    near_rows[:, :ffw],
                ],
                axis=1,
            )
            for c in range(CORES)
        ]
    )
    relay = exchange(
        relay_send.reshape(CORES * plane, far * cap, half + ffw), ("core", "near", "x")
    ).reshape(CORES * slots_here, half + ffw)

    weight = lax.dynamic_index_in_dim(
        down_weight[0].reshape(ys, CORES, piece, ffw), core, 1, keepdims=False
    ).reshape(half, ffw)
    relay, weight = lax.optimization_barrier((relay, weight))

    grads, acts = relay[:, :half], relay[:, half:]
    partial_value = dot(grads, acts, ROWS).astype(BF16)
    grad_down = lax.psum_scatter(partial_value, "y", scatter_dimension=0, tiled=True)

    halves = dot(grads, weight).reshape(CORES, slots_here, ffw)
    mine = lax.dynamic_index_in_dim(halves, core, 0, keepdims=False)
    theirs = lax.dynamic_index_in_dim(halves, 1 - core, 0, keepdims=False).astype(BF16)
    theirs = lax.ppermute(theirs, "core", [(0, 1), (1, 0)])
    projected = (mine + theirs.astype(F32)).astype(BF16)
    returned = exchange(
        projected.reshape(owners, 2, cap * ffw // 2), ("near", "x", "far")
    ).reshape(slots_here, ffw)
    back_target = (flat_ids % plane * far + flat_ids // plane) * cap + slot
    back_placing = (back_target[None, :] == all_slots).astype(BF16)
    back = dot(back_placing, returned, ROWS).reshape(tok, topk, ffw)
    grad_hidden = (combine[:, :, None] * back).astype(BF16)
    grad_weights = jnp.sum(hidden.astype(F32) * back, axis=2)
    return (grad_hidden, grad_weights, grad_down[None])


def solution(mesh):
    dp, expert = mesh.shape["dp"], mesh.shape["expert"]
    shape = (dp // CORES, CORES, expert // (XS * PAIR), PAIR, XS)
    fine = Mesh(mesh.devices.reshape(shape), ("y", "core", "far", "near", "x"))
    tokens = ("y", "core", "far", "near", "x")
    owner = ("far", "near", "x")
    placed = (
        P(tokens, None),
        P(tokens, None, None),
        P(tokens, None),
        P(tokens, None),
        P(owner, None, None),
    )
    return jax.shard_map(
        local,
        mesh=fine,
        in_specs=placed,
        out_specs=(
            P(tokens, None, None),
            P(tokens, None),
            P(owner, ("y", "core"), None),
        ),
        check_vma=False,
    )
```

time: 175 us -> 182 us (1.040)
  waiting for transfers between devices: 19.4 us -> 37.4 us
  local copies, waits for them, and re-layouts: 13.9 us -> 5.89 us
  starting transfers between devices: 33 us -> 26.8 us
  blocking collectives: 79 us -> 82.6 us
  matrix products: 13 us -> 10.8 us
    all_to_all x2, waiting for transfers between devices: 6.37 us -> 25.8 us  [exchange(): return lax.all_to_all(value, axes, split_axis=0, concat_axis=0, tiled=True)]
    transpose x1, local copies, waits for them, and re-layouts: 6 us -> 0.05 us  [local(): seen = gathered[:, :topk].astype(jnp.int32).T]
    all_to_all x2, starting transfers between devices: 29.1 us -> 24.8 us  [exchange(): return lax.all_to_all(value, axes, split_axis=0, concat_axis=0, tiled=True)]
    dot_general x7, matrix products: 13 us -> 10.8 us  [dot(): return lax.dot_general(a, b, dims, preferred_element_type=F32)]
    dynamic_slice x0 -> x1, local copies, waits for them, and re-layouts: none -> 2.1 us  [local(): lax.dynamic_index_in_dim(down_weight[0].reshape(ys, CORES, piece, ffw), c...]
    all_to_all x1, blocking collectives: 29.2 us -> 31.3 us  [exchange(): return lax.all_to_all(value, axes, split_axis=0, concat_axis=0, tiled=True)]
    ppermute x2 -> x1, starting transfers between devices: 3.84 us -> 2.05 us  [local(): theirs = lax.ppermute(theirs, 'core', [(0, 1), (1, 0)])]
    unnamed x17 -> x7, local copies, waits for them, and re-layouts: 3.83 us -> 2.22 us
  transfers between devices with their start and end apart: 5 -> 4, of which waited for: 3 -> 3; matrix products, arithmetic and copies ran while one was open for 9% -> 4% of each run, Pallas kernels for 0% -> 0%
where the time goes in v4:
time: 182 us; the launch traced here: 181 us
  blocking collectives  82.6 us (45%)
  waiting for transfers between devices  37.4 us (21%)
  starting transfers between devices  26.8 us (15%)
  between operations  14.3 us (8%)
  matrix products  10.8 us (6%)
  local copies, waits for them, and re-layouts  5.89 us (3%)
  other arithmetic  3.59 us (2%)
    all_gather x1, blocking collectives, local(): lax.all_gather(jnp.concatenate([slots_wide, by_core[:, 0, DIRECT:], by_co...  51.3 us
    all_to_all x1, blocking collectives, exchange(): return lax.all_to_all(value, axes, split_axis=0, concat_axis=0, tiled=True)  31.3 us
    all_to_all x2, waiting for transfers between devices, exchange(): return lax.all_to_all(value, axes, split_axis=0, concat_axis=0, tiled=True)  25.8 us
    all_to_all x2, starting transfers between devices, exchange(): return lax.all_to_all(value, axes, split_axis=0, concat_axis=0, tiled=True)  24.8 us
    dot_general x7, matrix products, dot(): return lax.dot_general(a, b, dims, preferred_element_type=F32)  10.8 us
    reduce_scatter x1, waiting for transfers between devices, local(): lax.psum_scatter(partial_value, 'y', scatter_dimension=0, tiled=True)  10.1 us
  transfers between devices with their start and end apart: 4, of which 3 were waited for; matrix products, arithmetic and copies ran while one was open for 4% of the time, Pallas kernels for 0%

profile of v4, /device:TPU:6, one launch (start us, length us, event | category | flops | bytes accessed | tf_op | source)
XLA Modules:
  0.0 181.5 jit_solution(11665913686045065259)
XLA Ops:
  7.2 0.0 copy-start.1
  7.2 0.8 copy.36
  8.0 0.8 copy.37
  8.7 0.1 reshape.212
  8.8 0.7 fusion.40
  9.5 0.1 fusion.24
  9.6 0.2 reduce_window_sum.11
  9.8 0.2 select_reduce_fusion
  10.0 1.0 fusion.16
  11.0 1.0 convolution_convert_fusion.4
  12.0 18.7 %all-to-all-start = ((bf16[8,24,1024]{2,1,0:T(8,128)(2,1)}), bf16[8,24,1024]{2,1,0:T(8,128)(2,1)S(1)}, u32[]{:S(2)}, u32[]{:S(2)}) async-start(bf16[8,24,1024]{2,1,0:T(8,128)(2,1)} %bitcast.7), calls=%async_computation | async-start | bytes 786432 | tf_op jit(solution)/shard_map/all_to_all | solution.py:21
  30.8 0.1 reduce_sum.21
  30.9 0.0 copy-done.1
  30.9 0.1 reshape.213
  31.0 0.1 reshape.214
  31.1 51.3 %all_gather.3 = bf16[128,3968]{1,0:T(8,128)(2,1)S(1)} all-gather(bf16[16,3968]{1,0:T(8,128)(2,1)S(1)} %fusion.21), channel_id=1, replica_groups=mesh['y'=8,'core'=2,'far'=8,'near'=2,'x'=4] {'far'}, dimensions={0}, use_global_device_ids=true | all-gather | bytes 1142784 | tf_op jit(solution)/shard_map/all_gather | solution.py:61
  82.6 0.2 compare_reduce_fusion
  82.8 0.1 and_convert_fusion
  82.9 0.0 all-to-all-done
  82.9 0.3 convolution_convert_fusion.3
  83.2 0.4 convolution_convert_fusion.1
  83.6 0.4 convolution_convert_fusion.2
  84.0 0.2 fusion.3
  84.1 1.5 pad_maximum_fusion
  85.7 6.0 %all-to-all-start.1 = ((bf16[16,24,2816]{2,1,0:T(8,128)(2,1)}), bf16[16,24,2816]{2,1,0:T(8,128)(2,1)}, u32[]{:S(2)}, u32[]{:S(2)}) async-start(bf16[16,24,2816]{2,1,0:T(8,128)(2,1)} %bitcast.11), calls=%async_computation.1 | async-start | bytes 4325376 | tf_op jit(solution)/shard_map/all_to_all | solution.py:21
  91.7 0.0 reduce-scatter.2.cloned.1.call-start
  91.7 2.1 %constant_dynamic-slice_fusion = bf16[8,1,256,768]{3,2,1,0:T(8,128)(2,1)S(1)} fusion(bf16[8,2,256,768]{3,2,1,0:T(8,128)(2,1)} %bitcast.46, s32[]{:T(128)S(6)} %select_n.104), kind=kLoop, calls=%fused_computation.88 | loop fusion | bytes 6291460 | tf_op jit(solution)/shard_map/jit(dynamic_index_in_dim)/dynamic_slice | solution.py:100
  93.8 25.8 %all-to-all-done.1 = bf16[16,24,2816]{2,1,0:T(8,128)(2,1)} async-done(((bf16[16,24,2816]{2,1,0:T(8,128)(2,1)}), bf16[16,24,2816]{2,1,0:T(8,128)(2,1)}, u32[]{:S(2)}, u32[]{:S(2)}) %all-to-all-start.1) | async-done | bytes 2162720 | tf_op jit(solution)/shard_map/all_to_all | solution.py:21
  119.6 5.0 %convolution_convert_fusion = bf16[2048,768]{1,0:T(8,128)(2,1)} fusion(bf16[384,2816]{1,0:T(8,128)(2,1)} %bitcast.12), kind=kOutput, calls=%fused_computation | convolution fusion | flops 1209532416 | bytes 5308416 | tf_op jit(solution)/shard_map/dot_general | solution.py:17
  124.6 0.0 reduce-scatter.2.cloned.1.call-update
  124.7 2.8 %fusion.1 = f32[384,768]{1,0:T(8,128)S(1)} fusion(bf16[2048,768]{1,0:T(8,128)(2,1)S(1)} %bitcast.45, bf16[384,2816]{1,0:T(8,128)(2,1)} %bitcast.12), kind=kOutput, calls=%fused_computation.5 | convolution fusion | flops 1207959552 | bytes 5898240 | tf_op jit(solution)/shard_map/dot_general | solution.py:17
  127.4 0.0 copy-start
  127.5 2.1 %collective-permute-start = (bf16[192,768]{1,0:T(8,128)(2,1)S(1)}, bf16[192,768]{1,0:T(8,128)(2,1)S(1)}, u32[]{:S(2)}, u32[]{:S(2)}) collective-permute-start(bf16[192,768]{1,0:T(8,128)(2,1)S(1)} %fusion.11), channel_id=1, source_target_pairs={{0,64},{64,0},{1,65},{65,1},{2,66},{66,2},{3,67},{67,3},{4,68},{68... | collective-permute-start | bytes 884744 | tf_op jit(solution)/shard_map/ppermute | solution.py:112
  129.6 1.5 collective-permute-done
  131.1 0.1 fusion.5
  131.2 0.2 reshape.223
  131.4 31.3 %all_to_all.15 = bf16[64,2,1152]{2,1,0:T(2,128)(2,1)S(1)} all-to-all(bf16[64,2,1152]{2,1,0:T(2,128)(2,1)S(1)} %reshape.223), channel_id=1, replica_groups=mesh['y'=8,'core'=2,'far'=8,'near'=2,'x'=4] {'near','x','far'}, dimensions={0} | all-to-all | bytes 589824 | tf_op jit(solution)/shard_map/all_to_all | solution.py:21
  162.7 0.2 reshape.225
  162.9 0.0 copy-done
  162.9 1.0 fusion.10
  163.9 0.7 copy.45
  164.5 10.1 %reduce-scatter.2.cloned.1.call-done = bf16[256,768]{1,0:T(8,128)(2,1)} async-done(((bf16[2048,768]{1,0:T(8,128)(2,1)}), bf16[256,768]{1,0:T(8,128)(2,1)}) %reduce-scatter.2.cloned.1.call-update) | async-done | bytes 393232 | tf_op jit(solution)/shard_map/reduce_scatter | solution.py:107
  (16 shorter events, 0.3 us)
Async XLA Ops:
  7.2 23.7 %copy-start.1 = (bf16[16,4096]{1,0:T(8,128)(2,1)S(1)}, bf16[16,4096]{1,0:T(8,128)(2,1)}, u32[]{:S(2)}) copy-start(bf16[16,4096]{1,0:T(8,128)(2,1)} %param.5) | copy-start | bytes 393220
  12.0 70.8 %all-to-all-start = ((bf16[8,24,1024]{2,1,0:T(8,128)(2,1)}), bf16[8,24,1024]{2,1,0:T(8,128)(2,1)S(1)}, u32[]{:S(2)}, u32[]{:S(2)}) async-start(bf16[8,24,1024]{2,1,0:T(8,128)(2,1)} %bitcast.7), calls=%async_computation | async-start | bytes 786432 | tf_op jit(solution)/shard_map/all_to_all | solution.py:21
  85.7 33.9 %all-to-all-start.1 = ((bf16[16,24,2816]{2,1,0:T(8,128)(2,1)}), bf16[16,24,2816]{2,1,0:T(8,128)(2,1)}, u32[]{:S(2)}, u32[]{:S(2)}) async-start(bf16[16,24,2816]{2,1,0:T(8,128)(2,1)} %bitcast.11), calls=%async_computation.1 | async-start | bytes 4325376 | tf_op jit(solution)/shard_map/all_to_all | solution.py:21
  91.7 82.9 %reduce-scatter.2.cloned.1.call-start = ((), (), s32[]{:S(2)}) async-start(), calls=%async_computation.4 | async-start | bytes 3538944 | tf_op jit(solution)/shard_map/reduce_scatter | solution.py:107
  127.4 35.4 %copy-start = (bf16[16,8,768]{2,1,0:T(8,128)(2,1)S(1)}, bf16[16,8,768]{2,1,0:T(8,128)(2,1)}, u32[]{:S(2)}) copy-start(bf16[16,8,768]{2,1,0:T(8,128)(2,1)} %param.6) | copy-start | bytes 589828
  127.5 3.6 %collective-permute-start = (bf16[192,768]{1,0:T(8,128)(2,1)S(1)}, bf16[192,768]{1,0:T(8,128)(2,1)S(1)}, u32[]{:S(2)}, u32[]{:S(2)}) collective-permute-start(bf16[192,768]{1,0:T(8,128)(2,1)S(1)} %fusion.11), channel_id=1, source_target_pairs={{0,64},{64,0},{1,65},{65,1},{2,66},{66,2},{3,67},{67,3},{4,68},{68... | collective-permute-start | bytes 884744 | tf_op jit(solution)/shard_map/ppermute | solution.py:112
Sparse Core Ops, SparseCore 0:
  124.8 49.7 reduce-scatter.1

commit v5 on v3

v5 whole, which is shorter than its diff:
```python
import functools

import jax
import jax.numpy as jnp
from jax import lax
from jax.experimental import pallas as pl
from jax.experimental.pallas import tpu as pltpu
from jax.sharding import Mesh
from jax.sharding import PartitionSpec as P

CORES = 2
XS = 4
PAIR = 2
DIRECT = 128
LANES = 128
F32 = jnp.float32
BF16 = jnp.bfloat16
ROWS = (((0,), (0,)), ((), ()))


def dot(a, b, dims=(((1,), (0,)), ((), ()))):
    return lax.dot_general(a, b, dims, preferred_element_type=F32)


def exchange(value, axes):
    return lax.all_to_all(value, axes, split_axis=0, concat_axis=0, tiled=True)


def over(number, by):
    return (number * (512 // by + 1)) >> 9


def iota(shape, dim):
    return lax.broadcasted_iota(jnp.int32, shape, dim)


def pack_kernel(owners, cap, pieces, owner_ref, combine_ref, hidden_ref, grad_ref, send_ref, pack_ref):
    topk, tok = owner_ref.shape
    pairs, ffw = hidden_ref.shape
    slots = owners * cap
    owner = owner_ref[...]
    wide = iota((LANES, tok), 0)
    names = sum((wide == owner[k : k + 1, :]).astype(F32) for k in range(topk))
    earlier = (iota((tok, tok), 0) < iota((tok, tok), 1)).astype(BF16)
    nth = dot(names.astype(BF16), earlier)
    row = iota((slots, LANES), 0)
    row_owner = over(row, cap)
    spread = (row_owner == iota((slots, LANES), 1)).astype(BF16)
    row_names = dot(spread, names.astype(BF16))
    row_nth = dot(spread, nth.astype(BF16))
    row_slot = (row - cap * row_owner).astype(F32)[:, :tok]
    by_token = ((row_names > 0) & (row_nth == row_slot)).astype(BF16)
    lane = iota((tok, pairs), 1)
    first = topk * iota((tok, pairs), 0)
    widen = ((lane >= first) & (lane < first + topk)).astype(BF16)
    own_k = (iota((topk, pairs), 1) & (topk - 1)) == iota((topk, pairs), 0)
    pair_owner = dot(owner.astype(F32).astype(BF16), widen)
    pair_owner = jnp.sum(jnp.where(own_k, pair_owner, 0.0), axis=0, keepdims=True)
    pair_combine = lax.dot_general(
        combine_ref[...],
        widen.astype(F32),
        (((1,), (0,)), ((), ())),
        precision=lax.Precision.HIGHEST,
        preferred_element_type=F32,
    )
    pair_combine = jnp.sum(jnp.where(own_k, pair_combine, 0.0), axis=0, keepdims=True)
    placing = jnp.where(row_owner.astype(F32) == pair_owner, dot(by_token, widen), 0.0)
    scale = jnp.sum(placing * pair_combine, axis=1, keepdims=True)
    send_ref[:, :ffw] = (dot(placing.astype(BF16), hidden_ref[...]) * scale).astype(BF16)
    piece = grad_ref.shape[1] // pieces
    for c in range(CORES):
        send_ref[:, ffw + c * DIRECT : ffw + (c + 1) * DIRECT] = dot(
            by_token, grad_ref[:, c * piece : c * piece + DIRECT]
        ).astype(BF16)
    numbers = (names * (nth + 1.0)).astype(BF16)
    same = (iota((tok, tok), 0) == iota((tok, tok), 1)).astype(BF16)
    pack_ref[:, :LANES] = dot(same, numbers, (((1,), (1,)), ((), ()))).astype(BF16)
    at = LANES
    for c in range(CORES):
        for y in range(pieces // CORES):
            start = (y * CORES + c) * piece
            skip = DIRECT if y == 0 else 0
            pack_ref[:, at : at + piece - skip] = grad_ref[:, start + skip : start + piece]
            at += piece - skip


def pick_kernel(far, plane, cap, far_ref, gathered_ref, out_ref):
    tokens = gathered_ref.shape[0]
    tok = tokens // far
    slots = plane * far * cap
    chosen = (iota((plane, LANES), 1) == far * iota((plane, LANES), 0) + far_ref[0]).astype(BF16)
    numbers = dot(chosen, gathered_ref[:, :LANES], (((1,), (1,)), ((), ())))
    row = iota((slots, tokens), 0)
    group = over(row, cap)
    slot = row - cap * group
    row_far, row_plane = group & (far - 1), group >> (far.bit_length() - 1)
    spread = (row_plane[:, :plane] == iota((slots, plane), 1)).astype(BF16)
    numbers = dot(spread, numbers.astype(BF16))
    column_far = iota((slots, tokens), 1) >> (tok.bit_length() - 1)
    picking = jnp.where(
        (column_far == row_far) & (numbers == (slot + 1).astype(F32)), 1.0, 0.0
    ).astype(BF16)
    step = 3 * LANES
    for at in range(0, out_ref.shape[1], step):
        out_ref[:, at : at + step] = dot(
            picking, gathered_ref[:, LANES + at : LANES + at + step]
        ).astype(BF16)


def local(out_grad, hidden, combine, expert_ids, down_weight):
    tok, width = out_grad.shape
    topk = expert_ids.shape[1]
    ffw = hidden.shape[2]
    xs, ys = lax.axis_size("x"), lax.axis_size("y")
    far, near = lax.axis_size("far"), lax.axis_size("near")
    core, far_here = lax.axis_index("core"), lax.axis_index("far")
    owners = far * near * xs
    plane = near * xs
    cap = min(tok, 3 * tok * topk // (2 * owners))
    rows = tok * topk
    slots_here = owners * cap
    half = width // CORES
    piece = half // ys
    relayed = half - DIRECT
    wide = ffw + CORES * DIRECT
    params = pltpu.CompilerParams(vmem_limit_bytes=32 << 20)

    owner = expert_ids % plane * far + expert_ids // plane
    send, pack = pl.pallas_call(
        functools.partial(pack_kernel, owners, cap, ys * CORES),
        out_shape=(
            jax.ShapeDtypeStruct((slots_here, wide), BF16),
            jax.ShapeDtypeStruct((tok, LANES + CORES * relayed), BF16),
        ),
        compiler_params=params,
        name="pack",
    )(owner.T, combine.T, hidden.reshape(rows, ffw), out_grad)
    got = exchange(
        send.reshape(owners, cap * wide // LANES, LANES), ("near", "x", "far")
    ).reshape(slots_here, wide)
    gathered = lax.all_gather(pack, "far", axis=0, tiled=True)

    gathered, got = lax.optimization_barrier((gathered, got))
    relay_rows = pl.pallas_call(
        functools.partial(pick_kernel, far, plane, cap),
        out_shape=jax.ShapeDtypeStruct((slots_here, CORES * relayed), BF16),
        in_specs=[
            pl.BlockSpec(memory_space=pltpu.SMEM),
            pl.BlockSpec(memory_space=pltpu.VMEM),
        ],
        compiler_params=params,
        name="pick",
    )(far_here.astype(jnp.int32).reshape(1), gathered)
    got_relay = exchange(
        relay_rows.reshape(plane, far * cap, CORES * relayed), ("near", "x")
    ).reshape(slots_here, CORES * relayed)

    swap = [(0, 1), (1, 0)]
    acts = got[:, :ffw]
    both_acts = jnp.concatenate([acts, lax.ppermute(acts, "core", swap)], axis=0)
    weight = down_weight[0].reshape(ys, CORES, piece, ffw).transpose(1, 0, 2, 3)
    weight = weight.reshape(CORES, half, ffw)
    got_relay, both_acts, weight = lax.optimization_barrier((got_relay, both_acts, weight))

    halves = [
        jnp.concatenate(
            [
                got[:, ffw + c * DIRECT : ffw + (c + 1) * DIRECT],
                got_relay[:, c * relayed : (c + 1) * relayed],
            ],
            axis=1,
        )
        for c in range(CORES)
    ]
    mine = jnp.where(core == 0, halves[0], halves[1])
    theirs = jnp.where(core == 0, halves[1], halves[0])

    both_grads = jnp.concatenate([mine, lax.ppermute(theirs, "core", swap)], axis=0)
    partial_value = dot(both_grads, both_acts, ROWS).astype(BF16)
    grad_down = lax.psum_scatter(partial_value, "y", scatter_dimension=0, tiled=True)

    projected = sum(dot(halves[c], weight[c]) for c in range(CORES)).astype(BF16)
    returned = exchange(
        projected.reshape(owners, 2, cap * ffw // 2), ("near", "x", "far")
    ).reshape(slots_here, ffw)
    slots = owner.reshape(rows)
    onehot = (slots[:, None] == jnp.arange(owners, dtype=jnp.int32)[None, :]).astype(jnp.int32)
    before = jnp.cumsum(onehot, axis=0) - onehot
    slots = slots * cap + jnp.sum(onehot * before, axis=1)
    placing = slots[None, :] == jnp.arange(slots_here, dtype=jnp.int32)[:, None]
    back = dot(placing.astype(BF16), returned, ROWS).reshape(tok, topk, ffw)
    grad_hidden = (combine[:, :, None] * back).astype(BF16)
    grad_weights = jnp.sum(hidden.astype(F32) * back, axis=2)
    return (grad_hidden, grad_weights, grad_down[None])


def solution(mesh):
    dp, expert = mesh.shape["dp"], mesh.shape["expert"]
    shape = (dp // CORES, CORES, expert // (XS * PAIR), PAIR, XS)
    fine = Mesh(mesh.devices.reshape(shape), ("y", "core", "far", "near", "x"))
    tokens = ("y", "core", "far", "near", "x")
    owner = ("far", "near", "x")
    placed = (
        P(tokens, None),
        P(tokens, None, None),
        P(tokens, None),
        P(tokens, None),
        P(owner, None, None),
    )
    return jax.shard_map(
        local,
        mesh=fine,
        in_specs=placed,
        out_specs=(
            P(tokens, None, None),
            P(tokens, None),
            P(owner, ("y", "core"), None),
        ),
        check_vma=False,
    )
```

time: 175 us -> 173 us (0.989)
  blocking collectives: 79 us -> 50 us
  waiting for transfers between devices: 19.4 us -> 38.7 us
  starting transfers between devices: 33 us -> 41.1 us
  matrix products: 13 us -> 9.95 us
  Pallas kernels: 0 us -> 2.55 us
    all_to_all x1 -> x0, blocking collectives: 29.2 us -> none  [exchange(): return lax.all_to_all(value, axes, split_axis=0, concat_axis=0, tiled=True)]
    all_to_all x2 -> x3, waiting for transfers between devices: 6.37 us -> 26.8 us  [exchange(): return lax.all_to_all(value, axes, split_axis=0, concat_axis=0, tiled=True)]
    all_to_all x2 -> x3, starting transfers between devices: 29.1 us -> 37.3 us  [exchange(): return lax.all_to_all(value, axes, split_axis=0, concat_axis=0, tiled=True)]
    dot_general x7 -> x4, matrix products: 13 us -> 9.95 us  [dot(): return lax.dot_general(a, b, dims, preferred_element_type=F32)]
    pallas_call x0 -> x2, Pallas kernels: none -> 2.55 us  [the longest x1 1.91 us: local(): pl.pallas_call(functools.partial(pick_kernel, far, plane, cap), out_shape...]
    unnamed x17 -> x22, local copies, waits for them, and re-layouts: 3.83 us -> 4.75 us
  transfers between devices with their start and end apart: 5 -> 6, of which waited for: 3 -> 4; matrix products, arithmetic and copies ran while one was open for 9% -> 9% of each run, Pallas kernels for 0% -> 0%
where the time goes in v5:
time: 173 us; the launch traced here: 172 us
  blocking collectives  50 us (29%)
  starting transfers between devices  41.1 us (24%)
  waiting for transfers between devices  38.7 us (22%)
  between operations  14.2 us (8%)
  local copies, waits for them, and re-layouts  14.1 us (8%)
  matrix products  9.95 us (6%)
  Pallas kernels  2.55 us (1%)
    all_gather x1, blocking collectives, local(): gathered = lax.all_gather(pack, 'far', axis=0, tiled=True)  50 us
    all_to_all x3, starting transfers between devices, exchange(): return lax.all_to_all(value, axes, split_axis=0, concat_axis=0, tiled=True)  37.3 us
    all_to_all x3, waiting for transfers between devices, exchange(): return lax.all_to_all(value, axes, split_axis=0, concat_axis=0, tiled=True)  26.8 us
    dot_general x4, matrix products, dot(): return lax.dot_general(a, b, dims, preferred_element_type=F32)  9.95 us
    reduce_scatter x1, waiting for transfers between devices, local(): lax.psum_scatter(partial_value, 'y', scatter_dimension=0, tiled=True)  9.63 us
    transpose x1, local copies, waits for them, and re-layouts, local(): weight = down_weight[0].reshape(ys, CORES, piece, ffw).transpose(1, 0, 2, 3)  5.98 us
    unnamed x22, local copies, waits for them, and re-layouts  4.75 us
  transfers between devices with their start and end apart: 6, of which 4 were waited for; matrix products, arithmetic and copies ran while one was open for 9% of the time, Pallas kernels for 0%

profile of v5, /device:TPU:6, one launch (start us, length us, event | category | flops | bytes accessed | tf_op | source)
XLA Modules:
  0.0 171.9 jit_solution(9942259709209034140)
XLA Ops:
  7.2 0.7 fusion.33.owner_ref
  7.9 0.9 copy-done
  8.8 0.9 copy-done.2
  9.7 0.7 copy-done.3
  10.4 0.6 pack.1
  11.0 0.9 reshape.67
  11.9 22.3 %all-to-all-start = ((bf16[64,24,128]{2,1,0:T(8,128)(2,1)}), bf16[64,24,128]{2,1,0:T(8,128)(2,1)S(1)}, u32[]{:S(2)}, u32[]{:S(2)}) async-start(bf16[64,24,128]{2,1,0:T(8,128)(2,1)} %reshape.67), calls=%async_computation | async-start | bytes 786432 | tf_op jit(solution)/shard_map/all_to_all | solution.py:26
  34.3 50.0 %all_gather.3.gathered_ref = bf16[128,3968]{1,0:T(8,128)(2,1)S(1)} all-gather(bf16[16,3968]{1,0:T(8,128)(2,1)S(1)} %get-tuple-element.10), channel_id=1, replica_groups=mesh['y'=8,'core'=2,'far'=8,'near'=2,'x'=4] {'far'}, dimensions={0}, use_global_device_ids=true | all-gather | bytes 1142784 | tf_op jit(solution)/shard_map/all_gather | solution.py:141
  84.2 0.0 all-to-all-done
  84.2 0.2 reshape.68
  84.4 1.9 %pick.1 = bf16[192,3840]{1,0:T(8,128)(2,1)} custom-call(s32[1]{0:T(128)} %bitcast.4.far_ref, bf16[128,3968]{1,0:T(8,128)(2,1)S(1)} %all_gather.3.gathered_ref), custom_call_target="tpu_custom_call" | custom-call | tf_op jit(solution)/shard_map/pick/pallas_call | solution.py:144
  86.3 6.9 %all-to-all-start.1 = ((bf16[8,24,3840]{2,1,0:T(8,128)(2,1)}), bf16[8,24,3840]{2,1,0:T(8,128)(2,1)S(1)}, u32[]{:S(2)}, u32[]{:S(2)}) async-start(bf16[8,24,3840]{2,1,0:T(8,128)(2,1)} %bitcast.5), calls=%async_computation.1 | async-start | bytes 2949120 | tf_op jit(solution)/shard_map/all_to_all | solution.py:26
  93.2 1.9 %collective-permute-start = (bf16[192,768]{1,0:T(8,128)(2,1)S(1)}, bf16[192,768]{1,0:T(8,128)(2,1)S(1)}, u32[]{:S(2)}, u32[]{:S(2)}) collective-permute-start(bf16[192,768]{1,0:T(8,128)(2,1)S(1)} %slice.22), channel_id=1, source_target_pairs={{0,64},{64,0},{1,65},{65,1},{2,66},{66,2},{3,67},{67,3},{4,68},{68... | collective-permute-start | bytes 884744 | tf_op jit(solution)/shard_map/ppermute | solution.py:160
  95.1 6.0 %copy.25 = bf16[2,8,256,768]{3,2,1,0:T(8,128)(2,1)} copy(bf16[2,8,256,768]{3,2,0,1:T(8,128)(2,1)} %bitcast.31) | data formatting | bytes 12582912 | tf_op jit(solution)/shard_map/transpose | solution.py:161
  101.1 0.6 fusion.30
  101.7 0.0 collective-permute-done
  101.8 6.4 %all-to-all-done.1 = bf16[8,24,3840]{2,1,0:T(8,128)(2,1)S(1)} async-done(((bf16[8,24,3840]{2,1,0:T(8,128)(2,1)}), bf16[8,24,3840]{2,1,0:T(8,128)(2,1)S(1)}, u32[]{:S(2)}, u32[]{:S(2)}) %all-to-all-start.1) | async-done | bytes 1474592 | tf_op jit(solution)/shard_map/all_to_all | solution.py:26
  108.2 0.1 fusion.29
  108.3 0.7 copy-done.5
  109.0 0.0 copy-done.7
  109.0 0.3 broadcast_select_fusion.1
  109.3 1.9 %collective-permute-start.1 = (bf16[192,2048]{1,0:T(8,128)(2,1)S(1)}, bf16[192,2048]{1,0:T(8,128)(2,1)S(1)}, u32[]{:S(2)}, u32[]{:S(2)}) collective-permute-start(bf16[192,2048]{1,0:T(8,128)(2,1)S(1)} %get-tuple-element.21), channel_id=1, source_target_pairs={{0,64},{64,0},{1,65},{65,1},{2,66},{66,2},{3,67},{67,3},{4,68},{68... | collective-permute-start | bytes 2359304 | tf_op jit(solution)/shard_map/ppermute | solution.py:178
  111.2 2.3 %collective-permute-done.1 = bf16[192,2048]{1,0:T(8,128)(2,1)S(1)} collective-permute-done((bf16[192,2048]{1,0:T(8,128)(2,1)S(1)}, bf16[192,2048]{1,0:T(8,128)(2,1)S(1)}, u32[]{:S(2)}, u32[]{:S(2)}) %collective-permute-start.1) | collective-permute-done | bytes 786464 | tf_op jit(solution)/shard_map/ppermute | solution.py:178
  113.4 3.6 %convolution_convert_fusion = bf16[2048,768]{1,0:T(8,128)(2,1)} fusion(bf16[384,768]{1,0:T(8,128)(2,1)S(1)} %pad_maximum_fusion.2, bf16[192,2048]{1,0:T(8,128)(2,1)S(1)} %collective-permute-done.1, bf16[192,2048]{1,0:T(8,128)(2,1)S(1)} %get-tuple-element.20), kind=kOutput, calls=%fused_computation | convolution fusion | flops 1212678144 | bytes 5308416 | tf_op jit(solution)/shard_map/dot_general | solution.py:22
  117.0 0.0 reduce-scatter.2.cloned.1.call-update
  117.0 0.8 copy-done.8
  117.8 2.7 %fusion = f32[192,768]{1,0:T(8,128)S(1)} fusion(bf16[2,2048,768]{2,1,0:T(8,128)(2,1)} %bitcast.32, bf16[192,1920]{1,0:T(8,128)(2,1)S(1)} %get-tuple-element.23, bf16[192,128]{1,0:T(8,128)(2,1)S(1)} %copy-done.8), kind=kOutput, calls=%fused_computation.1 | convolution fusion | flops 605552640 | bytes 4521984 | tf_op jit(solution)/shard_map/dot_general | solution.py:22
  120.5 0.0 copy-start.4
  120.5 0.0 copy-start.9
  120.5 2.7 %fusion.12 = bf16[192,768]{1,0:T(8,128)(2,1)S(1)} fusion(f32[192,768]{1,0:T(8,128)S(1)} %fusion, bf16[2,2048,768]{2,1,0:T(8,128)(2,1)} %bitcast.33, bf16[192,1920]{1,0:T(8,128)(2,1)S(1)} %get-tuple-element.22, bf16[192,128]{1,0:T(8,128)(2,1)S(1)} %copy-done.6), kind=kOutput, calls=%fused_computation.11 | convolution fusion | flops 605847552 | bytes 4816896 | tf_op jit(solution)/shard_map/dot_general | solution.py:22
  123.2 0.0 copy-start.1
  123.2 0.9 reshape.73
  124.1 8.1 %all-to-all-start.2 = ((bf16[64,2,1152]{2,1,0:T(2,128)(2,1)}), bf16[64,2,1152]{2,1,0:T(2,128)(2,1)S(1)}, u32[]{:S(2)}, u32[]{:S(2)}) async-start(bf16[64,2,1152]{2,1,0:T(2,128)(2,1)} %reshape.73), calls=%async_computation.2 | async-start | bytes 589824 | tf_op jit(solution)/shard_map/all_to_all | solution.py:26
  132.3 0.1 copy.21
  132.3 0.0 copy-done.9
  132.3 0.1 copy.22
  132.4 0.1 reshape.65
  132.5 0.1 fusion.19
  132.6 0.2 reduce_window_sum.11
  132.8 0.2 select_reduce_fusion
  133.0 0.1 reduce_sum.21
  133.0 0.1 copy.23
  133.1 0.1 copy.24
  133.2 20.4 %all-to-all-done.2 = bf16[64,2,1152]{2,1,0:T(2,128)(2,1)S(1)} async-done(((bf16[64,2,1152]{2,1,0:T(2,128)(2,1)}), bf16[64,2,1152]{2,1,0:T(2,128)(2,1)S(1)}, u32[]{:S(2)}, u32[]{:S(2)}) %all-to-all-start.2) | async-done | bytes 294944 | tf_op jit(solution)/shard_map/all_to_all | solution.py:26
  153.6 0.2 reshape.75
  153.8 1.0 multiply_reduce_fusion
  154.8 0.7 copy.26
  155.5 9.6 %reduce-scatter.2.cloned.1.call-done = bf16[256,768]{1,0:T(8,128)(2,1)} async-done(((bf16[2048,768]{1,0:T(8,128)(2,1)}), bf16[256,768]{1,0:T(8,128)(2,1)}) %reduce-scatter.2.cloned.1.call-update) | async-done | bytes 393232 | tf_op jit(solution)/shard_map/reduce_scatter | solution.py:180
  (15 shorter events, 0.1 us)
Async XLA Ops:
  7.9 0.9 copy-start
  8.8 0.9 copy-start.2
  9.7 0.7 copy-start.3
  11.9 72.3 %all-to-all-start = ((bf16[64,24,128]{2,1,0:T(8,128)(2,1)}), bf16[64,24,128]{2,1,0:T(8,128)(2,1)S(1)}, u32[]{:S(2)}, u32[]{:S(2)}) async-start(bf16[64,24,128]{2,1,0:T(8,128)(2,1)} %reshape.67), calls=%async_computation | async-start | bytes 786432 | tf_op jit(solution)/shard_map/all_to_all | solution.py:26
  86.3 21.9 %all-to-all-start.1 = ((bf16[8,24,3840]{2,1,0:T(8,128)(2,1)}), bf16[8,24,3840]{2,1,0:T(8,128)(2,1)S(1)}, u32[]{:S(2)}, u32[]{:S(2)}) async-start(bf16[8,24,3840]{2,1,0:T(8,128)(2,1)} %bitcast.5), calls=%async_computation.1 | async-start | bytes 2949120 | tf_op jit(solution)/shard_map/all_to_all | solution.py:26
  93.2 71.9 %reduce-scatter.2.cloned.1.call-start = ((), (), s32[]{:S(2)}) async-start(), calls=%async_computation.4 | async-start | bytes 3538944 | tf_op jit(solution)/shard_map/reduce_scatter | solution.py:180
  93.2 8.6 %collective-permute-start = (bf16[192,768]{1,0:T(8,128)(2,1)S(1)}, bf16[192,768]{1,0:T(8,128)(2,1)S(1)}, u32[]{:S(2)}, u32[]{:S(2)}) collective-permute-start(bf16[192,768]{1,0:T(8,128)(2,1)S(1)} %slice.22), channel_id=1, source_target_pairs={{0,64},{64,0},{1,65},{65,1},{2,66},{66,2},{3,67},{67,3},{4,68},{68... | collective-permute-start | bytes 884744 | tf_op jit(solution)/shard_map/ppermute | solution.py:160
  108.2 0.8 copy-start.5
  108.2 0.8 copy-start.7
  109.3 4.2 %collective-permute-start.1 = (bf16[192,2048]{1,0:T(8,128)(2,1)S(1)}, bf16[192,2048]{1,0:T(8,128)(2,1)S(1)}, u32[]{:S(2)}, u32[]{:S(2)}) collective-permute-start(bf16[192,2048]{1,0:T(8,128)(2,1)S(1)} %get-tuple-element.21), channel_id=1, source_target_pairs={{0,64},{64,0},{1,65},{65,1},{2,66},{66,2},{3,67},{67,3},{4,68},{68... | collective-permute-start | bytes 2359304 | tf_op jit(solution)/shard_map/ppermute | solution.py:178
  117.0 0.8 copy-start.8
  117.8 2.7 %copy-start.6 = (bf16[192,128]{1,0:T(8,128)(2,1)S(1)}, bf16[192,128]{1,0:T(8,128)(2,1)}, u32[]{:S(2)}) copy-start(bf16[192,128]{1,0:T(8,128)(2,1)} %get-tuple-element.26) | copy-start | bytes 147460
  120.5 11.7 %copy-start.4 = (f32[16,8]{0,1:T(8,128)S(1)}, f32[16,8]{0,1:T(8,128)}, u32[]{:S(2)}) copy-start(f32[16,8]{0,1:T(8,128)} %param.7) | copy-start | bytes 1540
  120.5 11.8 %copy-start.9 = (s32[16,8]{0,1:T(8,128)S(1)}, s32[16,8]{0,1:T(8,128)}, u32[]{:S(2)}) copy-start(s32[16,8]{0,1:T(8,128)} %param.8) | copy-start | bytes 1540
  123.2 30.5 %copy-start.1 = (bf16[16,8,768]{2,1,0:T(8,128)(2,1)S(1)}, bf16[16,8,768]{2,1,0:T(8,128)(2,1)}, u32[]{:S(2)}) copy-start(bf16[16,8,768]{2,1,0:T(8,128)(2,1)} %param.6) | copy-start | bytes 589828
  124.1 29.5 %all-to-all-start.2 = ((bf16[64,2,1152]{2,1,0:T(2,128)(2,1)}), bf16[64,2,1152]{2,1,0:T(2,128)(2,1)S(1)}, u32[]{:S(2)}, u32[]{:S(2)}) async-start(bf16[64,2,1152]{2,1,0:T(2,128)(2,1)} %reshape.73), calls=%async_computation.2 | async-start | bytes 589824 | tf_op jit(solution)/shard_map/all_to_all | solution.py:26
Sparse Core Ops, SparseCore 0:
  117.2 47.8 reduce-scatter.1

commit v6 on v5

--- a/solution.py
+++ b/solution.py
@@ -12,6 +12,7 @@
 XS = 4
 PAIR = 2
 DIRECT = 128
+PACK_LIMIT = 56 << 20
 LANES = 128
 F32 = jnp.float32
 BF16 = jnp.bfloat16
@@ -34,11 +35,23 @@
     return lax.broadcasted_iota(jnp.int32, shape, dim)
 
 
-def pack_kernel(owners, cap, pieces, owner_ref, combine_ref, hidden_ref, grad_ref, send_ref, pack_ref):
-    topk, tok = owner_ref.shape
+def pack_kernel(owners, cap, plane, pieces, *refs):
+    sources, (send_ref, pack_ref), inside = refs[:4], refs[4:6], refs[6:10]
+    tall_ref, sems = refs[10:]
+    copies = [
+        pltpu.make_async_copy(source, target, sems.at[i])
+        for i, (source, target) in enumerate(zip(sources, inside))
+    ]
+    for copy in copies:
+        copy.start()
+    for copy in copies:
+        copy.wait()
+    ids_ref, combine_ref, hidden_ref, grad_ref = inside
+    topk, tok = ids_ref.shape
     pairs, ffw = hidden_ref.shape
     slots = owners * cap
-    owner = owner_ref[...]
+    ids = ids_ref[...]
+    owner = (ids & (plane - 1)) * (owners // plane) + (ids >> (plane.bit_length() - 1))
     wide = iota((LANES, tok), 0)
     names = sum((wide == owner[k : k + 1, :]).astype(F32) for k in range(topk))
     earlier = (iota((tok, tok), 0) < iota((tok, tok), 1)).astype(BF16)
@@ -66,12 +79,15 @@
     pair_combine = jnp.sum(jnp.where(own_k, pair_combine, 0.0), axis=0, keepdims=True)
     placing = jnp.where(row_owner.astype(F32) == pair_owner, dot(by_token, widen), 0.0)
     scale = jnp.sum(placing * pair_combine, axis=1, keepdims=True)
-    send_ref[:, :ffw] = (dot(placing.astype(BF16), hidden_ref[...]) * scale).astype(BF16)
     piece = grad_ref.shape[1] // pieces
-    for c in range(CORES):
-        send_ref[:, ffw + c * DIRECT : ffw + (c + 1) * DIRECT] = dot(
-            by_token, grad_ref[:, c * piece : c * piece + DIRECT]
-        ).astype(BF16)
+    acts = dot(placing.astype(BF16), hidden_ref[...]) * scale
+    direct = [
+        dot(by_token, grad_ref[:, c * piece : c * piece + DIRECT]) for c in range(CORES)
+    ]
+    blocks = [acts[:, at : at + LANES] for at in range(0, ffw, LANES)] + direct
+    for i, block in enumerate(blocks):
+        tall_ref[pl.ds(i, slots, stride=len(blocks)), :] = block
+    send_ref[...] = tall_ref[...].astype(BF16)
     numbers = (names * (nth + 1.0)).astype(BF16)
     same = (iota((tok, tok), 0) == iota((tok, tok), 1)).astype(BF16)
     pack_ref[:, :LANES] = dot(same, numbers, (((1,), (1,)), ((), ()))).astype(BF16)
@@ -100,11 +116,13 @@
     picking = jnp.where(
         (column_far == row_far) & (numbers == (slot + 1).astype(F32)), 1.0, 0.0
     ).astype(BF16)
-    step = 3 * LANES
-    for at in range(0, out_ref.shape[1], step):
-        out_ref[:, at : at + step] = dot(
-            picking, gathered_ref[:, LANES + at : LANES + at + step]
-        ).astype(BF16)
+    columns, step = out_ref.shape[2], 3 * LANES
+    for c in range(CORES):
+        for at in range(0, columns, step):
+            start = LANES + c * columns + at
+            out_ref[c, :, at : at + step] = dot(
+                picking, gathered_ref[:, start : start + step]
+            ).astype(BF16)
 
 
 def local(out_grad, hidden, combine, expert_ids, down_weight):
@@ -125,16 +143,25 @@
     wide = ffw + CORES * DIRECT
     params = pltpu.CompilerParams(vmem_limit_bytes=32 << 20)
 
-    owner = expert_ids % plane * far + expert_ids // plane
+    tall = slots_here * wide // LANES
     send, pack = pl.pallas_call(
-        functools.partial(pack_kernel, owners, cap, ys * CORES),
+        functools.partial(pack_kernel, owners, cap, plane, ys * CORES),
         out_shape=(
-            jax.ShapeDtypeStruct((slots_here, wide), BF16),
+            jax.ShapeDtypeStruct((tall, LANES), BF16),
             jax.ShapeDtypeStruct((tok, LANES + CORES * relayed), BF16),
         ),
-        compiler_params=params,
+        in_specs=[pl.BlockSpec(memory_space=pl.ANY)] * 4,
+        scratch_shapes=[
+            pltpu.VMEM((topk, tok), jnp.int32),
+            pltpu.VMEM((topk, tok), F32),
+            pltpu.VMEM((rows, ffw), BF16),
+            pltpu.VMEM((tok, width), BF16),
+            pltpu.VMEM((tall, LANES), F32),
+            pltpu.SemaphoreType.DMA((4,)),
+        ],
+        compiler_params=pltpu.CompilerParams(vmem_limit_bytes=PACK_LIMIT),
         name="pack",
-    )(owner.T, combine.T, hidden.reshape(rows, ffw), out_grad)
+    )(expert_ids.T, combine.T, hidden.reshape(rows, ffw), out_grad)
     got = exchange(
         send.reshape(owners, cap * wide // LANES, LANES), ("near", "x", "far")
     ).reshape(slots_here, wide)
@@ -143,7 +170,7 @@
     gathered, got = lax.optimization_barrier((gathered, got))
     relay_rows = pl.pallas_call(
         functools.partial(pick_kernel, far, plane, cap),
-        out_shape=jax.ShapeDtypeStruct((slots_here, CORES * relayed), BF16),
+        out_shape=jax.ShapeDtypeStruct((CORES, slots_here, relayed), BF16),
         in_specs=[
             pl.BlockSpec(memory_space=pltpu.SMEM),
             pl.BlockSpec(memory_space=pltpu.VMEM),
@@ -151,39 +178,35 @@
         compiler_params=params,
         name="pick",
     )(far_here.astype(jnp.int32).reshape(1), gathered)
-    got_relay = exchange(
-        relay_rows.reshape(plane, far * cap, CORES * relayed), ("near", "x")
-    ).reshape(slots_here, CORES * relayed)
+    relay = exchange(
+        relay_rows.reshape(CORES * plane, far * cap, relayed), ("core", "near", "x")
+    ).reshape(CORES * slots_here, relayed)
 
     swap = [(0, 1), (1, 0)]
-    acts = got[:, :ffw]
-    both_acts = jnp.concatenate([acts, lax.ppermute(acts, "core", swap)], axis=0)
-    weight = down_weight[0].reshape(ys, CORES, piece, ffw).transpose(1, 0, 2, 3)
-    weight = weight.reshape(CORES, half, ffw)
-    got_relay, both_acts, weight = lax.optimization_barrier((got_relay, both_acts, weight))
-
-    halves = [
-        jnp.concatenate(
-            [
-                got[:, ffw + c * DIRECT : ffw + (c + 1) * DIRECT],
-                got_relay[:, c * relayed : (c + 1) * relayed],
-            ],
-            axis=1,
-        )
-        for c in range(CORES)
-    ]
-    mine = jnp.where(core == 0, halves[0], halves[1])
-    theirs = jnp.where(core == 0, halves[1], halves[0])
-
-    both_grads = jnp.concatenate([mine, lax.ppermute(theirs, "core", swap)], axis=0)
-    partial_value = dot(both_grads, both_acts, ROWS).astype(BF16)
+    acts, sides = got[:, :ffw], (got[:, ffw : ffw + DIRECT], got[:, ffw + DIRECT :])
+    own, out = [jnp.where(core == 0, sides[c], sides[1 - c]) for c in range(CORES)]
+    own = jnp.concatenate([acts, own], axis=1)
+    other = lax.ppermute(jnp.concatenate([acts, out], axis=1), "core", swap)
+    both = jnp.concatenate(
+        [jnp.where(core == 0, own, other), jnp.where(core == 0, other, own)], axis=0
+    )
+    weight = lax.dynamic_index_in_dim(
+        down_weight[0].reshape(ys, CORES, piece, ffw), core, 1, keepdims=False
+    ).reshape(half, ffw)
+    relay, both, weight = lax.optimization_barrier((relay, both, weight))
+
+    grads = jnp.concatenate([both[:, ffw:], relay], axis=1)
+    partial_value = dot(grads, both[:, :ffw], ROWS).astype(BF16)
     grad_down = lax.psum_scatter(partial_value, "y", scatter_dimension=0, tiled=True)
 
-    projected = sum(dot(halves[c], weight[c]) for c in range(CORES)).astype(BF16)
+    halves = dot(grads, weight).reshape(CORES, slots_here, ffw)
+    mine = lax.dynamic_index_in_dim(halves, core, 0, keepdims=False)
+    theirs = lax.dynamic_index_in_dim(halves, 1 - core, 0, keepdims=False).astype(BF16)
+    projected = (mine + lax.ppermute(theirs, "core", swap).astype(F32)).astype(BF16)
     returned = exchange(
         projected.reshape(owners, 2, cap * ffw // 2), ("near", "x", "far")
     ).reshape(slots_here, ffw)
-    slots = owner.reshape(rows)
+    slots = (expert_ids % plane * far + expert_ids // plane).reshape(rows)
     onehot = (slots[:, None] == jnp.arange(owners, dtype=jnp.int32)[None, :]).astype(jnp.int32)
     before = jnp.cumsum(onehot, axis=0) - onehot
     slots = slots * cap + jnp.sum(onehot * before, axis=1)

time: 173 us -> 172 us (level)
  local copies, waits for them, and re-layouts: 14.1 us -> 5.32 us
  waiting for transfers between devices: 38.7 us -> 43.8 us
  Pallas kernels: 2.55 us -> 4.48 us
  other arithmetic: 1.46 us -> 3.34 us
    all_to_all x3, waiting for transfers between devices: 26.8 us -> 33.1 us  [exchange(): return lax.all_to_all(value, axes, split_axis=0, concat_axis=0, tiled=True)]
    transpose x1 -> x0, local copies, waits for them, and re-layouts: 5.98 us -> none  [local(): weight = down_weight[0].reshape(ys, CORES, piece, ffw).transpose(1, 0, 2, 3)]
    unnamed x22 -> x9, local copies, waits for them, and re-layouts: 4.75 us -> 0.82 us
    dynamic_slice x0 -> x1, local copies, waits for them, and re-layouts: none -> 2.1 us  [local(): lax.dynamic_index_in_dim(down_weight[0].reshape(ys, CORES, piece, ffw), c...]
    pallas_call x1, Pallas kernels: 0.64 us -> 2.55 us  [local(): pl.pallas_call(functools.partial(pack_kernel, owners, cap, plane, ys * CO...]
    dot_general x4 -> x3, matrix products: 9.95 us -> 8.77 us  [dot(): return lax.dot_general(a, b, dims, preferred_element_type=F32)]
  transfers between devices with their start and end apart: 6 -> 6, of which waited for: 4 -> 4; matrix products, arithmetic and copies ran while one was open for 9% -> 7% of each run, Pallas kernels for 0% -> 0%
where the time goes in v6:
time: 172 us
  blocking collectives  50.3 us (29%)
  waiting for transfers between devices  43.8 us (25%)
  starting transfers between devices  41.5 us (24%)
  between operations  14.2 us (8%)
  matrix products  8.77 us (5%)
  local copies, waits for them, and re-layouts  5.32 us (3%)
  Pallas kernels  4.48 us (3%)
  other arithmetic  3.34 us (2%)
    all_gather x1, blocking collectives, local(): gathered = lax.all_gather(pack, 'far', axis=0, tiled=True)  50.3 us
    all_to_all x3, starting transfers between devices, exchange(): return lax.all_to_all(value, axes, split_axis=0, concat_axis=0, tiled=True)  37.3 us
    all_to_all x3, waiting for transfers between devices, exchange(): return lax.all_to_all(value, axes, split_axis=0, concat_axis=0, tiled=True)  33.1 us
    reduce_scatter x1, waiting for transfers between devices, local(): lax.psum_scatter(partial_value, 'y', scatter_dimension=0, tiled=True)  9.19 us
    dot_general x3, matrix products, dot(): return lax.dot_general(a, b, dims, preferred_element_type=F32)  8.77 us
  transfers between devices with their start and end apart: 6, of which 4 were waited for; matrix products, arithmetic and copies ran while one was open for 7% of the time, Pallas kernels for 0%

profile of v6, /device:TPU:6, one launch (start us, length us, event | category | flops | bytes accessed | tf_op | source)
XLA Modules:
  0.0 171.7 jit_solution(13531583189977334397)
XLA Ops:
  7.2 2.5 %pack.1 = (bf16[1536,128]{1,0:T(8,128)(2,1)}, bf16[16,3968]{1,0:T(8,128)(2,1)}) custom-call(s32[8,16]{1,0:T(8,128)} %bitcast.31, f32[8,16]{1,0:T(8,128)} %bitcast.30, bf16[128,768]{1,0:T(8,128)(2,1)} %bitcast.29, bf16[16,4096]{1,0:T(8,128)(2,1)} %refs_3_.1), custom_call_target="tpu_custom_call" | custom-call | tf_op jit(solution)/shard_map/pack/pallas_call | solution.py:147
  9.7 22.3 %all-to-all-start = ((bf16[64,24,128]{2,1,0:T(8,128)(2,1)}), bf16[64,24,128]{2,1,0:T(8,128)(2,1)S(1)}, u32[]{:S(2)}, u32[]{:S(2)}) async-start(bf16[64,24,128]{2,1,0:T(8,128)(2,1)} %bitcast.28), calls=%async_computation | async-start | bytes 786432 | tf_op jit(solution)/shard_map/all_to_all | solution.py:27
  32.0 50.3 %all_gather.3.gathered_ref = bf16[128,3968]{1,0:T(8,128)(2,1)S(1)} all-gather(bf16[16,3968]{1,0:T(8,128)(2,1)} %get-tuple-element.10), channel_id=1, replica_groups=mesh['y'=8,'core'=2,'far'=8,'near'=2,'x'=4] {'far'}, dimensions={0}, use_global_device_ids=true | all-gather | bytes 1142784 | tf_op jit(solution)/shard_map/all_gather | solution.py:168
  82.4 0.0 all-to-all-done
  82.4 0.2 reshape.74
  82.5 1.9 %pick.1 = bf16[2,192,1920]{2,1,0:T(8,128)(2,1)} custom-call(s32[1]{0:T(128)} %bitcast.1.far_ref, bf16[128,3968]{1,0:T(8,128)(2,1)S(1)} %all_gather.3.gathered_ref), custom_call_target="tpu_custom_call" | custom-call | tf_op jit(solution)/shard_map/pick/pallas_call | solution.py:171
  84.5 6.5 %all-to-all-start.1 = ((bf16[16,24,1920]{2,1,0:T(8,128)(2,1)}), bf16[16,24,1920]{2,1,0:T(8,128)(2,1)}, u32[]{:S(2)}, u32[]{:S(2)}) async-start(bf16[16,24,1920]{2,1,0:T(8,128)(2,1)} %bitcast.6), calls=%async_computation.1 | async-start | bytes 2949120 | tf_op jit(solution)/shard_map/all_to_all | solution.py:27
  91.0 0.0 reduce-scatter.2.cloned.1.call-start
  91.1 0.8 pad_maximum_fusion.5
  91.8 2.0 %collective-permute-start = (bf16[192,896]{1,0:T(8,128)(2,1)}, bf16[192,896]{1,0:T(8,128)(2,1)}, u32[]{:S(2)}, u32[]{:S(2)}) collective-permute-start(bf16[192,896]{1,0:T(8,128)(2,1)} %pad_maximum_fusion.5), channel_id=1, source_target_pairs={{0,64},{64,0},{1,65},{65,1},{2,66},{66,2},{3,67},{67,3},{4,68},{68... | collective-permute-start | bytes 1032200 | tf_op jit(solution)/shard_map/ppermute | solution.py:189
  93.9 2.1 %constant_dynamic-slice_fusion = bf16[8,1,256,768]{3,2,1,0:T(8,128)(2,1)S(1)} fusion(bf16[8,2,256,768]{3,2,1,0:T(8,128)(2,1)} %bitcast.25, s32[]{:T(128)S(6)} %select_n.53), kind=kLoop, calls=%fused_computation.37 | loop fusion | bytes 6291460 | tf_op jit(solution)/shard_map/jit(dynamic_index_in_dim)/dynamic_slice | solution.py:193
  96.0 0.0 collective-permute-done
  96.0 1.1 broadcast_select_fusion.1
  97.1 0.9 pad_maximum_fusion.3
  98.0 12.6 %all-to-all-done.1 = bf16[16,24,1920]{2,1,0:T(8,128)(2,1)} async-done(((bf16[16,24,1920]{2,1,0:T(8,128)(2,1)}), bf16[16,24,1920]{2,1,0:T(8,128)(2,1)}, u32[]{:S(2)}, u32[]{:S(2)}) %all-to-all-start.1) | async-done | bytes 1474592 | tf_op jit(solution)/shard_map/all_to_all | solution.py:27
  110.6 0.9 slice.18
  111.5 5.0 %convolution_convert_fusion = bf16[2048,768]{1,0:T(8,128)(2,1)} fusion(bf16[384,1920]{1,0:T(8,128)(2,1)} %bitcast.7, bf16[384,128]{1,0:T(8,128)(2,1)S(1)} %slice.18, bf16[384,896]{1,0:T(8,128)(2,1)} %pad_maximum_fusion.3), kind=kOutput, calls=%fused_computation | convolution fusion | flops 1212678144 | bytes 5308416 | tf_op jit(solution)/shard_map/dot_general | solution.py:23
  116.5 0.0 reduce-scatter.2.cloned.1.call-update
  116.5 2.8 %fusion = f32[384,768]{1,0:T(8,128)S(1)} fusion(bf16[2048,768]{1,0:T(8,128)(2,1)S(1)} %bitcast.24, bf16[384,1920]{1,0:T(8,128)(2,1)} %bitcast.7, bf16[384,128]{1,0:T(8,128)(2,1)S(1)} %slice.18), kind=kOutput, calls=%fused_computation.2 | convolution fusion | flops 1211105280 | bytes 5898240 | tf_op jit(solution)/shard_map/dot_general | solution.py:23
  119.3 0.0 copy-start.1
  119.3 0.0 copy-start.2
  119.4 0.0 copy-start
  119.4 2.1 %collective-permute-start.1 = (bf16[192,768]{1,0:T(8,128)(2,1)S(1)}, bf16[192,768]{1,0:T(8,128)(2,1)S(1)}, u32[]{:S(2)}, u32[]{:S(2)}) collective-permute-start(bf16[192,768]{1,0:T(8,128)(2,1)S(1)} %fusion.3), channel_id=1, source_target_pairs={{0,64},{64,0},{1,65},{65,1},{2,66},{66,2},{3,67},{67,3},{4,68},{68... | collective-permute-start | bytes 884744 | tf_op jit(solution)/shard_map/ppermute | solution.py:205
  121.4 1.5 collective-permute-done.1
  123.0 0.1 fusion.1
  123.0 0.9 reshape.79
  124.0 8.5 %all-to-all-start.2 = ((bf16[64,2,1152]{2,1,0:T(2,128)(2,1)}), bf16[64,2,1152]{2,1,0:T(2,128)(2,1)S(1)}, u32[]{:S(2)}, u32[]{:S(2)}) async-start(bf16[64,2,1152]{2,1,0:T(2,128)(2,1)} %reshape.79), calls=%async_computation.2 | async-start | bytes 589824 | tf_op jit(solution)/shard_map/all_to_all | solution.py:27
  132.5 0.0 copy-done.1
  132.5 0.1 copy.18
  132.6 0.0 copy-done.2
  132.6 0.1 copy.19
  132.7 0.1 reshape.70
  132.8 0.1 fusion.8
  132.9 0.2 reduce_window_sum.11
  133.0 0.2 select_reduce_fusion
  133.2 0.1 reduce_sum.21
  133.3 20.5 %all-to-all-done.2 = bf16[64,2,1152]{2,1,0:T(2,128)(2,1)S(1)} async-done(((bf16[64,2,1152]{2,1,0:T(2,128)(2,1)}), bf16[64,2,1152]{2,1,0:T(2,128)(2,1)S(1)}, u32[]{:S(2)}, u32[]{:S(2)}) %all-to-all-start.2) | async-done | bytes 294944 | tf_op jit(solution)/shard_map/all_to_all | solution.py:27
  153.8 0.2 reshape.81
  154.0 0.0 copy-done
  154.0 1.0 multiply_reduce_fusion
  155.0 0.7 copy.23
  155.7 9.2 %reduce-scatter.2.cloned.1.call-done = bf16[256,768]{1,0:T(8,128)(2,1)} async-done(((bf16[2048,768]{1,0:T(8,128)(2,1)}), bf16[256,768]{1,0:T(8,128)(2,1)}) %reduce-scatter.2.cloned.1.call-update) | async-done | bytes 393232 | tf_op jit(solution)/shard_map/reduce_scatter | solution.py:200
  (5 shorter events, 0.1 us)
Async XLA Ops:
  9.7 72.7 %all-to-all-start = ((bf16[64,24,128]{2,1,0:T(8,128)(2,1)}), bf16[64,24,128]{2,1,0:T(8,128)(2,1)S(1)}, u32[]{:S(2)}, u32[]{:S(2)}) async-start(bf16[64,24,128]{2,1,0:T(8,128)(2,1)} %bitcast.28), calls=%async_computation | async-start | bytes 786432 | tf_op jit(solution)/shard_map/all_to_all | solution.py:27
  84.5 26.1 %all-to-all-start.1 = ((bf16[16,24,1920]{2,1,0:T(8,128)(2,1)}), bf16[16,24,1920]{2,1,0:T(8,128)(2,1)}, u32[]{:S(2)}, u32[]{:S(2)}) async-start(bf16[16,24,1920]{2,1,0:T(8,128)(2,1)} %bitcast.6), calls=%async_computation.1 | async-start | bytes 2949120 | tf_op jit(solution)/shard_map/all_to_all | solution.py:27
  91.0 73.9 %reduce-scatter.2.cloned.1.call-start = ((), (), s32[]{:S(2)}) async-start(), calls=%async_computation.4 | async-start | bytes 3538944 | tf_op jit(solution)/shard_map/reduce_scatter | solution.py:200
  91.8 4.2 %collective-permute-start = (bf16[192,896]{1,0:T(8,128)(2,1)}, bf16[192,896]{1,0:T(8,128)(2,1)}, u32[]{:S(2)}, u32[]{:S(2)}) collective-permute-start(bf16[192,896]{1,0:T(8,128)(2,1)} %pad_maximum_fusion.5), channel_id=1, source_target_pairs={{0,64},{64,0},{1,65},{65,1},{2,66},{66,2},{3,67},{67,3},{4,68},{68... | collective-permute-start | bytes 1032200 | tf_op jit(solution)/shard_map/ppermute | solution.py:189
  119.3 13.2 %copy-start.1 = (f32[16,8]{0,1:T(8,128)S(1)}, f32[16,8]{0,1:T(8,128)}, u32[]{:S(2)}) copy-start(f32[16,8]{0,1:T(8,128)} %param.7) | copy-start | bytes 1540
  119.3 13.3 %copy-start.2 = (s32[16,8]{0,1:T(8,128)S(1)}, s32[16,8]{0,1:T(8,128)}, u32[]{:S(2)}) copy-start(s32[16,8]{0,1:T(8,128)} %param.8) | copy-start | bytes 1540
  119.4 34.6 %copy-start = (bf16[16,8,768]{2,1,0:T(8,128)(2,1)S(1)}, bf16[16,8,768]{2,1,0:T(8,128)(2,1)}, u32[]{:S(2)}) copy-start(bf16[16,8,768]{2,1,0:T(8,128)(2,1)} %param.6) | copy-start | bytes 589828
  119.4 3.6 %collective-permute-start.1 = (bf16[192,768]{1,0:T(8,128)(2,1)S(1)}, bf16[192,768]{1,0:T(8,128)(2,1)S(1)}, u32[]{:S(2)}, u32[]{:S(2)}) collective-permute-start(bf16[192,768]{1,0:T(8,128)(2,1)S(1)} %fusion.3), channel_id=1, source_target_pairs={{0,64},{64,0},{1,65},{65,1},{2,66},{66,2},{3,67},{67,3},{4,68},{68... | collective-permute-start | bytes 884744 | tf_op jit(solution)/shard_map/ppermute | solution.py:205
  124.0 29.9 %all-to-all-start.2 = ((bf16[64,2,1152]{2,1,0:T(2,128)(2,1)}), bf16[64,2,1152]{2,1,0:T(2,128)(2,1)S(1)}, u32[]{:S(2)}, u32[]{:S(2)}) async-start(bf16[64,2,1152]{2,1,0:T(2,128)(2,1)} %reshape.79), calls=%async_computation.2 | async-start | bytes 589824 | tf_op jit(solution)/shard_map/all_to_all | solution.py:27
Sparse Core Ops, SparseCore 0:
  116.6 48.1 reduce-scatter.1

commit v7 on v6

--- a/solution.py
+++ b/solution.py
@@ -36,8 +36,8 @@
 
 
 def pack_kernel(owners, cap, plane, pieces, *refs):
-    sources, (send_ref, pack_ref), inside = refs[:4], refs[4:6], refs[6:10]
-    tall_ref, sems = refs[10:]
+    sources, (send_ref, pack_ref, direct_ref), inside = refs[:4], refs[4:7], refs[7:11]
+    sems = refs[11]
     copies = [
         pltpu.make_async_copy(source, target, sems.at[i])
         for i, (source, target) in enumerate(zip(sources, inside))
@@ -80,14 +80,9 @@
     placing = jnp.where(row_owner.astype(F32) == pair_owner, dot(by_token, widen), 0.0)
     scale = jnp.sum(placing * pair_combine, axis=1, keepdims=True)
     piece = grad_ref.shape[1] // pieces
-    acts = dot(placing.astype(BF16), hidden_ref[...]) * scale
-    direct = [
-        dot(by_token, grad_ref[:, c * piece : c * piece + DIRECT]) for c in range(CORES)
-    ]
-    blocks = [acts[:, at : at + LANES] for at in range(0, ffw, LANES)] + direct
-    for i, block in enumerate(blocks):
-        tall_ref[pl.ds(i, slots, stride=len(blocks)), :] = block
-    send_ref[...] = tall_ref[...].astype(BF16)
+    send_ref[...] = (dot(placing.astype(BF16), hidden_ref[...]) * scale).astype(BF16)
+    for c in range(CORES):
+        direct_ref[:, c * DIRECT : (c + 1) * DIRECT] = grad_ref[:, c * piece : c * piece + DIRECT]
     numbers = (names * (nth + 1.0)).astype(BF16)
     same = (iota((tok, tok), 0) == iota((tok, tok), 1)).astype(BF16)
     pack_ref[:, :LANES] = dot(same, numbers, (((1,), (1,)), ((), ()))).astype(BF16)
@@ -100,7 +95,7 @@
             at += piece - skip
 
 
-def pick_kernel(far, plane, cap, far_ref, gathered_ref, out_ref):
+def pick_kernel(far, plane, cap, far_ref, gathered_ref, direct_ref, out_ref):
     tokens = gathered_ref.shape[0]
     tok = tokens // far
     slots = plane * far * cap
@@ -116,11 +111,14 @@
     picking = jnp.where(
         (column_far == row_far) & (numbers == (slot + 1).astype(F32)), 1.0, 0.0
     ).astype(BF16)
-    columns, step = out_ref.shape[2], 3 * LANES
+    half, step = out_ref.shape[1] // CORES, 3 * LANES
     for c in range(CORES):
-        for at in range(0, columns, step):
-            start = LANES + c * columns + at
-            out_ref[c, :, at : at + step] = dot(
+        out_ref[:, c * half : c * half + DIRECT] = dot(
+            picking, direct_ref[:, c * DIRECT : (c + 1) * DIRECT]
+        ).astype(BF16)
+        for at in range(0, half - DIRECT, step):
+            start, to = LANES + c * (half - DIRECT) + at, c * half + DIRECT + at
+            out_ref[:, to : to + step] = dot(
                 picking, gathered_ref[:, start : start + step]
             ).astype(BF16)
 
@@ -140,15 +138,14 @@
     half = width // CORES
     piece = half // ys
     relayed = half - DIRECT
-    wide = ffw + CORES * DIRECT
     params = pltpu.CompilerParams(vmem_limit_bytes=32 << 20)
 
-    tall = slots_here * wide // LANES
-    send, pack = pl.pallas_call(
+    send, pack, direct = pl.pallas_call(
         functools.partial(pack_kernel, owners, cap, plane, ys * CORES),
         out_shape=(
-            jax.ShapeDtypeStruct((tall, LANES), BF16),
+            jax.ShapeDtypeStruct((slots_here, ffw), BF16),
             jax.ShapeDtypeStruct((tok, LANES + CORES * relayed), BF16),
+            jax.ShapeDtypeStruct((tok, CORES * DIRECT), BF16),
         ),
         in_specs=[pl.BlockSpec(memory_space=pl.ANY)] * 4,
         scratch_shapes=[
@@ -156,53 +153,48 @@
             pltpu.VMEM((topk, tok), F32),
             pltpu.VMEM((rows, ffw), BF16),
             pltpu.VMEM((tok, width), BF16),
-            pltpu.VMEM((tall, LANES), F32),
             pltpu.SemaphoreType.DMA((4,)),
         ],
         compiler_params=pltpu.CompilerParams(vmem_limit_bytes=PACK_LIMIT),
         name="pack",
     )(expert_ids.T, combine.T, hidden.reshape(rows, ffw), out_grad)
-    got = exchange(
-        send.reshape(owners, cap * wide // LANES, LANES), ("near", "x", "far")
-    ).reshape(slots_here, wide)
+    at_far = jnp.arange(far, dtype=jnp.int32)[:, None, None] == far_here
+    direct = lax.psum(jnp.where(at_far, direct[None], jnp.zeros((), BF16)), "far")
+    direct = direct.reshape(far * tok, CORES * DIRECT)
+    acts = exchange(
+        send.reshape(owners, 2, cap * ffw // 2), ("near", "x", "far")
+    ).reshape(slots_here, ffw)
     gathered = lax.all_gather(pack, "far", axis=0, tiled=True)
 
-    gathered, got = lax.optimization_barrier((gathered, got))
+    gathered, acts = lax.optimization_barrier((gathered, acts))
     relay_rows = pl.pallas_call(
         functools.partial(pick_kernel, far, plane, cap),
-        out_shape=jax.ShapeDtypeStruct((CORES, slots_here, relayed), BF16),
+        out_shape=jax.ShapeDtypeStruct((slots_here, width), BF16),
         in_specs=[
             pl.BlockSpec(memory_space=pltpu.SMEM),
+            pl.BlockSpec(memory_space=pltpu.VMEM),
             pl.BlockSpec(memory_space=pltpu.VMEM),
         ],
         compiler_params=params,
         name="pick",
-    )(far_here.astype(jnp.int32).reshape(1), gathered)
+    )(far_here.astype(jnp.int32).reshape(1), gathered, direct)
     relay = exchange(
-        relay_rows.reshape(CORES * plane, far * cap, relayed), ("core", "near", "x")
-    ).reshape(CORES * slots_here, relayed)
+        relay_rows.reshape(plane, far * cap, width), ("near", "x")
+    ).reshape(slots_here, width)
 
     swap = [(0, 1), (1, 0)]
-    acts, sides = got[:, :ffw], (got[:, ffw : ffw + DIRECT], got[:, ffw + DIRECT :])
-    own, out = [jnp.where(core == 0, sides[c], sides[1 - c]) for c in range(CORES)]
-    own = jnp.concatenate([acts, own], axis=1)
-    other = lax.ppermute(jnp.concatenate([acts, out], axis=1), "core", swap)
-    both = jnp.concatenate(
-        [jnp.where(core == 0, own, other), jnp.where(core == 0, other, own)], axis=0
-    )
-    weight = lax.dynamic_index_in_dim(
-        down_weight[0].reshape(ys, CORES, piece, ffw), core, 1, keepdims=False
-    ).reshape(half, ffw)
-    relay, both, weight = lax.optimization_barrier((relay, both, weight))
-
-    grads = jnp.concatenate([both[:, ffw:], relay], axis=1)
-    partial_value = dot(grads, both[:, :ffw], ROWS).astype(BF16)
+    both_acts = jnp.concatenate([acts, lax.ppermute(acts, "core", swap)], axis=0)
+    weight = down_weight[0].reshape(ys, CORES, piece, ffw).transpose(1, 0, 2, 3)
+    weight = weight.reshape(width, ffw)
+    relay, both_acts, weight = lax.optimization_barrier((relay, both_acts, weight))
+
+    sides = relay[:, :half], relay[:, half:]
+    mine, theirs = [jnp.where(core == 0, sides[c], sides[1 - c]) for c in range(CORES)]
+    both_grads = jnp.concatenate([mine, lax.ppermute(theirs, "core", swap)], axis=0)
+    partial_value = dot(both_grads, both_acts, ROWS).astype(BF16)
     grad_down = lax.psum_scatter(partial_value, "y", scatter_dimension=0, tiled=True)
 
-    halves = dot(grads, weight).reshape(CORES, slots_here, ffw)
-    mine = lax.dynamic_index_in_dim(halves, core, 0, keepdims=False)
-    theirs = lax.dynamic_index_in_dim(halves, 1 - core, 0, keepdims=False).astype(BF16)
-    projected = (mine + lax.ppermute(theirs, "core", swap).astype(F32)).astype(BF16)
+    projected = dot(relay, weight).astype(BF16)
     returned = exchange(
         projected.reshape(owners, 2, cap * ffw // 2), ("near", "x", "far")
     ).reshape(slots_here, ffw)

time: 172 us -> 226 us (1.31)
  waiting for transfers between devices: 43.8 us -> 99.2 us
  local copies, waits for them, and re-layouts: 5.32 us -> 10.9 us
  blocking collectives: 50.3 us -> 45.1 us
    psum x0 -> x1, waiting for transfers between devices: none -> 58.1 us  [local(): lax.psum(jnp.where(at_far, direct[None], jnp.zeros((), BF16)), 'far')]
    transpose x0 -> x1, local copies, waits for them, and re-layouts: none -> 6 us  [local(): weight = down_weight[0].reshape(ys, CORES, piece, ffw).transpose(1, 0, 2, 3)]
    all_to_all x3, waiting for transfers between devices: 33.1 us -> 27.4 us  [exchange(): return lax.all_to_all(value, axes, split_axis=0, concat_axis=0, tiled=True)]
    all_gather x1, blocking collectives: 50.3 us -> 45.1 us  [local(): gathered = lax.all_gather(pack, 'far', axis=0, tiled=True)]
  transfers between devices with their start and end apart: 6 -> 7, of which waited for: 4 -> 5; matrix products, arithmetic and copies ran while one was open for 7% -> 7% of each run, Pallas kernels for 0% -> 0%
where the time goes in v7:
time: 226 us
  waiting for transfers between devices  99.2 us (44%)
  blocking collectives  45.1 us (20%)
  starting transfers between devices  41.1 us (18%)
  between operations  14.2 us (6%)
  local copies, waits for them, and re-layouts  10.9 us (5%)
  matrix products  8.76 us (4%)
  Pallas kernels  4.41 us (2%)
    psum x1, waiting for transfers between devices, local(): lax.psum(jnp.where(at_far, direct[None], jnp.zeros((), BF16)), 'far')  58.1 us
    all_gather x1, blocking collectives, local(): gathered = lax.all_gather(pack, 'far', axis=0, tiled=True)  45.1 us
    all_to_all x3, starting transfers between devices, exchange(): return lax.all_to_all(value, axes, split_axis=0, concat_axis=0, tiled=True)  37.2 us
    all_to_all x3, waiting for transfers between devices, exchange(): return lax.all_to_all(value, axes, split_axis=0, concat_axis=0, tiled=True)  27.4 us
    reduce_scatter x1, waiting for transfers between devices, local(): lax.psum_scatter(partial_value, 'y', scatter_dimension=0, tiled=True)  11.4 us
    dot_general x3, matrix products, dot(): return lax.dot_general(a, b, dims, preferred_element_type=F32)  8.76 us
    transpose x1, local copies, waits for them, and re-layouts, local(): weight = down_weight[0].reshape(ys, CORES, piece, ffw).transpose(1, 0, 2, 3)  6 us
  transfers between devices with their start and end apart: 7, of which 5 were waited for; matrix products, arithmetic and copies ran while one was open for 7% of the time, Pallas kernels for 0%

profile of v7, /device:TPU:6, one launch (start us, length us, event | category | flops | bytes accessed | tf_op | source)
XLA Modules:
  0.0 225.7 jit_solution(6472130127565587610)
XLA Ops:
  7.2 2.4 %pack.1 = (bf16[192,768]{1,0:T(8,128)(2,1)}, bf16[16,3968]{1,0:T(8,128)(2,1)}, bf16[16,256]{1,0:T(8,128)(2,1)}) custom-call(s32[8,16]{1,0:T(8,128)} %bitcast.28, f32[8,16]{1,0:T(8,128)} %bitcast.27, bf16[128,768]{1,0:T(8,128)(2,1)} %bitcast.26, bf16[16,4096]{1,0:T(8,128)(2,1)} %refs_3_.1), custom_call_target="tpu_custom_call" | custom-call | tf_op jit(solution)/shard_map/pack/pallas_call | solution.py:143
  9.6 1.9 reshape.77
  11.5 22.3 %all-to-all-start = ((bf16[64,2,1152]{2,1,0:T(2,128)(2,1)}), bf16[64,2,1152]{2,1,0:T(2,128)(2,1)S(1)}, u32[]{:S(2)}, u32[]{:S(2)}) async-start(bf16[64,2,1152]{2,1,0:T(2,128)(2,1)} %reshape.77), calls=%async_computation | async-start | bytes 589824 | tf_op jit(solution)/shard_map/all_to_all | solution.py:27
  33.8 0.0 all-reduce.2.cloned.1.call-start
  33.8 1.4 broadcast_select_fusion.2
  35.2 0.0 all-reduce.2.cloned.1.call-update
  35.3 45.1 %all_gather.3.gathered_ref = bf16[128,3968]{1,0:T(8,128)(2,1)S(1)} all-gather(bf16[16,3968]{1,0:T(8,128)(2,1)} %get-tuple-element.11), channel_id=1, replica_groups=mesh['y'=8,'core'=2,'far'=8,'near'=2,'x'=4] {'far'}, dimensions={0}, use_global_device_ids=true | all-gather | bytes 1142784 | tf_op jit(solution)/shard_map/all_gather | solution.py:167
  80.4 0.0 all-to-all-done
  80.4 0.2 reshape.78
  80.6 58.1 %all-reduce.2.cloned.1.call-done.direct_ref = bf16[128,256]{1,0:T(8,128)(2,1)} async-done(((bf16[128,256]{1,0:T(8,128)(2,1)}), bf16[128,256]{1,0:T(8,128)(2,1)}) %all-reduce.2.cloned.1.call-update) | async-done | bytes 65552 | tf_op jit(solution)/shard_map/psum | solution.py:162
  138.7 0.0 copy-start
  138.7 0.8 copy-done
  139.6 2.0 pick.1
  141.6 5.0 %all-to-all-start.1 = ((bf16[8,24,4096]{2,1,0:T(8,128)(2,1)}), bf16[8,24,4096]{2,1,0:T(8,128)(2,1)S(1)}, u32[]{:S(2)}, u32[]{:S(2)}) async-start(bf16[8,24,4096]{2,1,0:T(8,128)(2,1)} %bitcast.6), calls=%async_computation.1 | async-start | bytes 3145728 | tf_op jit(solution)/shard_map/all_to_all | solution.py:27
  146.5 0.0 reduce-scatter.2.cloned.1.call-start
  146.5 1.9 collective-permute-start
  148.5 6.0 %copy.29 = bf16[2,8,256,768]{3,2,1,0:T(8,128)(2,1)} copy(bf16[2,8,256,768]{3,2,0,1:T(8,128)(2,1)} %bitcast.21) | data formatting | bytes 12582912 | tf_op jit(solution)/shard_map/transpose | solution.py:187
  154.5 0.0 collective-permute-done
  154.5 6.9 %all-to-all-done.1 = bf16[8,24,4096]{2,1,0:T(8,128)(2,1)S(1)} async-done(((bf16[8,24,4096]{2,1,0:T(8,128)(2,1)}), bf16[8,24,4096]{2,1,0:T(8,128)(2,1)S(1)}, u32[]{:S(2)}, u32[]{:S(2)}) %all-to-all-start.1) | async-done | bytes 1572896 | tf_op jit(solution)/shard_map/all_to_all | solution.py:27
  161.4 0.1 broadcast_select_fusion.1
  161.5 1.9 collective-permute-start.1
  163.5 2.3 collective-permute-done.1
  165.7 3.6 %convolution_convert_fusion = bf16[2048,768]{1,0:T(8,128)(2,1)} fusion(bf16[384,768]{1,0:T(8,128)(2,1)S(1)} %pad_maximum_fusion, bf16[192,2048]{1,0:T(8,128)(2,1)S(1)} %collective-permute-done.1, bf16[192,2048]{1,0:T(8,128)(2,1)S(1)} %get-tuple-element.22), kind=kOutput, calls=%fused_computation | convolution fusion | flops 1212678144 | bytes 5308416 | tf_op jit(solution)/shard_map/dot_general | solution.py:23
  169.3 0.0 reduce-scatter.2.cloned.1.call-update
  169.3 0.0 copy-start.2
  169.3 0.0 copy-start.3
  169.3 4.2 %convolution_convert_fusion.1 = bf16[192,768]{1,0:T(8,128)(2,1)S(1)} fusion(bf16[192,4096]{1,0:T(8,128)(2,1)S(1)} %bitcast.24, bf16[4096,768]{1,0:T(8,128)(2,1)} %bitcast.22), kind=kOutput, calls=%fused_computation.4 | convolution fusion | flops 1208107008 | bytes 8159232 | tf_op jit(solution)/shard_map/dot_general | solution.py:23
  173.5 0.0 copy-start.1
  173.5 0.9 reshape.83
  174.4 9.9 %all-to-all-start.2 = ((bf16[64,2,1152]{2,1,0:T(2,128)(2,1)}), bf16[64,2,1152]{2,1,0:T(2,128)(2,1)S(1)}, u32[]{:S(2)}, u32[]{:S(2)}) async-start(bf16[64,2,1152]{2,1,0:T(2,128)(2,1)} %reshape.83), calls=%async_computation.2 | async-start | bytes 589824 | tf_op jit(solution)/shard_map/all_to_all | solution.py:27
  184.3 0.0 copy-done.2
  184.3 0.1 copy.24
  184.4 0.0 copy-done.3
  184.4 0.1 copy.25
  184.5 0.1 reshape.74
  184.6 0.1 fusion.7
  184.7 0.2 reduce_window_sum.11
  184.9 0.2 select_reduce_fusion
  185.0 0.1 reduce_sum.21
  185.2 20.5 %all-to-all-done.2 = bf16[64,2,1152]{2,1,0:T(2,128)(2,1)S(1)} async-done(((bf16[64,2,1152]{2,1,0:T(2,128)(2,1)}), bf16[64,2,1152]{2,1,0:T(2,128)(2,1)S(1)}, u32[]{:S(2)}, u32[]{:S(2)}) %all-to-all-start.2) | async-done | bytes 294944 | tf_op jit(solution)/shard_map/all_to_all | solution.py:27
  205.6 0.2 reshape.85
  205.8 0.0 copy-done.1
  205.8 1.0 multiply_reduce_fusion
  206.9 0.7 copy.30
  207.5 11.4 %reduce-scatter.2.cloned.1.call-done = bf16[256,768]{1,0:T(8,128)(2,1)} async-done(((bf16[2048,768]{1,0:T(8,128)(2,1)}), bf16[256,768]{1,0:T(8,128)(2,1)}) %reduce-scatter.2.cloned.1.call-update) | async-done | bytes 393232 | tf_op jit(solution)/shard_map/reduce_scatter | solution.py:195
  (4 shorter events, 0.1 us)
Async XLA Ops:
  11.5 68.9 %all-to-all-start = ((bf16[64,2,1152]{2,1,0:T(2,128)(2,1)}), bf16[64,2,1152]{2,1,0:T(2,128)(2,1)S(1)}, u32[]{:S(2)}, u32[]{:S(2)}) async-start(bf16[64,2,1152]{2,1,0:T(2,128)(2,1)} %reshape.77), calls=%async_computation | async-start | bytes 589824 | tf_op jit(solution)/shard_map/all_to_all | solution.py:27
  33.8 105.0 %all-reduce.2.cloned.1.call-start = ((), (), s32[]{:S(2)}) async-start(), calls=%async_computation.4 | async-start | bytes 131072 | tf_op jit(solution)/shard_map/psum | solution.py:162
  138.7 0.8 copy-start
  141.6 19.9 %all-to-all-start.1 = ((bf16[8,24,4096]{2,1,0:T(8,128)(2,1)}), bf16[8,24,4096]{2,1,0:T(8,128)(2,1)S(1)}, u32[]{:S(2)}, u32[]{:S(2)}) async-start(bf16[8,24,4096]{2,1,0:T(8,128)(2,1)} %bitcast.6), calls=%async_computation.1 | async-start | bytes 3145728 | tf_op jit(solution)/shard_map/all_to_all | solution.py:27
  146.5 72.3 %reduce-scatter.2.cloned.1.call-start = ((), (), s32[]{:S(2)}) async-start(), calls=%async_computation.5 | async-start | bytes 3538944 | tf_op jit(solution)/shard_map/reduce_scatter | solution.py:195
  146.5 7.9 %collective-permute-start = (bf16[192,768]{1,0:T(8,128)(2,1)S(1)}, bf16[192,768]{1,0:T(8,128)(2,1)S(1)}, u32[]{:S(2)}, u32[]{:S(2)}) collective-permute-start(bf16[192,768]{1,0:T(8,128)(2,1)S(1)} %reshape.78), channel_id=1, source_target_pairs={{0,64},{64,0},{1,65},{65,1},{2,66},{66,2},{3,67},{67,3},{4,68},{68... | collective-permute-start | bytes 884744 | tf_op jit(solution)/shard_map/ppermute | solution.py:186
  161.5 4.2 %collective-permute-start.1 = (bf16[192,2048]{1,0:T(8,128)(2,1)S(1)}, bf16[192,2048]{1,0:T(8,128)(2,1)S(1)}, u32[]{:S(2)}, u32[]{:S(2)}) collective-permute-start(bf16[192,2048]{1,0:T(8,128)(2,1)S(1)} %get-tuple-element.23), channel_id=1, source_target_pairs={{0,64},{64,0},{1,65},{65,1},{2,66},{66,2},{3,67},{67,3},{4,68},{68... | collective-permute-start | bytes 2359304 | tf_op jit(solution)/shard_map/ppermute | solution.py:193
  169.3 15.0 %copy-start.2 = (f32[16,8]{0,1:T(8,128)S(1)}, f32[16,8]{0,1:T(8,128)}, u32[]{:S(2)}) copy-start(f32[16,8]{0,1:T(8,128)} %param.7) | copy-start | bytes 1540
  169.3 15.1 %copy-start.3 = (s32[16,8]{0,1:T(8,128)S(1)}, s32[16,8]{0,1:T(8,128)}, u32[]{:S(2)}) copy-start(s32[16,8]{0,1:T(8,128)} %param.8) | copy-start | bytes 1540
  173.5 32.3 %copy-start.1 = (bf16[16,8,768]{2,1,0:T(8,128)(2,1)S(1)}, bf16[16,8,768]{2,1,0:T(8,128)(2,1)}, u32[]{:S(2)}) copy-start(bf16[16,8,768]{2,1,0:T(8,128)(2,1)} %param.6) | copy-start | bytes 589828
  174.4 31.2 %all-to-all-start.2 = ((bf16[64,2,1152]{2,1,0:T(2,128)(2,1)}), bf16[64,2,1152]{2,1,0:T(2,128)(2,1)S(1)}, u32[]{:S(2)}, u32[]{:S(2)}) async-start(bf16[64,2,1152]{2,1,0:T(2,128)(2,1)} %reshape.83), calls=%async_computation.2 | async-start | bytes 589824 | tf_op jit(solution)/shard_map/all_to_all | solution.py:27
Sparse Core Ops, SparseCore 0:
  38.6 100.0 all-reduce.1
  169.4 49.4 reduce-scatter.1

commit v8 on v6

--- a/solution.py
+++ b/solution.py
@@ -116,13 +116,11 @@
     picking = jnp.where(
         (column_far == row_far) & (numbers == (slot + 1).astype(F32)), 1.0, 0.0
     ).astype(BF16)
-    columns, step = out_ref.shape[2], 3 * LANES
-    for c in range(CORES):
-        for at in range(0, columns, step):
-            start = LANES + c * columns + at
-            out_ref[c, :, at : at + step] = dot(
-                picking, gathered_ref[:, start : start + step]
-            ).astype(BF16)
+    step = 3 * LANES
+    for at in range(0, out_ref.shape[1], step):
+        out_ref[:, at : at + step] = dot(
+            picking, gathered_ref[:, LANES + at : LANES + at + step]
+        ).astype(BF16)
 
 
 def local(out_grad, hidden, combine, expert_ids, down_weight):
@@ -170,7 +168,7 @@
     gathered, got = lax.optimization_barrier((gathered, got))
     relay_rows = pl.pallas_call(
         functools.partial(pick_kernel, far, plane, cap),
-        out_shape=jax.ShapeDtypeStruct((CORES, slots_here, relayed), BF16),
+        out_shape=jax.ShapeDtypeStruct((slots_here, CORES * relayed), BF16),
         in_specs=[
             pl.BlockSpec(memory_space=pltpu.SMEM),
             pl.BlockSpec(memory_space=pltpu.VMEM),
@@ -179,30 +177,43 @@
         name="pick",
     )(far_here.astype(jnp.int32).reshape(1), gathered)
     relay = exchange(
-        relay_rows.reshape(CORES * plane, far * cap, relayed), ("core", "near", "x")
-    ).reshape(CORES * slots_here, relayed)
+        relay_rows.reshape(plane, far * cap, CORES * relayed), ("near", "x")
+    ).reshape(slots_here, CORES * relayed)
 
     swap = [(0, 1), (1, 0)]
-    acts, sides = got[:, :ffw], (got[:, ffw : ffw + DIRECT], got[:, ffw + DIRECT :])
-    own, out = [jnp.where(core == 0, sides[c], sides[1 - c]) for c in range(CORES)]
-    own = jnp.concatenate([acts, own], axis=1)
-    other = lax.ppermute(jnp.concatenate([acts, out], axis=1), "core", swap)
-    both = jnp.concatenate(
-        [jnp.where(core == 0, own, other), jnp.where(core == 0, other, own)], axis=0
-    )
-    weight = lax.dynamic_index_in_dim(
-        down_weight[0].reshape(ys, CORES, piece, ffw), core, 1, keepdims=False
-    ).reshape(half, ffw)
-    relay, both, weight = lax.optimization_barrier((relay, both, weight))
-
-    grads = jnp.concatenate([both[:, ffw:], relay], axis=1)
-    partial_value = dot(grads, both[:, :ffw], ROWS).astype(BF16)
-    grad_down = lax.psum_scatter(partial_value, "y", scatter_dimension=0, tiled=True)
-
-    halves = dot(grads, weight).reshape(CORES, slots_here, ffw)
-    mine = lax.dynamic_index_in_dim(halves, core, 0, keepdims=False)
-    theirs = lax.dynamic_index_in_dim(halves, 1 - core, 0, keepdims=False).astype(BF16)
-    projected = (mine + lax.ppermute(theirs, "core", swap).astype(F32)).astype(BF16)
+    acts = got[:, :ffw]
+    both_acts = jnp.concatenate([acts, lax.ppermute(acts, "core", swap)], axis=0)
+    weight = down_weight[0].reshape(ys, CORES, piece, ffw).transpose(1, 0, 2, 3)
+    weight = weight.reshape(width, ffw)
+    relay, both_acts, weight = lax.optimization_barrier((relay, both_acts, weight))
+
+    halves = [
+        jnp.concatenate(
+            [
+                got[:, ffw + c * DIRECT : ffw + (c + 1) * DIRECT],
+                relay[:, c * relayed : (c + 1) * relayed],
+            ],
+            axis=1,
+        )
+        for c in range(CORES)
+    ]
+    mine, theirs = [jnp.where(core == 0, halves[c], halves[1 - c]) for c in range(CORES)]
+    both_grads = jnp.concatenate([mine, lax.ppermute(theirs, "core", swap)], axis=0)
+    part = ffw // 2
+    grad_down = jnp.concatenate(
+        [
+            lax.psum_scatter(
+                dot(both_grads, both_acts[:, at : at + part], ROWS).astype(BF16),
+                "y",
+                scatter_dimension=0,
+                tiled=True,
+            )
+            for at in range(0, ffw, part)
+        ],
+        axis=1,
+    )
+
+    projected = (dot(halves[0], weight[:half]) + dot(halves[1], weight[half:])).astype(BF16)
     returned = exchange(
         projected.reshape(owners, 2, cap * ffw // 2), ("near", "x", "far")
     ).reshape(slots_here, ffw)

time: 172 us -> 216 us (1.26)
  waiting for transfers between devices: 43.8 us -> 79.6 us
  local copies, waits for them, and re-layouts: 5.32 us -> 11.4 us
  matrix products: 8.77 us -> 12.2 us
    reduce_scatter x1 -> x2, waiting for transfers between devices: 9.19 us -> 50.5 us  [local(): lax.psum_scatter(dot(both_grads, both_acts[:, at:at + part], ROWS).astype...]
    all_to_all x3, waiting for transfers between devices: 33.1 us -> 26.9 us  [exchange(): return lax.all_to_all(value, axes, split_axis=0, concat_axis=0, tiled=True)]
    transpose x0 -> x1, local copies, waits for them, and re-layouts: none -> 5.99 us  [local(): weight = down_weight[0].reshape(ys, CORES, piece, ffw).transpose(1, 0, 2, 3)]
    dot_general x3 -> x5, matrix products: 8.77 us -> 12.2 us  [dot(): return lax.dot_general(a, b, dims, preferred_element_type=F32)]
    unnamed x9 -> x19, local copies, waits for them, and re-layouts: 0.82 us -> 3.19 us
  transfers between devices with their start and end apart: 6 -> 7, of which waited for: 4 -> 4; matrix products, arithmetic and copies ran while one was open for 7% -> 9% of each run, Pallas kernels for 0% -> 0%
where the time goes in v8:
time: 216 us
  waiting for transfers between devices  79.6 us (37%)
  blocking collectives  50.3 us (23%)
  starting transfers between devices  40.8 us (19%)
  between operations  14.2 us (7%)
  matrix products  12.2 us (6%)
  local copies, waits for them, and re-layouts  11.4 us (5%)
  Pallas kernels  4.46 us (2%)
  other arithmetic  2.57 us (1%)
    reduce_scatter x2, waiting for transfers between devices, local(): lax.psum_scatter(dot(both_grads, both_acts[:, at:at + part], ROWS).astype...  50.5 us
    all_gather x1, blocking collectives, local(): gathered = lax.all_gather(pack, 'far', axis=0, tiled=True)  50.3 us
    all_to_all x3, starting transfers between devices, exchange(): return lax.all_to_all(value, axes, split_axis=0, concat_axis=0, tiled=True)  36.9 us
    all_to_all x3, waiting for transfers between devices, exchange(): return lax.all_to_all(value, axes, split_axis=0, concat_axis=0, tiled=True)  26.9 us
    dot_general x5, matrix products, dot(): return lax.dot_general(a, b, dims, preferred_element_type=F32)  12.2 us
    transpose x1, local copies, waits for them, and re-layouts, local(): weight = down_weight[0].reshape(ys, CORES, piece, ffw).transpose(1, 0, 2, 3)  5.99 us
  transfers between devices with their start and end apart: 7, of which 4 were waited for; matrix products, arithmetic and copies ran while one was open for 9% of the time, Pallas kernels for 0%

profile of v8, /device:TPU:6, one launch (start us, length us, event | category | flops | bytes accessed | tf_op | source)
XLA Modules:
  0.0 215.6 jit_solution(9014477091205171096)
XLA Ops:
  7.2 2.5 %pack.1 = (bf16[1536,128]{1,0:T(8,128)(2,1)}, bf16[16,3968]{1,0:T(8,128)(2,1)}) custom-call(s32[8,16]{1,0:T(8,128)} %bitcast.25, f32[8,16]{1,0:T(8,128)} %bitcast.26, bf16[128,768]{1,0:T(8,128)(2,1)} %bitcast.24, bf16[16,4096]{1,0:T(8,128)(2,1)} %refs_3_.1), custom_call_target="tpu_custom_call" | custom-call | tf_op jit(solution)/shard_map/pack/pallas_call | solution.py:145
  9.7 22.3 %all-to-all-start = ((bf16[64,24,128]{2,1,0:T(8,128)(2,1)}), bf16[64,24,128]{2,1,0:T(8,128)(2,1)S(1)}, u32[]{:S(2)}, u32[]{:S(2)}) async-start(bf16[64,24,128]{2,1,0:T(8,128)(2,1)} %bitcast.23), calls=%async_computation | async-start | bytes 786432 | tf_op jit(solution)/shard_map/all_to_all | solution.py:27
  32.0 50.3 %all_gather.3.gathered_ref = bf16[128,3968]{1,0:T(8,128)(2,1)S(1)} all-gather(bf16[16,3968]{1,0:T(8,128)(2,1)} %get-tuple-element.10), channel_id=1, replica_groups=mesh['y'=8,'core'=2,'far'=8,'near'=2,'x'=4] {'far'}, dimensions={0}, use_global_device_ids=true | all-gather | bytes 1142784 | tf_op jit(solution)/shard_map/all_gather | solution.py:166
  82.4 0.0 all-to-all-done
  82.4 0.2 reshape.68
  82.5 1.9 pick.1
  84.5 6.5 %all-to-all-start.1 = ((bf16[8,24,3840]{2,1,0:T(8,128)(2,1)}), bf16[8,24,3840]{2,1,0:T(8,128)(2,1)S(1)}, u32[]{:S(2)}, u32[]{:S(2)}) async-start(bf16[8,24,3840]{2,1,0:T(8,128)(2,1)} %bitcast.6), calls=%async_computation.1 | async-start | bytes 2949120 | tf_op jit(solution)/shard_map/all_to_all | solution.py:27
  90.9 0.0 reduce-scatter.3.cloned.1.call-start
  91.0 1.9 collective-permute-start
  92.9 6.0 %copy.29 = bf16[2,8,256,768]{3,2,1,0:T(8,128)(2,1)} copy(bf16[2,8,256,768]{3,2,0,1:T(8,128)(2,1)} %bitcast.19) | data formatting | bytes 12582912 | tf_op jit(solution)/shard_map/transpose | solution.py:186
  98.9 0.7 fusion.28
  99.5 0.0 collective-permute-done
  99.6 6.4 %all-to-all-done.1 = bf16[8,24,3840]{2,1,0:T(8,128)(2,1)S(1)} async-done(((bf16[8,24,3840]{2,1,0:T(8,128)(2,1)}), bf16[8,24,3840]{2,1,0:T(8,128)(2,1)S(1)}, u32[]{:S(2)}, u32[]{:S(2)}) %all-to-all-start.1) | async-done | bytes 1474592 | tf_op jit(solution)/shard_map/all_to_all | solution.py:27
  106.0 0.1 fusion.27
  106.1 0.7 copy-done.1
  106.8 0.0 copy-done.3
  106.8 0.3 broadcast_select_fusion.1
  107.1 1.9 collective-permute-start.1
  109.0 2.3 %collective-permute-done.1 = bf16[192,2048]{1,0:T(8,128)(2,1)S(1)} collective-permute-done((bf16[192,2048]{1,0:T(8,128)(2,1)S(1)}, bf16[192,2048]{1,0:T(8,128)(2,1)S(1)}, u32[]{:S(2)}, u32[]{:S(2)}) %collective-permute-start.1) | collective-permute-done | bytes 786464 | tf_op jit(solution)/shard_map/ppermute | solution.py:201
  111.2 0.9 copy-done.7
  112.1 2.3 %convolution_convert_fusion.1 = bf16[2048,384]{1,0:T(8,128)(2,1)} fusion(bf16[192,2048]{1,0:T(8,128)(2,1)S(1)} %collective-permute-done.1, bf16[192,2048]{1,0:T(8,128)(2,1)S(1)} %get-tuple-element.20, bf16[384,768]{1,0:T(8,128)(2,1)S(1)} %pad_maximum_fusion.5), kind=kOutput, calls=%fused_computation.5 | convolution fusion | flops 607911936 | bytes 3440640 | tf_op jit(solution)/shard_map/dot_general | solution.py:23
  114.4 0.0 reduce-scatter.3.cloned.1.call-update
  114.5 0.0 reduce-scatter.5.cloned.1.call-start
  114.5 3.5 %convolution_convert_fusion = bf16[2048,384]{1,0:T(8,128)(2,1)} fusion(bf16[192,2048]{1,0:T(8,128)(2,1)} %copy-done.7, bf16[192,2048]{1,0:T(8,128)(2,1)S(1)} %get-tuple-element.20, bf16[384,768]{1,0:T(8,128)(2,1)S(1)} %pad_maximum_fusion.5), kind=kOutput, calls=%fused_computation.4 | convolution fusion | flops 607911936 | bytes 3440640 | tf_op jit(solution)/shard_map/dot_general | solution.py:23
  118.1 0.0 reduce-scatter.5.cloned.1.call-update
  118.1 0.8 copy-done.4
  118.9 2.7 %fusion = f32[192,768]{1,0:T(8,128)S(1)} fusion(bf16[4096,768]{1,0:T(8,128)(2,1)} %bitcast.20, bf16[192,1920]{1,0:T(8,128)(2,1)S(1)} %get-tuple-element.23, bf16[192,128]{1,0:T(8,128)(2,1)S(1)} %copy-done.4), kind=kOutput, calls=%fused_computation | convolution fusion | flops 605552640 | bytes 4521984 | tf_op jit(solution)/shard_map/dot_general | solution.py:23
  121.5 0.0 copy-done.2
  121.5 0.0 copy-start.5
  121.6 0.0 copy-start.6
  121.6 2.7 %fusion.7 = bf16[192,768]{1,0:T(8,128)(2,1)S(1)} fusion(f32[192,768]{1,0:T(8,128)S(1)} %fusion, bf16[4096,768]{1,0:T(8,128)(2,1)} %bitcast.21, bf16[192,1920]{1,0:T(8,128)(2,1)S(1)} %get-tuple-element.22, bf16[192,128]{1,0:T(8,128)(2,1)S(1)} %copy-done.2), kind=kOutput, calls=%fused_computation.8 | convolution fusion | flops 605847552 | bytes 4816896 | tf_op jit(solution)/shard_map/dot_general | solution.py:23
  124.3 0.0 copy-start
  124.3 0.9 reshape.73
  125.2 8.1 %all-to-all-start.2 = ((bf16[64,2,1152]{2,1,0:T(2,128)(2,1)}), bf16[64,2,1152]{2,1,0:T(2,128)(2,1)S(1)}, u32[]{:S(2)}, u32[]{:S(2)}) async-start(bf16[64,2,1152]{2,1,0:T(2,128)(2,1)} %reshape.73), calls=%async_computation.2 | async-start | bytes 589824 | tf_op jit(solution)/shard_map/all_to_all | solution.py:27
  133.3 0.0 copy-done.5
  133.3 0.1 copy.25
  133.4 0.1 copy.24
  133.5 0.1 reshape.65
  133.6 0.1 fusion.16
  133.7 0.2 reduce_window_sum.11
  133.8 0.2 select_reduce_fusion
  134.0 0.1 reduce_sum.21
  134.1 20.5 %all-to-all-done.2 = bf16[64,2,1152]{2,1,0:T(2,128)(2,1)S(1)} async-done(((bf16[64,2,1152]{2,1,0:T(2,128)(2,1)}), bf16[64,2,1152]{2,1,0:T(2,128)(2,1)S(1)}, u32[]{:S(2)}, u32[]{:S(2)}) %all-to-all-start.2) | async-done | bytes 294944 | tf_op jit(solution)/shard_map/all_to_all | solution.py:27
  154.6 0.2 reshape.75
  154.8 1.0 multiply_reduce_fusion
  155.8 0.7 copy.30
  156.5 50.5 %reduce-scatter.5.cloned.1.call-done = bf16[256,384]{1,0:T(8,128)(2,1)} async-done(((bf16[2048,384]{1,0:T(8,128)(2,1)}), bf16[256,384]{1,0:T(8,128)(2,1)}) %reduce-scatter.5.cloned.1.call-update) | async-done | bytes 196624 | tf_op jit(solution)/shard_map/reduce_scatter | solution.py:205
  206.9 1.8 maximum_bitcast_fusion
  (12 shorter events, 0.1 us)
Async XLA Ops:
  9.7 72.7 %all-to-all-start = ((bf16[64,24,128]{2,1,0:T(8,128)(2,1)}), bf16[64,24,128]{2,1,0:T(8,128)(2,1)S(1)}, u32[]{:S(2)}, u32[]{:S(2)}) async-start(bf16[64,24,128]{2,1,0:T(8,128)(2,1)} %bitcast.23), calls=%async_computation | async-start | bytes 786432 | tf_op jit(solution)/shard_map/all_to_all | solution.py:27
  84.5 21.5 %all-to-all-start.1 = ((bf16[8,24,3840]{2,1,0:T(8,128)(2,1)}), bf16[8,24,3840]{2,1,0:T(8,128)(2,1)S(1)}, u32[]{:S(2)}, u32[]{:S(2)}) async-start(bf16[8,24,3840]{2,1,0:T(8,128)(2,1)} %bitcast.6), calls=%async_computation.1 | async-start | bytes 2949120 | tf_op jit(solution)/shard_map/all_to_all | solution.py:27
  90.9 65.6 %reduce-scatter.3.cloned.1.call-start = ((), (), s32[]{:S(2)}) async-start(), calls=%async_computation.5 | async-start | bytes 1769472 | tf_op jit(solution)/shard_map/reduce_scatter | solution.py:205
  91.0 8.6 %collective-permute-start = (bf16[192,768]{1,0:T(8,128)(2,1)S(1)}, bf16[192,768]{1,0:T(8,128)(2,1)S(1)}, u32[]{:S(2)}, u32[]{:S(2)}) collective-permute-start(bf16[192,768]{1,0:T(8,128)(2,1)S(1)} %slice.28), channel_id=1, source_target_pairs={{0,64},{64,0},{1,65},{65,1},{2,66},{66,2},{3,67},{67,3},{4,68},{68... | collective-permute-start | bytes 884744 | tf_op jit(solution)/shard_map/ppermute | solution.py:185
  106.0 0.8 copy-start.1
  106.0 0.8 copy-start.3
  107.1 4.2 %collective-permute-start.1 = (bf16[192,2048]{1,0:T(8,128)(2,1)S(1)}, bf16[192,2048]{1,0:T(8,128)(2,1)S(1)}, u32[]{:S(2)}, u32[]{:S(2)}) collective-permute-start(bf16[192,2048]{1,0:T(8,128)(2,1)S(1)} %get-tuple-element.21), channel_id=1, source_target_pairs={{0,64},{64,0},{1,65},{65,1},{2,66},{66,2},{3,67},{67,3},{4,68},{68... | collective-permute-start | bytes 2359304 | tf_op jit(solution)/shard_map/ppermute | solution.py:201
  111.2 0.9 copy-start.7
  114.5 92.5 %reduce-scatter.5.cloned.1.call-start = ((), (), s32[]{:S(2)}) async-start(), calls=%async_computation.6 | async-start | bytes 1769472 | tf_op jit(solution)/shard_map/reduce_scatter | solution.py:205
  118.1 0.8 copy-start.4
  118.9 2.7 %copy-start.2 = (bf16[192,128]{1,0:T(8,128)(2,1)S(1)}, bf16[192,128]{1,0:T(8,128)(2,1)}, u32[]{:S(2)}) copy-start(bf16[192,128]{1,0:T(8,128)(2,1)} %get-tuple-element.26) | copy-start | bytes 147460
  121.5 11.8 %copy-start.5 = (s32[16,8]{0,1:T(8,128)S(1)}, s32[16,8]{0,1:T(8,128)}, u32[]{:S(2)}) copy-start(s32[16,8]{0,1:T(8,128)} %param.8) | copy-start | bytes 1540
  121.6 11.8 %copy-start.6 = (f32[16,8]{0,1:T(8,128)S(1)}, f32[16,8]{0,1:T(8,128)}, u32[]{:S(2)}) copy-start(f32[16,8]{0,1:T(8,128)} %param.7) | copy-start | bytes 1540
  124.3 30.5 %copy-start = (bf16[16,8,768]{2,1,0:T(8,128)(2,1)S(1)}, bf16[16,8,768]{2,1,0:T(8,128)(2,1)}, u32[]{:S(2)}) copy-start(bf16[16,8,768]{2,1,0:T(8,128)(2,1)} %param.6) | copy-start | bytes 589828
  125.2 29.4 %all-to-all-start.2 = ((bf16[64,2,1152]{2,1,0:T(2,128)(2,1)}), bf16[64,2,1152]{2,1,0:T(2,128)(2,1)S(1)}, u32[]{:S(2)}, u32[]{:S(2)}) async-start(bf16[64,2,1152]{2,1,0:T(2,128)(2,1)} %reshape.73), calls=%async_computation.2 | async-start | bytes 589824 | tf_op jit(solution)/shard_map/all_to_all | solution.py:27
Sparse Core Ops, SparseCore 0:
  114.6 41.5 reduce-scatter.2
  159.6 47.3 reduce-scatter.4

commit v9 on v8

--- a/solution.py
+++ b/solution.py
@@ -199,19 +199,8 @@
     ]
     mine, theirs = [jnp.where(core == 0, halves[c], halves[1 - c]) for c in range(CORES)]
     both_grads = jnp.concatenate([mine, lax.ppermute(theirs, "core", swap)], axis=0)
-    part = ffw // 2
-    grad_down = jnp.concatenate(
-        [
-            lax.psum_scatter(
-                dot(both_grads, both_acts[:, at : at + part], ROWS).astype(BF16),
-                "y",
-                scatter_dimension=0,
-                tiled=True,
-            )
-            for at in range(0, ffw, part)
-        ],
-        axis=1,
-    )
+    partial_value = dot(both_grads, both_acts, ROWS).astype(BF16)
+    grad_down = lax.psum_scatter(partial_value, "y", scatter_dimension=0, tiled=True)
 
     projected = (dot(halves[0], weight[:half]) + dot(halves[1], weight[half:])).astype(BF16)
     returned = exchange(

time: 216 us -> 170 us (0.79)
  waiting for transfers between devices: 79.6 us -> 38.8 us
  matrix products: 12.2 us -> 9.95 us
    reduce_scatter x2 -> x1, waiting for transfers between devices: 50.5 us -> 9.68 us  [local(): lax.psum_scatter(partial_value, 'y', scatter_dimension=0, tiled=True)]
    dot_general x5 -> x4, matrix products: 12.2 us -> 9.95 us  [dot(): return lax.dot_general(a, b, dims, preferred_element_type=F32)]
  transfers between devices with their start and end apart: 7 -> 6, of which waited for: 4 -> 4; matrix products, arithmetic and copies ran while one was open for 9% -> 9% of each run, Pallas kernels for 0% -> 0%
where the time goes in v9:
time: 170 us
  blocking collectives  50.3 us (30%)
  starting transfers between devices  40.7 us (24%)
  waiting for transfers between devices  38.8 us (23%)
  between operations  14.2 us (8%)
  local copies, waits for them, and re-layouts  10.5 us (6%)
  matrix products  9.95 us (6%)
  Pallas kernels  4.48 us (3%)
    all_gather x1, blocking collectives, local(): gathered = lax.all_gather(pack, 'far', axis=0, tiled=True)  50.3 us
    all_to_all x3, starting transfers between devices, exchange(): return lax.all_to_all(value, axes, split_axis=0, concat_axis=0, tiled=True)  36.9 us
    all_to_all x3, waiting for transfers between devices, exchange(): return lax.all_to_all(value, axes, split_axis=0, concat_axis=0, tiled=True)  26.9 us
    dot_general x4, matrix products, dot(): return lax.dot_general(a, b, dims, preferred_element_type=F32)  9.95 us
    reduce_scatter x1, waiting for transfers between devices, local(): lax.psum_scatter(partial_value, 'y', scatter_dimension=0, tiled=True)  9.68 us
    transpose x1, local copies, waits for them, and re-layouts, local(): weight = down_weight[0].reshape(ys, CORES, piece, ffw).transpose(1, 0, 2, 3)  6 us
  transfers between devices with their start and end apart: 6, of which 4 were waited for; matrix products, arithmetic and copies ran while one was open for 9% of the time, Pallas kernels for 0%

profile of v9, /device:TPU:6, one launch (start us, length us, event | category | flops | bytes accessed | tf_op | source)
XLA Modules:
  0.0 169.8 jit_solution(2227059331874889061)
XLA Ops:
  7.2 2.5 %pack.1 = (bf16[1536,128]{1,0:T(8,128)(2,1)}, bf16[16,3968]{1,0:T(8,128)(2,1)}) custom-call(s32[8,16]{1,0:T(8,128)} %bitcast.25, f32[8,16]{1,0:T(8,128)} %bitcast.26, bf16[128,768]{1,0:T(8,128)(2,1)} %bitcast.24, bf16[16,4096]{1,0:T(8,128)(2,1)} %refs_3_.1), custom_call_target="tpu_custom_call" | custom-call | tf_op jit(solution)/shard_map/pack/pallas_call | solution.py:145
  9.7 22.3 %all-to-all-start = ((bf16[64,24,128]{2,1,0:T(8,128)(2,1)}), bf16[64,24,128]{2,1,0:T(8,128)(2,1)S(1)}, u32[]{:S(2)}, u32[]{:S(2)}) async-start(bf16[64,24,128]{2,1,0:T(8,128)(2,1)} %bitcast.23), calls=%async_computation | async-start | bytes 786432 | tf_op jit(solution)/shard_map/all_to_all | solution.py:27
  32.0 50.3 %all_gather.3.gathered_ref = bf16[128,3968]{1,0:T(8,128)(2,1)S(1)} all-gather(bf16[16,3968]{1,0:T(8,128)(2,1)} %get-tuple-element.10), channel_id=1, replica_groups=mesh['y'=8,'core'=2,'far'=8,'near'=2,'x'=4] {'far'}, dimensions={0}, use_global_device_ids=true | all-gather | bytes 1142784 | tf_op jit(solution)/shard_map/all_gather | solution.py:166
  82.4 0.0 all-to-all-done
  82.4 0.2 reshape.68
  82.5 1.9 %pick.1 = bf16[192,3840]{1,0:T(8,128)(2,1)} custom-call(s32[1]{0:T(128)} %bitcast.5.far_ref, bf16[128,3968]{1,0:T(8,128)(2,1)S(1)} %all_gather.3.gathered_ref), custom_call_target="tpu_custom_call" | custom-call | tf_op jit(solution)/shard_map/pick/pallas_call | solution.py:169
  84.5 6.5 %all-to-all-start.1 = ((bf16[8,24,3840]{2,1,0:T(8,128)(2,1)}), bf16[8,24,3840]{2,1,0:T(8,128)(2,1)S(1)}, u32[]{:S(2)}, u32[]{:S(2)}) async-start(bf16[8,24,3840]{2,1,0:T(8,128)(2,1)} %bitcast.6), calls=%async_computation.1 | async-start | bytes 2949120 | tf_op jit(solution)/shard_map/all_to_all | solution.py:27
  91.0 0.0 reduce-scatter.2.cloned.1.call-start
  91.0 1.9 %collective-permute-start = (bf16[192,768]{1,0:T(8,128)(2,1)S(1)}, bf16[192,768]{1,0:T(8,128)(2,1)S(1)}, u32[]{:S(2)}, u32[]{:S(2)}) collective-permute-start(bf16[192,768]{1,0:T(8,128)(2,1)S(1)} %slice.22), channel_id=1, source_target_pairs={{0,64},{64,0},{1,65},{65,1},{2,66},{66,2},{3,67},{67,3},{4,68},{68... | collective-permute-start | bytes 884744 | tf_op jit(solution)/shard_map/ppermute | solution.py:185
  92.9 6.0 %copy.29 = bf16[2,8,256,768]{3,2,1,0:T(8,128)(2,1)} copy(bf16[2,8,256,768]{3,2,0,1:T(8,128)(2,1)} %bitcast.19) | data formatting | bytes 12582912 | tf_op jit(solution)/shard_map/transpose | solution.py:186
  98.9 0.6 fusion.28
  99.6 0.0 collective-permute-done
  99.6 6.4 %all-to-all-done.1 = bf16[8,24,3840]{2,1,0:T(8,128)(2,1)S(1)} async-done(((bf16[8,24,3840]{2,1,0:T(8,128)(2,1)}), bf16[8,24,3840]{2,1,0:T(8,128)(2,1)S(1)}, u32[]{:S(2)}, u32[]{:S(2)}) %all-to-all-start.1) | async-done | bytes 1474592 | tf_op jit(solution)/shard_map/all_to_all | solution.py:27
  106.0 0.0 copy-start.1
  106.0 0.0 copy-start.3
  106.0 0.1 fusion.27
  106.1 0.7 copy-done.1
  106.8 0.0 copy-done.3
  106.8 0.3 broadcast_select_fusion.1
  107.1 1.9 %collective-permute-start.1 = (bf16[192,2048]{1,0:T(8,128)(2,1)S(1)}, bf16[192,2048]{1,0:T(8,128)(2,1)S(1)}, u32[]{:S(2)}, u32[]{:S(2)}) collective-permute-start(bf16[192,2048]{1,0:T(8,128)(2,1)S(1)} %get-tuple-element.21), channel_id=1, source_target_pairs={{0,64},{64,0},{1,65},{65,1},{2,66},{66,2},{3,67},{67,3},{4,68},{68... | collective-permute-start | bytes 2359304 | tf_op jit(solution)/shard_map/ppermute | solution.py:201
  109.0 2.3 %collective-permute-done.1 = bf16[192,2048]{1,0:T(8,128)(2,1)S(1)} collective-permute-done((bf16[192,2048]{1,0:T(8,128)(2,1)S(1)}, bf16[192,2048]{1,0:T(8,128)(2,1)S(1)}, u32[]{:S(2)}, u32[]{:S(2)}) %collective-permute-start.1) | collective-permute-done | bytes 786464 | tf_op jit(solution)/shard_map/ppermute | solution.py:201
  111.2 3.6 %convolution_convert_fusion = bf16[2048,768]{1,0:T(8,128)(2,1)} fusion(bf16[384,768]{1,0:T(8,128)(2,1)S(1)} %pad_maximum_fusion.2, bf16[192,2048]{1,0:T(8,128)(2,1)S(1)} %collective-permute-done.1, bf16[192,2048]{1,0:T(8,128)(2,1)S(1)} %get-tuple-element.20), kind=kOutput, calls=%fused_computation | convolution fusion | flops 1212678144 | bytes 5308416 | tf_op jit(solution)/shard_map/dot_general | solution.py:23
  114.8 0.0 copy-start.4
  114.8 0.0 reduce-scatter.2.cloned.1.call-update
  114.8 0.8 copy-done.4
  115.6 2.7 %fusion = f32[192,768]{1,0:T(8,128)S(1)} fusion(bf16[4096,768]{1,0:T(8,128)(2,1)} %bitcast.20, bf16[192,1920]{1,0:T(8,128)(2,1)S(1)} %get-tuple-element.23, bf16[192,128]{1,0:T(8,128)(2,1)S(1)} %copy-done.4), kind=kOutput, calls=%fused_computation.1 | convolution fusion | flops 605552640 | bytes 4521984 | tf_op jit(solution)/shard_map/dot_general | solution.py:23
  118.3 0.0 copy-done.2
  118.3 0.0 copy-start.5
  118.3 0.0 copy-start.6
  118.3 2.7 %fusion.10 = bf16[192,768]{1,0:T(8,128)(2,1)S(1)} fusion(f32[192,768]{1,0:T(8,128)S(1)} %fusion, bf16[4096,768]{1,0:T(8,128)(2,1)} %bitcast.21, bf16[192,1920]{1,0:T(8,128)(2,1)S(1)} %get-tuple-element.22, bf16[192,128]{1,0:T(8,128)(2,1)S(1)} %copy-done.2), kind=kOutput, calls=%fused_computation.9 | convolution fusion | flops 605847552 | bytes 4816896 | tf_op jit(solution)/shard_map/dot_general | solution.py:23
  121.0 0.0 copy-start
  121.0 0.9 reshape.73
  121.9 8.1 %all-to-all-start.2 = ((bf16[64,2,1152]{2,1,0:T(2,128)(2,1)}), bf16[64,2,1152]{2,1,0:T(2,128)(2,1)S(1)}, u32[]{:S(2)}, u32[]{:S(2)}) async-start(bf16[64,2,1152]{2,1,0:T(2,128)(2,1)} %reshape.73), calls=%async_computation.2 | async-start | bytes 589824 | tf_op jit(solution)/shard_map/all_to_all | solution.py:27
  130.1 0.0 copy-done.5
  130.1 0.1 copy.25
  130.1 0.0 copy-done.6
  130.1 0.1 copy.24
  130.2 0.1 reshape.65
  130.3 0.1 fusion.17
  130.4 0.2 reduce_window_sum.11
  130.6 0.2 select_reduce_fusion
  130.8 0.1 reduce_sum.21
  130.9 20.5 %all-to-all-done.2 = bf16[64,2,1152]{2,1,0:T(2,128)(2,1)S(1)} async-done(((bf16[64,2,1152]{2,1,0:T(2,128)(2,1)}), bf16[64,2,1152]{2,1,0:T(2,128)(2,1)S(1)}, u32[]{:S(2)}, u32[]{:S(2)}) %all-to-all-start.2) | async-done | bytes 294944 | tf_op jit(solution)/shard_map/all_to_all | solution.py:27
  151.4 0.2 reshape.75
  151.6 0.0 copy-done
  151.6 1.0 multiply_reduce_fusion
  152.6 0.7 copy.30
  153.3 9.7 %reduce-scatter.2.cloned.1.call-done = bf16[256,768]{1,0:T(8,128)(2,1)} async-done(((bf16[2048,768]{1,0:T(8,128)(2,1)}), bf16[256,768]{1,0:T(8,128)(2,1)}) %reduce-scatter.2.cloned.1.call-update) | async-done | bytes 393232 | tf_op jit(solution)/shard_map/reduce_scatter | solution.py:203
  (5 shorter events, 0.1 us)
Async XLA Ops:
  9.7 72.7 %all-to-all-start = ((bf16[64,24,128]{2,1,0:T(8,128)(2,1)}), bf16[64,24,128]{2,1,0:T(8,128)(2,1)S(1)}, u32[]{:S(2)}, u32[]{:S(2)}) async-start(bf16[64,24,128]{2,1,0:T(8,128)(2,1)} %bitcast.23), calls=%async_computation | async-start | bytes 786432 | tf_op jit(solution)/shard_map/all_to_all | solution.py:27
  84.5 21.5 %all-to-all-start.1 = ((bf16[8,24,3840]{2,1,0:T(8,128)(2,1)}), bf16[8,24,3840]{2,1,0:T(8,128)(2,1)S(1)}, u32[]{:S(2)}, u32[]{:S(2)}) async-start(bf16[8,24,3840]{2,1,0:T(8,128)(2,1)} %bitcast.6), calls=%async_computation.1 | async-start | bytes 2949120 | tf_op jit(solution)/shard_map/all_to_all | solution.py:27
  91.0 72.0 %reduce-scatter.2.cloned.1.call-start = ((), (), s32[]{:S(2)}) async-start(), calls=%async_computation.4 | async-start | bytes 3538944 | tf_op jit(solution)/shard_map/reduce_scatter | solution.py:203
  91.0 8.6 %collective-permute-start = (bf16[192,768]{1,0:T(8,128)(2,1)S(1)}, bf16[192,768]{1,0:T(8,128)(2,1)S(1)}, u32[]{:S(2)}, u32[]{:S(2)}) collective-permute-start(bf16[192,768]{1,0:T(8,128)(2,1)S(1)} %slice.22), channel_id=1, source_target_pairs={{0,64},{64,0},{1,65},{65,1},{2,66},{66,2},{3,67},{67,3},{4,68},{68... | collective-permute-start | bytes 884744 | tf_op jit(solution)/shard_map/ppermute | solution.py:185
  106.0 0.8 copy-start.1
  106.0 0.8 copy-start.3
  107.1 4.2 %collective-permute-start.1 = (bf16[192,2048]{1,0:T(8,128)(2,1)S(1)}, bf16[192,2048]{1,0:T(8,128)(2,1)S(1)}, u32[]{:S(2)}, u32[]{:S(2)}) collective-permute-start(bf16[192,2048]{1,0:T(8,128)(2,1)S(1)} %get-tuple-element.21), channel_id=1, source_target_pairs={{0,64},{64,0},{1,65},{65,1},{2,66},{66,2},{3,67},{67,3},{4,68},{68... | collective-permute-start | bytes 2359304 | tf_op jit(solution)/shard_map/ppermute | solution.py:201
  114.8 0.8 copy-start.4
  115.6 2.7 %copy-start.2 = (bf16[192,128]{1,0:T(8,128)(2,1)S(1)}, bf16[192,128]{1,0:T(8,128)(2,1)}, u32[]{:S(2)}) copy-start(bf16[192,128]{1,0:T(8,128)(2,1)} %get-tuple-element.26) | copy-start | bytes 147460
  118.3 11.8 %copy-start.5 = (s32[16,8]{0,1:T(8,128)S(1)}, s32[16,8]{0,1:T(8,128)}, u32[]{:S(2)}) copy-start(s32[16,8]{0,1:T(8,128)} %param.8) | copy-start | bytes 1540
  118.3 11.8 %copy-start.6 = (f32[16,8]{0,1:T(8,128)S(1)}, f32[16,8]{0,1:T(8,128)}, u32[]{:S(2)}) copy-start(f32[16,8]{0,1:T(8,128)} %param.7) | copy-start | bytes 1540
  121.0 30.5 %copy-start = (bf16[16,8,768]{2,1,0:T(8,128)(2,1)S(1)}, bf16[16,8,768]{2,1,0:T(8,128)(2,1)}, u32[]{:S(2)}) copy-start(bf16[16,8,768]{2,1,0:T(8,128)(2,1)} %param.6) | copy-start | bytes 589828
  121.9 29.4 %all-to-all-start.2 = ((bf16[64,2,1152]{2,1,0:T(2,128)(2,1)}), bf16[64,2,1152]{2,1,0:T(2,128)(2,1)S(1)}, u32[]{:S(2)}, u32[]{:S(2)}) async-start(bf16[64,2,1152]{2,1,0:T(2,128)(2,1)} %reshape.73), calls=%async_computation.2 | async-start | bytes 589824 | tf_op jit(solution)/shard_map/all_to_all | solution.py:27
Sparse Core Ops, SparseCore 0:
  115.0 47.9 reduce-scatter.1

commit v10 on v9

--- a/solution.py
+++ b/solution.py
@@ -183,9 +183,12 @@
     swap = [(0, 1), (1, 0)]
     acts = got[:, :ffw]
     both_acts = jnp.concatenate([acts, lax.ppermute(acts, "core", swap)], axis=0)
-    weight = down_weight[0].reshape(ys, CORES, piece, ffw).transpose(1, 0, 2, 3)
-    weight = weight.reshape(width, ffw)
-    relay, both_acts, weight = lax.optimization_barrier((relay, both_acts, weight))
+    weight = down_weight[0].reshape(ys, CORES, piece, ffw)
+    weights = [
+        lax.dynamic_index_in_dim(weight, c, 1, keepdims=False).reshape(half, ffw)
+        for c in (core, 1 - core)
+    ]
+    relay, both_acts, weights = lax.optimization_barrier((relay, both_acts, weights))
 
     halves = [
         jnp.concatenate(
@@ -202,7 +205,7 @@
     partial_value = dot(both_grads, both_acts, ROWS).astype(BF16)
     grad_down = lax.psum_scatter(partial_value, "y", scatter_dimension=0, tiled=True)
 
-    projected = (dot(halves[0], weight[:half]) + dot(halves[1], weight[half:])).astype(BF16)
+    projected = (dot(mine, weights[0]) + dot(theirs, weights[1])).astype(BF16)
     returned = exchange(
         projected.reshape(owners, 2, cap * ffw // 2), ("near", "x", "far")
     ).reshape(slots_here, ffw)

time: 170 us -> 172 us (1.012)
  other arithmetic: 0.78 us -> 2.67 us
    transpose x1 -> x0, local copies, waits for them, and re-layouts: 6 us -> none  [local(): weight = down_weight[0].reshape(ys, CORES, piece, ffw).transpose(1, 0, 2, 3)]
    dynamic_slice x0 -> x1, local copies, waits for them, and re-layouts: none -> 4.98 us  [local(): lax.dynamic_index_in_dim(weight, c, 1, keepdims=False).reshape(half, ffw)]
    concatenate x1, other arithmetic: 0.04 us -> 1.93 us  [local(): jnp.concatenate([acts, lax.ppermute(acts, 'core', swap)], axis=0)]
  transfers between devices with their start and end apart: 6 -> 6, of which waited for: 4 -> 4; matrix products, arithmetic and copies ran while one was open for 9% -> 10% of each run, Pallas kernels for 0% -> 0%
where the time goes in v10:
time: 172 us
  blocking collectives  50.3 us (29%)
  starting transfers between devices  40.7 us (24%)
  waiting for transfers between devices  38.9 us (23%)
  between operations  14.2 us (8%)
  local copies, waits for them, and re-layouts  11 us (6%)
  matrix products  9.24 us (5%)
  Pallas kernels  4.49 us (3%)
  other arithmetic  2.67 us (2%)
    all_gather x1, blocking collectives, local(): gathered = lax.all_gather(pack, 'far', axis=0, tiled=True)  50.3 us
    all_to_all x3, starting transfers between devices, exchange(): return lax.all_to_all(value, axes, split_axis=0, concat_axis=0, tiled=True)  36.9 us
    all_to_all x3, waiting for transfers between devices, exchange(): return lax.all_to_all(value, axes, split_axis=0, concat_axis=0, tiled=True)  25.4 us
    reduce_scatter x1, waiting for transfers between devices, local(): lax.psum_scatter(partial_value, 'y', scatter_dimension=0, tiled=True)  11.2 us
    dot_general x4, matrix products, dot(): return lax.dot_general(a, b, dims, preferred_element_type=F32)  9.24 us
    dynamic_slice x1, local copies, waits for them, and re-layouts, local(): lax.dynamic_index_in_dim(weight, c, 1, keepdims=False).reshape(half, ffw)  4.98 us
  transfers between devices with their start and end apart: 6, of which 4 were waited for; matrix products, arithmetic and copies ran while one was open for 10% of the time, Pallas kernels for 0%

profile of v10, /device:TPU:6, one launch (start us, length us, event | category | flops | bytes accessed | tf_op | source)
XLA Modules:
  0.0 171.5 jit_solution(9609861388822870095)
XLA Ops:
  7.2 2.5 %pack.1 = (bf16[1536,128]{1,0:T(8,128)(2,1)}, bf16[16,3968]{1,0:T(8,128)(2,1)}) custom-call(s32[8,16]{1,0:T(8,128)} %bitcast.27, f32[8,16]{1,0:T(8,128)} %bitcast.28, bf16[128,768]{1,0:T(8,128)(2,1)} %bitcast.26, bf16[16,4096]{1,0:T(8,128)(2,1)} %refs_3_.1), custom_call_target="tpu_custom_call" | custom-call | tf_op jit(solution)/shard_map/pack/pallas_call | solution.py:145
  9.7 22.3 %all-to-all-start = ((bf16[64,24,128]{2,1,0:T(8,128)(2,1)}), bf16[64,24,128]{2,1,0:T(8,128)(2,1)S(1)}, u32[]{:S(2)}, u32[]{:S(2)}) async-start(bf16[64,24,128]{2,1,0:T(8,128)(2,1)} %bitcast.25), calls=%async_computation | async-start | bytes 786432 | tf_op jit(solution)/shard_map/all_to_all | solution.py:27
  32.0 50.3 %all_gather.3.gathered_ref = bf16[128,3968]{1,0:T(8,128)(2,1)S(1)} all-gather(bf16[16,3968]{1,0:T(8,128)(2,1)} %get-tuple-element.11), channel_id=1, replica_groups=mesh['y'=8,'core'=2,'far'=8,'near'=2,'x'=4] {'far'}, dimensions={0}, use_global_device_ids=true | all-gather | bytes 1142784 | tf_op jit(solution)/shard_map/all_gather | solution.py:166
  82.4 0.0 all-to-all-done
  82.4 0.2 reshape.73
  82.5 1.9 %pick.1 = bf16[192,3840]{1,0:T(8,128)(2,1)} custom-call(s32[1]{0:T(128)} %bitcast.5.far_ref, bf16[128,3968]{1,0:T(8,128)(2,1)S(1)} %all_gather.3.gathered_ref), custom_call_target="tpu_custom_call" | custom-call | tf_op jit(solution)/shard_map/pick/pallas_call | solution.py:169
  84.5 6.5 %all-to-all-start.1 = ((bf16[8,24,3840]{2,1,0:T(8,128)(2,1)}), bf16[8,24,3840]{2,1,0:T(8,128)(2,1)}, u32[]{:S(2)}, u32[]{:S(2)}) async-start(bf16[8,24,3840]{2,1,0:T(8,128)(2,1)} %bitcast.6), calls=%async_computation.1 | async-start | bytes 2949120 | tf_op jit(solution)/shard_map/all_to_all | solution.py:27
  91.0 0.0 reduce-scatter.2.cloned.1.call-start
  91.0 0.7 slice.16
  91.7 1.9 %collective-permute-start = (bf16[192,768]{1,0:T(8,128)(2,1)}, bf16[192,768]{1,0:T(8,128)(2,1)}, u32[]{:S(2)}, u32[]{:S(2)}) collective-permute-start(bf16[192,768]{1,0:T(8,128)(2,1)} %slice.16), channel_id=1, source_target_pairs={{0,64},{64,0},{1,65},{65,1},{2,66},{66,2},{3,67},{67,3},{4,68},{68... | collective-permute-start | bytes 884744 | tf_op jit(solution)/shard_map/ppermute | solution.py:185
  93.6 5.0 %constant_dynamic-slice_fusion.1 = (bf16[8,1,256,768]{3,2,1,0:T(8,128)(2,1)S(1)}, bf16[8,1,256,768]{3,2,1,0:T(8,128)(2,1)}) fusion(bf16[8,2,256,768]{3,2,1,0:T(8,128)(2,1)} %bitcast.24, s32[]{:T(128)S(6)} %select_n.35, s32[]{:T(128)S(6)} %select_n.34), kind=kLoop, calls=%fused_computation.34 | loop fusion | bytes 12582920 | tf_op jit(solution)/shard_map/jit(dynamic_index_in_dim)/dynamic_slice | solution.py:188
  98.6 0.7 fusion.17
  99.3 0.0 collective-permute-done
  99.3 1.9 %pad_maximum_fusion.2 = bf16[384,768]{1,0:T(8,128)(2,1)} fusion(bf16[192,768]{1,0:T(8,128)(2,1)} %collective-permute-done, bf16[192,768]{1,0:T(8,128)(2,1)} %slice.16), kind=kLoop, calls=%fused_computation.10 | loop fusion | flops 1179648 | bytes 1179648 | tf_op jit(solution)/shard_map/concatenate | solution.py:185
  101.2 4.9 %all-to-all-done.1 = bf16[8,24,3840]{2,1,0:T(8,128)(2,1)} async-done(((bf16[8,24,3840]{2,1,0:T(8,128)(2,1)}), bf16[8,24,3840]{2,1,0:T(8,128)(2,1)}, u32[]{:S(2)}, u32[]{:S(2)}) %all-to-all-start.1) | async-done | bytes 1474592 | tf_op jit(solution)/shard_map/all_to_all | solution.py:27
  106.1 1.5 fusion.16
  107.6 0.0 copy-done.4
  107.6 0.0 copy-done.5
  107.6 0.3 broadcast_select_fusion
  107.9 0.0 copy-start
  107.9 0.0 copy-start.2
  107.9 0.9 copy-done
  108.8 1.9 %collective-permute-start.1 = (bf16[192,2048]{1,0:T(8,128)(2,1)S(1)}, bf16[192,2048]{1,0:T(8,128)(2,1)S(1)}, u32[]{:S(2)}, u32[]{:S(2)}) collective-permute-start(bf16[192,2048]{1,0:T(8,128)(2,1)S(1)} %get-tuple-element.24), channel_id=1, source_target_pairs={{0,64},{64,0},{1,65},{65,1},{2,66},{66,2},{3,67},{67,3},{4,68},{68... | collective-permute-start | bytes 2359304 | tf_op jit(solution)/shard_map/ppermute | solution.py:204
  110.7 2.3 %collective-permute-done.1 = bf16[192,2048]{1,0:T(8,128)(2,1)S(1)} collective-permute-done((bf16[192,2048]{1,0:T(8,128)(2,1)S(1)}, bf16[192,2048]{1,0:T(8,128)(2,1)S(1)}, u32[]{:S(2)}, u32[]{:S(2)}) %collective-permute-start.1) | collective-permute-done | bytes 786464 | tf_op jit(solution)/shard_map/ppermute | solution.py:204
  113.0 0.0 copy-done.2
  113.0 0.0 copy-done.3
  113.0 3.5 %convolution_convert_fusion = bf16[2048,768]{1,0:T(8,128)(2,1)} fusion(bf16[384,768]{1,0:T(8,128)(2,1)S(1)} %copy-done.3, bf16[192,2048]{1,0:T(8,128)(2,1)S(1)} %collective-permute-done.1, bf16[192,2048]{1,0:T(8,128)(2,1)S(1)} %get-tuple-element.25), kind=kOutput, calls=%fused_computation | convolution fusion | flops 1212678144 | bytes 5308416 | tf_op jit(solution)/shard_map/dot_general | solution.py:23
  116.5 0.0 reduce-scatter.2.cloned.1.call-update
  116.5 3.0 %fusion.18 = f32[192,768]{1,0:T(8,128)S(1)} fusion(bf16[192,2048]{1,0:T(8,128)(2,1)} %copy-done.2, bf16[2048,768]{1,0:T(8,128)(2,1)} %bitcast.23), kind=kOutput, calls=%fused_computation.38 | convolution fusion | flops 603979776 | bytes 4521984 | tf_op jit(solution)/shard_map/dot_general | solution.py:23
  119.5 0.0 copy-done.1
  119.5 0.0 copy-start.6
  119.5 0.0 copy-start.7
  119.5 0.8 fusion.3
  120.3 0.9 reshape.79
  121.2 8.1 %all-to-all-start.2 = ((bf16[64,2,1152]{2,1,0:T(2,128)(2,1)}), bf16[64,2,1152]{2,1,0:T(2,128)(2,1)S(1)}, u32[]{:S(2)}, u32[]{:S(2)}) async-start(bf16[64,2,1152]{2,1,0:T(2,128)(2,1)} %reshape.79), calls=%async_computation.2 | async-start | bytes 589824 | tf_op jit(solution)/shard_map/all_to_all | solution.py:27
  129.3 0.1 copy.19
  129.4 0.0 copy-done.7
  129.4 0.1 copy.18
  129.5 0.1 reshape.70
  129.6 0.1 fusion.8
  129.7 0.2 reduce_window_sum.11
  129.9 0.2 select_reduce_fusion
  130.0 0.1 reduce_sum.21
  130.2 20.5 %all-to-all-done.2 = bf16[64,2,1152]{2,1,0:T(2,128)(2,1)S(1)} async-done(((bf16[64,2,1152]{2,1,0:T(2,128)(2,1)}), bf16[64,2,1152]{2,1,0:T(2,128)(2,1)S(1)}, u32[]{:S(2)}, u32[]{:S(2)}) %all-to-all-start.2) | async-done | bytes 294944 | tf_op jit(solution)/shard_map/all_to_all | solution.py:27
  150.7 0.2 reshape.81
  150.9 2.0 %multiply_reduce_fusion = (f32[16,8]{1,0:T(8,128)S(1)}, bf16[16,8,768]{2,1,0:T(8,128)(2,1)}) fusion(bf16[16,8,768]{2,1,0:T(8,128)(2,1)} %param.6, f32[16,8]{1,0:T(8,128)S(1)} %copy.18, bf16[192,768,1]{1,0,2:T(8,128)(2,1)S(1)} %reshape.81, s32[16,8]{1,0:T(8,128)S(1)} %multiply_add_fusion), kind=kOutput, calls=%fused_computation.11 | convolution fusion | flops 38264704 | bytes 689664 | tf_op jit(solution)/shard_map/dot_general | solution.py:23
  152.8 0.7 copy.23
  153.5 11.2 %reduce-scatter.2.cloned.1.call-done = bf16[256,768]{1,0:T(8,128)(2,1)} async-done(((bf16[2048,768]{1,0:T(8,128)(2,1)}), bf16[256,768]{1,0:T(8,128)(2,1)}) %reduce-scatter.2.cloned.1.call-update) | async-done | bytes 393232 | tf_op jit(solution)/shard_map/reduce_scatter | solution.py:206
  (7 shorter events, 0.1 us)
Async XLA Ops:
  9.7 72.7 %all-to-all-start = ((bf16[64,24,128]{2,1,0:T(8,128)(2,1)}), bf16[64,24,128]{2,1,0:T(8,128)(2,1)S(1)}, u32[]{:S(2)}, u32[]{:S(2)}) async-start(bf16[64,24,128]{2,1,0:T(8,128)(2,1)} %bitcast.25), calls=%async_computation | async-start | bytes 786432 | tf_op jit(solution)/shard_map/all_to_all | solution.py:27
  84.5 21.6 %all-to-all-start.1 = ((bf16[8,24,3840]{2,1,0:T(8,128)(2,1)}), bf16[8,24,3840]{2,1,0:T(8,128)(2,1)}, u32[]{:S(2)}, u32[]{:S(2)}) async-start(bf16[8,24,3840]{2,1,0:T(8,128)(2,1)} %bitcast.6), calls=%async_computation.1 | async-start | bytes 2949120 | tf_op jit(solution)/shard_map/all_to_all | solution.py:27
  91.0 73.7 %reduce-scatter.2.cloned.1.call-start = ((), (), s32[]{:S(2)}) async-start(), calls=%async_computation.4 | async-start | bytes 3538944 | tf_op jit(solution)/shard_map/reduce_scatter | solution.py:206
  91.7 7.6 %collective-permute-start = (bf16[192,768]{1,0:T(8,128)(2,1)}, bf16[192,768]{1,0:T(8,128)(2,1)}, u32[]{:S(2)}, u32[]{:S(2)}) collective-permute-start(bf16[192,768]{1,0:T(8,128)(2,1)} %slice.16), channel_id=1, source_target_pairs={{0,64},{64,0},{1,65},{65,1},{2,66},{66,2},{3,67},{67,3},{4,68},{68... | collective-permute-start | bytes 884744 | tf_op jit(solution)/shard_map/ppermute | solution.py:185
  99.3 8.3 %copy-start.4 = (bf16[192,128]{1,0:T(8,128)(2,1)S(1)}, bf16[192,128]{1,0:T(8,128)(2,1)}, u32[]{:S(2)}) copy-start(bf16[192,128]{1,0:T(8,128)(2,1)} %get-tuple-element.30) | copy-start | bytes 147460
  99.3 8.4 %copy-start.5 = (bf16[192,128]{1,0:T(8,128)(2,1)S(1)}, bf16[192,128]{1,0:T(8,128)(2,1)}, u32[]{:S(2)}) copy-start(bf16[192,128]{1,0:T(8,128)(2,1)} %get-tuple-element.31) | copy-start | bytes 147460
  106.1 6.9 %copy-start.3 = (bf16[384,768]{1,0:T(8,128)(2,1)S(1)}, bf16[384,768]{1,0:T(8,128)(2,1)}, u32[]{:S(2)}) copy-start(bf16[384,768]{1,0:T(8,128)(2,1)} %pad_maximum_fusion.2) | copy-start | bytes 1769476
  107.9 0.9 copy-start
  107.9 5.0 %copy-start.2 = (bf16[192,2048]{1,0:T(8,128)(2,1)}, bf16[192,2048]{1,0:T(8,128)(2,1)S(1)}, u32[]{:S(2)}) copy-start(bf16[192,2048]{1,0:T(8,128)(2,1)S(1)} %get-tuple-element.25) | copy-start | bytes 2359300
  108.8 4.2 %collective-permute-start.1 = (bf16[192,2048]{1,0:T(8,128)(2,1)S(1)}, bf16[192,2048]{1,0:T(8,128)(2,1)S(1)}, u32[]{:S(2)}, u32[]{:S(2)}) collective-permute-start(bf16[192,2048]{1,0:T(8,128)(2,1)S(1)} %get-tuple-element.24), channel_id=1, source_target_pairs={{0,64},{64,0},{1,65},{65,1},{2,66},{66,2},{3,67},{67,3},{4,68},{68... | collective-permute-start | bytes 2359304 | tf_op jit(solution)/shard_map/ppermute | solution.py:204
  116.5 3.0 %copy-start.1 = (bf16[192,2048]{1,0:T(8,128)(2,1)S(1)}, bf16[192,2048]{1,0:T(8,128)(2,1)}, u32[]{:S(2)}) copy-start(bf16[192,2048]{1,0:T(8,128)(2,1)} %copy-done) | copy-start | bytes 2359300
  119.5 9.8 %copy-start.6 = (s32[16,8]{0,1:T(8,128)S(1)}, s32[16,8]{0,1:T(8,128)}, u32[]{:S(2)}) copy-start(s32[16,8]{0,1:T(8,128)} %param.8) | copy-start | bytes 1540
  119.5 9.9 %copy-start.7 = (f32[16,8]{0,1:T(8,128)S(1)}, f32[16,8]{0,1:T(8,128)}, u32[]{:S(2)}) copy-start(f32[16,8]{0,1:T(8,128)} %param.7) | copy-start | bytes 1540
  121.2 29.4 %all-to-all-start.2 = ((bf16[64,2,1152]{2,1,0:T(2,128)(2,1)}), bf16[64,2,1152]{2,1,0:T(2,128)(2,1)S(1)}, u32[]{:S(2)}, u32[]{:S(2)}) async-start(bf16[64,2,1152]{2,1,0:T(2,128)(2,1)} %reshape.79), calls=%async_computation.2 | async-start | bytes 589824 | tf_op jit(solution)/shard_map/all_to_all | solution.py:27
Sparse Core Ops, SparseCore 0:
  116.6 47.9 reduce-scatter.1
